TPU v7x, 512 devices: a whole 4x4x16 slice. The times are simulated.
512 devices in a mesh: elem: 64 (over y, z), mode: 8 (over x, core).
Axes of the slice: x: 4, y: 4, z: 16, core: 2. Of those that a mesh axis runs over, the one named last changes fastest.
Arguments:
- velocity: float32 [3, 512, 41472], P(None, 'mode', 'elem'), may hold values from -0.375 to 0.375
- metric: float32 [4, 41472], P(None, 'elem'), may hold values from -4 to 4
- mass: float32 [41472], P('elem'), may hold values from 0.1 to 1
- local_ids: int32 [41472], P('elem'), may hold values from 0 to 584, as said below
- edge_ids: int32 [64, 2, 65], P('elem'), may hold values from 0 to 584, as said below
Outputs:
- velocity_new: float32 [3, 512, 41472], P(None, 'mode', 'elem')
- pressure: float32 [512, 41472], P('mode', 'elem')
Inputs may be any that keep to these rules, and one draw needn't show every extreme that they name: `local_ids`: on each device every number of 0 to 584 is used; copies of one node on a device carry one number. Quads share nodes only with quads of their own device and, through the nodes of edge_ids, with the devices just before and after it around the cycle of elem indices. edge_ids[e, 0] and edge_ids[e, 1] each list 65 distinct local numbers of device e, disjoint from each other: the nodes shared with device e - 1 and with device e + 1 (around the cycle). edge_ids[e, 1, k] and edge_ids[e + 1, 0, k] name the same node.
All inputs are finite; a program needn't handle non-finite values.
Results may differ from a plain program's by a relative error of at most 0.0001.
Values sent between devices are 32-bit elements; how exact they have to be, the bound alone decides.
No kernel may reach another device: no remote copies, remote signals or barrier semaphores. Data moves between devices by JAX's collectives and lax.ppermute only.
A program may use at most 64 MiB of HBM per device.

v0:
```python
import math

import jax
import jax.numpy as jnp
import numpy as np
from jax import lax
from jax.sharding import PartitionSpec as P

SIDE = 9
QUAD_NODES = 81
PLANES = 512
ITERS = 2
LOCAL_NODES = 585


penalty = 1.0
time_step = 0.01


def padded(block, sides, width):
    for axis, dim in sides:
        count = lax.axis_size(axis)
        forward = [(i, i + 1) for i in range(count - 1)]
        forward.append((count - 1, 0))
        backward = [(target, source) for source, target in forward]
        low = lax.ppermute(
            lax.slice_in_dim(block, block.shape[dim] - width, None, axis=dim), axis, forward
        )
        high = lax.ppermute(lax.slice_in_dim(block, 0, width, axis=dim), axis, backward)
        block = jnp.concatenate([low, block, high], axis=dim)
    return block


def legendre_pair(points, degree):
    previous = points * 0.0 + 1.0
    current = points.copy()
    for order in range(2, degree + 1):
        following = ((2.0 * order - 1.0) * points * current - (order - 1.0) * previous) / order
        previous = current
        current = following
    return (previous, current)


def derivative_table():
    degree = SIDE - 1
    points = np.cos(math.pi * np.arange(degree + 1) / degree)
    for sweep in range(100):
        lower, upper = legendre_pair(points, degree)
        points = points - (points * upper - lower) / ((degree + 1.0) * upper)
    points = points[::-1].copy()
    values = legendre_pair(points, degree)[1]
    identity = np.eye(SIDE)
    differ = points[:, None] - points[None, :] + identity
    matrix = np.where(identity > 0.5, 0.0, values[:, None] / (values[None, :] * differ))
    matrix[0, 0] = -degree * (degree + 1) / 4.0
    matrix[degree, degree] = degree * (degree + 1) / 4.0
    along_r = np.kron(matrix, identity)
    along_s = np.kron(identity, matrix)
    return np.concatenate([along_r.T, along_s.T], axis=1).astype(np.float32)


def fourier_tables(planes):
    positions = jnp.arange(planes, dtype=jnp.int32)
    mode_number = positions // 2
    frequency = jnp.where(positions == 1, planes // 2, mode_number)
    phase_int = positions[:, None] * frequency[None, :] % planes
    angles = 2.0 * math.pi / planes * phase_int.astype(jnp.float32)
    cosine = jnp.cos(angles)
    sines = jnp.sin(angles)
    cos_like = (positions % 2 == 0) | (positions == 1)
    synthesis = jnp.where(cos_like[None, :], cosine, sines)
    wavenumber = 8.0 / planes * mode_number.astype(jnp.float32)
    slope_table = jnp.where(
        cos_like[None, :], -wavenumber[None, :] * sines, wavenumber[None, :] * cosine
    )
    weight = jnp.where(positions < 2, 1.0, 2.0) / planes
    retained = (mode_number <= planes // 3) & (positions != 1)
    forward = jnp.transpose(synthesis * jnp.where(retained, weight, 0.0)[None, :])
    return (synthesis, slope_table, forward, wavenumber)


def along_z(spectral, wavenumber):
    dims_shape = spectral.shape
    paired = spectral.reshape(dims_shape[:-2] + (dims_shape[-2] // 2, 2, dims_shape[-1]))
    rate_col = wavenumber[0::2][:, None]
    turned = jnp.stack([rate_col * paired[..., 1, :], -rate_col * paired[..., 0, :]], axis=-2)
    return turned.reshape(dims_shape)


def element_grad(field, metric, diff_table):
    derived = jnp.dot(
        field.reshape(-1, QUAD_NODES),
        diff_table,
        precision=lax.Precision.HIGHEST,
        preferred_element_type=jnp.float32,
    )
    grad_r = derived[:, :QUAD_NODES].reshape(field.shape)
    grad_s = derived[:, QUAD_NODES:].reshape(field.shape)
    return (metric[0] * grad_r + metric[2] * grad_s, metric[1] * grad_r + metric[3] * grad_s)


def element_div(flux_x, flux_y, metric, diff_table):
    part_r = metric[0] * flux_x + metric[1] * flux_y
    part_s = metric[2] * flux_x + metric[3] * flux_y
    joined = jnp.concatenate(
        [part_r.reshape(-1, QUAD_NODES), part_s.reshape(-1, QUAD_NODES)], axis=1
    )
    return jnp.dot(
        joined, diff_table.T, precision=lax.Precision.HIGHEST, preferred_element_type=jnp.float32
    ).reshape(flux_x.shape)


def assemble(values, local_ids, edge_ids):
    summed = jnp.zeros((values.shape[0], LOCAL_NODES), jnp.float32).at[:, local_ids].add(values)
    outgoing = jnp.stack([summed[:, edge_ids[0, 0]], summed[:, edge_ids[0, 1]]], axis=0)
    arrived = padded(outgoing, (("elem", 0),), 1)
    summed = summed.at[:, edge_ids[0, 0]].add(arrived[0]).at[:, edge_ids[0, 1]].add(arrived[3])
    return summed[:, local_ids]


def on_device(velocity, metric, mass, local_ids, edge_ids):
    diff_table = jnp.asarray(derivative_table())
    synthesis, slope_table, forward, wavenumber = fourier_tables(PLANES)
    rows_dev = velocity.shape[1]
    nodes_dev = velocity.shape[2]
    local_rate = lax.dynamic_slice_in_dim(wavenumber, lax.axis_index("mode") * rows_dev, rows_dev)
    grad_x, grad_y = element_grad(velocity, metric, diff_table)
    fields = jnp.concatenate([velocity, grad_x, grad_y, along_z(velocity, local_rate)], axis=0)
    planes_all = lax.all_to_all(fields, "mode", split_axis=2, concat_axis=1, tiled=True)
    physical = jnp.einsum("nj,fjm->fnm", synthesis, planes_all, precision=lax.Precision.HIGHEST)
    grad_z = physical[9:12]
    nonlinear = -(physical[0] * physical[3:6] + physical[1] * physical[6:9] + physical[2] * grad_z)
    spectral = jnp.einsum("jn,cnm->cjm", forward, nonlinear, precision=lax.Precision.HIGHEST)
    convect = lax.all_to_all(spectral, "mode", split_axis=1, concat_axis=2, tiled=True)
    weighted = (mass * convect).reshape(3 * rows_dev, nodes_dev)
    stacked = jnp.concatenate([weighted, mass[None, :], jnp.ones_like(mass)[None, :]], axis=0)
    assembled = assemble(stacked, local_ids, edge_ids)
    projected = assembled[: 3 * rows_dev].reshape(convect.shape) / assembled[3 * rows_dev]
    inverse = 1.0 / assembled[3 * rows_dev + 1]
    velocity_star = velocity + time_step * projected
    star_x, star_y = element_grad(velocity_star[:2], metric, diff_table)
    divergence = star_x[0] + star_y[1] + along_z(velocity_star[2], local_rate)
    right_side = -assemble(mass * divergence, local_ids, edge_ids) / time_step
    helmholtz_shift = (local_rate * local_rate + penalty)[:, None]

    def inner_product(left, right):
        return jnp.sum(inverse * left * right, axis=1)

    def squares(vector):
        return lax.psum(inner_product(vector, vector), "elem")

    pressure = jnp.zeros_like(right_side)
    residual = right_side
    direction = right_side
    norm_now = squares(residual)
    for iteration in range(ITERS):
        field_x, field_y = element_grad(direction, metric, diff_table)
        element_part = (
            element_div(mass * field_x, mass * field_y, metric, diff_table)
            + helmholtz_shift * mass * direction
        )
        applied = assemble(element_part, local_ids, edge_ids)
        step_size = norm_now / lax.psum(inner_product(direction, applied), "elem")
        pressure = pressure + step_size[:, None] * direction
        residual = residual - step_size[:, None] * applied
        norm_next = squares(residual)
        direction = residual + (norm_next / norm_now)[:, None] * direction
        norm_now = norm_next
    press_x, press_y = element_grad(pressure, metric, diff_table)
    press_z = along_z(pressure, local_rate)
    velocity_new = velocity_star - time_step * jnp.stack([press_x, press_y, press_z], axis=0)
    return (velocity_new, pressure)


def solution(mesh):
    in_specs = (
        P(None, "mode", "elem"),
        P(None, "elem"),
        P("elem"),
        P("elem"),
        P("elem", None, None),
    )
    out_specs = (P(None, "mode", "elem"), P("mode", "elem"))
    return jax.shard_map(
        on_device, mesh=mesh, in_specs=in_specs, out_specs=out_specs, check_vma=False
    )
```

profile of v0, /device:TPU:2, one launch (start us, length us, event | category | flops | bytes accessed | tf_op | source)
XLA Modules:
  0.0 642.8 jit_solution(10215064107909812526)
XLA Ops:
  0.6 1.4 reshape.456
  2.1 1.5 reshape.453
  5.9 1.4 convolution_bitcast_fusion
  9.2 4.8 copy.117
  13.9 7.4 %reshape.704 = f32[8,1,62208]{2,1,0:T(1,128)} reshape(f32[648,12,64]{2,1,0:T(8,128)} %bitcast.180) | data formatting | bytes 3981312
  21.3 9.9 %all-to-all-start = ((f32[8,1,62208]{2,1,0:T(1,128)}), f32[8,1,62208]{2,1,0:T(1,128)S(1)}, u32[]{:S(2)}, u32[]{:S(2)}) async-start(f32[8,1,62208]{2,1,0:T(1,128)} %reshape.704), calls=%async_computation | async-start | bytes 3981312 | tf_op jit(solution)/shard_map/all_to_all | solution.py:129
  31.7 24.0 %all-to-all-done = f32[8,1,62208]{2,1,0:T(1,128)S(1)} async-done(((f32[8,1,62208]{2,1,0:T(1,128)}), f32[8,1,62208]{2,1,0:T(1,128)S(1)}, u32[]{:S(2)}, u32[]{:S(2)}) %all-to-all-start) | async-done | bytes 1990688 | tf_op jit(solution)/shard_map/all_to_all | solution.py:129
  56.3 7.3 %reduce.16 = f32[8,62208]{1,0:T(8,128)} reduce(f32[8,1,62208]{2,1,0:T(1,128)S(1)} %all-to-all-done, f32[]{:T(128)} %broadcast.405), dimensions={1}, to_apply=%all_to_all.26.reduce_sub_computation | reduce | bytes 3981316 | tf_op jit(solution)/shard_map/all_to_all | solution.py:129
  63.6 5.0 reshape.705
  68.6 6.1 copy.118
  74.7 15.7 %convolution_bitcast_fusion.1 = f32[12,512,81]{1,2,0:T(8,128)S(1)} fusion(f32[12,512,81]{2,1,0:T(8,128)} %bitcast.188, s32[512]{0:T(512)S(1)} %fusion.94, pred[512]{0:T(512)(128)(4,1)S(1)} %fusion.97), kind=kOutput, calls=%fused_computation.26 | convolution fusion | flops 3061579776 | bytes 3983872 | tf_op jit(solution)/shard_map/nj,fjm->fnm/dot_general | solution.py:130
  90.5 5.4 convolution_bitcast_fusion.2
  96.4 2.1 reshape.706
  98.5 4.8 all-to-all-start.1
  104.1 7.9 %all-to-all-done.1 = f32[8,1,15552]{2,1,0:T(1,128)S(1)} async-done(((f32[8,1,15552]{2,1,0:T(1,128)}), f32[8,1,15552]{2,1,0:T(1,128)S(1)}, u32[]{:S(2)}, u32[]{:S(2)}) %all-to-all-start.1) | async-done | bytes 497696 | tf_op jit(solution)/shard_map/all_to_all | solution.py:134
  112.0 1.9 reduce.17
  113.9 1.0 reshape.707
  116.0 5.7 scatter_custom_fusion
  122.4 1.9 collective-permute-start
  125.0 9.3 %collective-permute-start.1 = (f32[1,194,65]{1,2,0:T(8,128)S(1)}, f32[1,194,65]{1,2,0:T(8,128)S(1)}, u32[]{:S(2)}, u32[]{:S(2)}) collective-permute-start(f32[1,194,65]{1,2,0:T(8,128)S(1)} %bitcast.190), channel_id=1, source_target_pairs={{8,0},{16,8},{24,16},{32,24},{40,32},{48,40},{56,48},{64,56},{72,6... | collective-permute-start | bytes 151328 | tf_op jit(solution)/shard_map/ppermute | solution.py:29
  134.3 1.3 scatter_custom_fusion.1
  136.2 1.3 scatter_custom_fusion.2
  137.5 2.6 gather_fusion.2
  141.4 0.8 fusion.117
  144.2 6.1 scatter_custom_fusion.3
  151.5 1.9 collective-permute-start.2
  153.4 7.6 %collective-permute-start.3 = (f32[1,64,65]{1,2,0:T(8,128)S(1)}, f32[1,64,65]{1,2,0:T(8,128)S(1)}, u32[]{:S(2)}, u32[]{:S(2)}) collective-permute-start(f32[1,64,65]{1,2,0:T(8,128)S(1)} %bitcast.192), channel_id=1, source_target_pairs={{8,0},{16,8},{24,16},{32,24},{40,32},{48,40},{56,48},{64,56},{72,6... | collective-permute-start | bytes 49928 | tf_op jit(solution)/shard_map/ppermute | solution.py:29
  161.8 1.1 scatter_custom_fusion.4
  162.9 1.1 scatter_custom_fusion.5
  164.1 1.7 gather_fusion.5
  168.0 6.1 scatter_custom_fusion.6
  175.3 1.9 collective-permute-start.4
  177.2 7.2 %collective-permute-start.5 = (f32[1,64,65]{1,2,0:T(8,128)S(1)}, f32[1,64,65]{1,2,0:T(8,128)S(1)}, u32[]{:S(2)}, u32[]{:S(2)}) collective-permute-start(f32[1,64,65]{1,2,0:T(8,128)S(1)} %bitcast.196), channel_id=1, source_target_pairs={{8,0},{16,8},{24,16},{32,24},{40,32},{48,40},{56,48},{64,56},{72,6... | collective-permute-start | bytes 49928 | tf_op jit(solution)/shard_map/ppermute | solution.py:29
  184.5 1.3 scatter_custom_fusion.7
  186.1 1.1 scatter_custom_fusion.8
  187.2 1.7 gather_fusion.8
  189.3 143.6 %all-reduce = (f32[64]{0:T(128)S(1)}, f32[64]{0:T(128)S(1)}) all-reduce(f32[64]{0:T(128)S(1)} %get-tuple-element.11, f32[64]{0:T(128)S(1)} %get-tuple-element.10), channel_id=1, replica_groups=mesh['elem'=64,'mode'=8] {'elem'}, use_global_device_ids=true, to_apply=%region_7.8 | all-reduce | flops 128 | bytes 1024 | tf_op jit(solution)/shard_map/psum | solution.py:150
  333.1 138.0 %psum.30 = f32[64]{0:T(128)S(1)} all-reduce(f32[64]{0:T(128)S(1)} %fusion.32), channel_id=1, replica_groups=mesh['elem'=64,'mode'=8] {'elem'}, use_global_device_ids=true, to_apply=%region_14.15 | all-reduce | flops 64 | bytes 512 | tf_op jit(solution)/shard_map/psum | solution.py:150
  473.5 6.1 scatter_custom_fusion.9
  480.8 3.9 collective-permute-start.6
  484.7 5.3 collective-permute-start.7
  490.7 1.1 scatter_custom_fusion.10
  491.9 1.1 scatter_custom_fusion.11
  493.0 1.7 gather_fusion.11
  495.0 143.3 %psum.31 = f32[64]{0:T(128)S(1)} all-reduce(f32[64]{0:T(128)S(1)} %fusion.40), channel_id=1, replica_groups=mesh['elem'=64,'mode'=8] {'elem'}, use_global_device_ids=true, to_apply=%region_19.20 | all-reduce | flops 64 | bytes 512 | tf_op jit(solution)/shard_map/psum | solution.py:163
  638.4 0.8 multiply_add_fusion.4
  639.4 0.8 fusion.22
  641.8 0.9 fusion.9
  (171 shorter events, 25.3 us)
Async XLA Ops:
  2.1 3.8 copy-start.9
  2.1 3.8 copy-start.3
  4.3 3.0 copy-start.10
  4.3 0.6 copy-start.12
  7.9 1.1 copy-start
  21.3 10.2 %copy-start.8 = (f32[648]{0:T(1024)S(1)}, f32[648]{0:T(1024)}, u32[]{:S(2)}) copy-start(f32[648]{0:T(1024)} %param.8) | copy-start | bytes 7780
  21.3 10.3 %copy-start.18 = (s32[1,2,65]{2,1,0:T(2,128)S(1)}, s32[1,2,65]{2,1,0:T(2,128)}, u32[]{:S(2)}) copy-start(s32[1,2,65]{2,1,0:T(2,128)} %param.10) | copy-start | bytes 1564
  21.3 34.5 %all-to-all-start = ((f32[8,1,62208]{2,1,0:T(1,128)}), f32[8,1,62208]{2,1,0:T(1,128)S(1)}, u32[]{:S(2)}, u32[]{:S(2)}) async-start(f32[8,1,62208]{2,1,0:T(1,128)} %reshape.704), calls=%async_computation | async-start | bytes 3981312 | tf_op jit(solution)/shard_map/all_to_all | solution.py:129
  31.6 32.0 %copy-start.16 = (s32[65]{0:T(128)}, s32[65]{0:T(128)S(1)}, u32[]{:S(2)}) copy-start(s32[65]{0:T(128)S(1)} %get-tuple-element.41) | copy-start | bytes 784
  31.6 32.0 %copy-start.17 = (s32[65]{0:T(128)}, s32[65]{0:T(128)S(1)}, u32[]{:S(2)}) copy-start(s32[65]{0:T(128)S(1)} %get-tuple-element.42) | copy-start | bytes 784
  95.9 7.4 %copy-start.15 = (s32[648]{0:T(1024)S(1)}, s32[648]{0:T(1024)}, u32[]{:S(2)}) copy-start(s32[648]{0:T(1024)} %param.9) | copy-start | bytes 7780
  98.5 13.5 %all-to-all-start.1 = ((f32[8,1,15552]{2,1,0:T(1,128)}), f32[8,1,15552]{2,1,0:T(1,128)S(1)}, u32[]{:S(2)}, u32[]{:S(2)}) async-start(f32[8,1,15552]{2,1,0:T(1,128)} %reshape.706), calls=%async_computation.1 | async-start | bytes 999424 | tf_op jit(solution)/shard_map/all_to_all | solution.py:134
  122.4 11.9 %collective-permute-start = (f32[1,194,65]{1,2,0:T(8,128)S(1)}, f32[1,194,65]{1,2,0:T(8,128)S(1)}, u32[]{:S(2)}, u32[]{:S(2)}) collective-permute-start(f32[1,194,65]{1,2,0:T(8,128)S(1)} %bitcast.191), channel_id=1, source_target_pairs={{0,8},{8,16},{16,24},{24,32},{32,40},{40,48},{48,56},{56,64},{64,7... | collective-permute-start | bytes 151328 | tf_op jit(solution)/shard_map/ppermute | solution.py:26
  125.0 11.2 %collective-permute-start.1 = (f32[1,194,65]{1,2,0:T(8,128)S(1)}, f32[1,194,65]{1,2,0:T(8,128)S(1)}, u32[]{:S(2)}, u32[]{:S(2)}) collective-permute-start(f32[1,194,65]{1,2,0:T(8,128)S(1)} %bitcast.190), channel_id=1, source_target_pairs={{8,0},{16,8},{24,16},{32,24},{40,32},{48,40},{56,48},{64,56},{72,6... | collective-permute-start | bytes 151328 | tf_op jit(solution)/shard_map/ppermute | solution.py:29
  140.6 0.9 copy-start.4
  140.9 1.3 copy-start.1
  142.3 1.1 copy-start.11
  142.3 1.1 copy-start.13
  142.3 0.9 slice-start
  143.8 17.7 %copy-start.5 = (f32[512,81]{1,0:T(8,128)S(1)}, f32[512,81]{1,0:T(8,128)}, u32[]{:S(2)}) copy-start(f32[512,81]{1,0:T(8,128)} %broadcast_bitcast_fusion.1) | copy-start | bytes 497668
  151.5 10.3 %collective-permute-start.2 = (f32[1,64,65]{1,2,0:T(8,128)S(1)}, f32[1,64,65]{1,2,0:T(8,128)S(1)}, u32[]{:S(2)}, u32[]{:S(2)}) collective-permute-start(f32[1,64,65]{1,2,0:T(8,128)S(1)} %bitcast.194), channel_id=1, source_target_pairs={{0,8},{8,16},{16,24},{24,32},{32,40},{40,48},{48,56},{56,64},{64,7... | collective-permute-start | bytes 49928 | tf_op jit(solution)/shard_map/ppermute | solution.py:26
  153.4 9.5 %collective-permute-start.3 = (f32[1,64,65]{1,2,0:T(8,128)S(1)}, f32[1,64,65]{1,2,0:T(8,128)S(1)}, u32[]{:S(2)}, u32[]{:S(2)}) collective-permute-start(f32[1,64,65]{1,2,0:T(8,128)S(1)} %bitcast.192), channel_id=1, source_target_pairs={{8,0},{16,8},{24,16},{32,24},{40,32},{48,40},{56,48},{64,56},{72,6... | collective-permute-start | bytes 49928 | tf_op jit(solution)/shard_map/ppermute | solution.py:29
  161.8 4.8 copy-start.7
  164.1 3.0 copy-start.6
  165.9 1.8 copy-start.14
  175.3 9.2 %collective-permute-start.4 = (f32[1,64,65]{1,2,0:T(8,128)S(1)}, f32[1,64,65]{1,2,0:T(8,128)S(1)}, u32[]{:S(2)}, u32[]{:S(2)}) collective-permute-start(f32[1,64,65]{1,2,0:T(8,128)S(1)} %bitcast.197), channel_id=1, source_target_pairs={{0,8},{8,16},{16,24},{24,32},{32,40},{40,48},{48,56},{56,64},{64,7... | collective-permute-start | bytes 49928 | tf_op jit(solution)/shard_map/ppermute | solution.py:26
  177.2 8.9 %collective-permute-start.5 = (f32[1,64,65]{1,2,0:T(8,128)S(1)}, f32[1,64,65]{1,2,0:T(8,128)S(1)}, u32[]{:S(2)}, u32[]{:S(2)}) collective-permute-start(f32[1,64,65]{1,2,0:T(8,128)S(1)} %bitcast.196), channel_id=1, source_target_pairs={{8,0},{16,8},{24,16},{32,24},{40,32},{48,40},{56,48},{64,56},{72,6... | collective-permute-start | bytes 49928 | tf_op jit(solution)/shard_map/ppermute | solution.py:29
  480.8 9.9 %collective-permute-start.6 = (f32[1,64,65]{1,2,0:T(8,128)S(1)}, f32[1,64,65]{1,2,0:T(8,128)S(1)}, u32[]{:S(2)}, u32[]{:S(2)}) collective-permute-start(f32[1,64,65]{1,2,0:T(8,128)S(1)} %bitcast.195), channel_id=1, source_target_pairs={{0,8},{8,16},{16,24},{24,32},{32,40},{40,48},{48,56},{56,64},{64,7... | collective-permute-start | bytes 49928 | tf_op jit(solution)/shard_map/ppermute | solution.py:26
  484.7 7.1 %collective-permute-start.7 = (f32[1,64,65]{1,2,0:T(8,128)S(1)}, f32[1,64,65]{1,2,0:T(8,128)S(1)}, u32[]{:S(2)}, u32[]{:S(2)}) collective-permute-start(f32[1,64,65]{1,2,0:T(8,128)S(1)} %bitcast.193), channel_id=1, source_target_pairs={{8,0},{16,8},{24,16},{32,24},{40,32},{48,40},{56,48},{64,56},{72,6... | collective-permute-start | bytes 49928 | tf_op jit(solution)/shard_map/ppermute | solution.py:29
  640.3 1.5 copy-start.2
where the time goes:
time: 649 us; the launch traced here: 643 us
  blocking collectives  425 us (65%)
  local copies, waits for them, and re-layouts  53.7 us (8%)
  starting transfers between devices  53.7 us (8%)
  other arithmetic  49 us (8%)
  waiting for transfers between devices  32.8 us (5%)
  matrix products  26.8 us (4%)
    psum x2, blocking collectives, squares(): return lax.psum(inner_product(vector, vector), 'elem')  282 us
    psum x1, blocking collectives, on_device(): step_size = norm_now / lax.psum(inner_product(direction, applied), 'elem')  143 us
    ppermute x4, starting transfers between devices, padded(): lax.ppermute(lax.slice_in_dim(block, 0, width, axis=dim), axis, backward)  29.4 us
    all_to_all x1, waiting for transfers between devices, on_device(): lax.all_to_all(fields, 'mode', split_axis=2, concat_axis=1, tiled=True)  24 us
    scatter-add x4, other arithmetic, assemble(): jnp.zeros((values.shape[0], LOCAL_NODES), jnp.float32).at[:, local_ids]  23.9 us
    unnamed x42, local copies, waits for them, and re-layouts  16.3 us
    dot_general x1, matrix products, on_device(): jnp.einsum('nj,fjm->fnm', synthesis, planes_all, precision=lax.Precision....  15.7 us
  transfers between devices with their start and end apart: 10, of which 4 were waited for; matrix products, arithmetic and copies ran while one was open for 1% of the time, Pallas kernels for 0%

commit v1 on v0

v1 whole, which is shorter than its diff:
```python
import functools
import math

import jax
import jax.numpy as jnp
import numpy as np
from jax import lax
from jax.experimental import pallas as pl
from jax.experimental.pallas import tpu as pltpu
from jax.sharding import PartitionSpec as P

SIDE = 9
QUAD_NODES = 81
PLANES = 512
QUADS = 8
EDGE = 65
LANES = 128
WIDE = QUADS * LANES
PACK = 256
ROWS = 64
KEPT = 384
STACK = 200

PENALTY = 1.0
TIME_STEP = 0.01

f32 = jnp.float32
bf16 = jnp.bfloat16


def legendre_pair(points, degree):
    previous = points * 0.0 + 1.0
    current = points.copy()
    for order in range(2, degree + 1):
        following = ((2.0 * order - 1.0) * points * current - (order - 1.0) * previous) / order
        previous = current
        current = following
    return (previous, current)


def derivative_matrix():
    degree = SIDE - 1
    points = np.cos(math.pi * np.arange(degree + 1) / degree)
    for sweep in range(100):
        lower, upper = legendre_pair(points, degree)
        points = points - (points * upper - lower) / ((degree + 1.0) * upper)
    points = points[::-1].copy()
    values = legendre_pair(points, degree)[1]
    identity = np.eye(SIDE)
    differ = points[:, None] - points[None, :] + identity
    matrix = np.where(identity > 0.5, 0.0, values[:, None] / (values[None, :] * differ))
    matrix[0, 0] = -degree * (degree + 1) / 4.0
    matrix[degree, degree] = degree * (degree + 1) / 4.0
    return matrix


def halves(table):
    high = table.astype(np.float32).astype(jnp.bfloat16)
    low = (table - high.astype(np.float64)).astype(np.float32).astype(jnp.bfloat16)
    return np.stack([high, low])


def derivative_tables():
    matrix = derivative_matrix()
    table = np.zeros((LANES, 2 * LANES))
    table[:QUAD_NODES, :QUAD_NODES] = np.kron(matrix, np.eye(SIDE)).T
    table[:QUAD_NODES, LANES : LANES + QUAD_NODES] = np.kron(np.eye(SIDE), matrix).T
    table = table.astype(np.float32).astype(np.float64)
    return halves(table), halves(table.T.copy())


def fourier_tables():
    positions = np.arange(PLANES)
    mode_number = positions // 2
    frequency = np.where(positions == 1, PLANES // 2, mode_number)
    angles = 2.0 * math.pi / PLANES * (positions[:, None] * frequency[None, :] % PLANES)
    cosine = np.cos(angles)
    sines = np.sin(angles)
    cos_like = (positions % 2 == 0) | (positions == 1)
    synthesis = np.where(cos_like[None, :], cosine, sines)
    wavenumber = 8.0 / PLANES * mode_number
    slope = np.where(cos_like[None, :], -wavenumber[None, :] * sines, wavenumber[None, :] * cosine)
    weight = np.where(positions < 2, 1.0, 2.0) / PLANES
    retained = (mode_number <= PLANES // 3) & (positions != 1)
    forward = (synthesis * np.where(retained, weight, 0.0)[None, :]).T
    return halves(np.concatenate([synthesis, slope])), halves(forward[:KEPT])


def split2(x):
    high = x.astype(bf16)
    return high, (x - high.astype(f32)).astype(bf16)


def split3(x):
    high = x.astype(bf16)
    rest = x - high.astype(f32)
    middle = rest.astype(bf16)
    return high, middle, (rest - middle.astype(f32)).astype(bf16)


def mm(a, b):
    return jnp.dot(a, b, preferred_element_type=f32)


def times_table(x, table):
    rows = x.shape[0]
    high, low = split2(x)
    both = mm(jnp.concatenate([high, low], axis=0), table[0])
    return both[:rows] + both[rows:] + mm(high, table[1])


def table_times(table, x):
    high, low = split2(x)
    cols = x.shape[1]
    both = mm(table[0], jnp.concatenate([high, low], axis=1))
    return both[:, :cols] + both[:, cols:] + mm(table[1], high)


def times_incidence(x, incidence):
    rows = x.shape[0]
    out = mm(jnp.concatenate(split3(x), axis=0), incidence)
    return out[:rows] + (out[rows : 2 * rows] + out[2 * rows :])


def stacked(x):
    return jnp.concatenate([x[:, LANES * q : LANES * (q + 1)] for q in range(QUADS)], axis=0)


def unstacked(x):
    rows = x.shape[0] // QUADS
    return jnp.concatenate([x[rows * q : rows * (q + 1)] for q in range(QUADS)], axis=1)


def gradient(x, metric, table):
    derived = times_table(stacked(x), table)
    along_r = unstacked(derived[:, :LANES])
    along_s = unstacked(derived[:, LANES:])
    return (
        metric[0:1] * along_r + metric[2:3] * along_s,
        metric[1:2] * along_r + metric[3:4] * along_s,
    )


def rates(mode):
    row = lax.broadcasted_iota(jnp.int32, (ROWS, 1), 0)
    return (8.0 / PLANES) * ((mode * ROWS + row) // 2).astype(f32), row % 2 == 0


def along_z(x, mode):
    rate, even = rates(mode)
    return rate * jnp.where(even, pltpu.roll(x, ROWS - 1, 0), -pltpu.roll(x, 1, 0))


def unpacked(x, field):
    if field:
        x = pltpu.roll(x, PACK - QUAD_NODES * field, 1)
    return x[:, :LANES]


def pack_kernel(velocity, packed):
    for q in range(QUADS):
        for c in range(3):
            packed[q, :, QUAD_NODES * c : QUAD_NODES * (c + 1)] = velocity[
                c, :, QUAD_NODES * q : QUAD_NODES * (q + 1)
            ]
        packed[q, :, 3 * QUAD_NODES :] = jnp.zeros((ROWS, PACK - 3 * QUAD_NODES), f32)


def prepare_kernel(mode, velocity, nodal, ids, edges, field, nodal_wide, own_metric, joins, rims):
    lane = lax.broadcasted_iota(jnp.int32, (1, LANES), 1)
    field[...] = jnp.zeros_like(field)
    nodal_wide[...] = jnp.zeros_like(nodal_wide)
    for q in range(QUADS):
        here = slice(LANES * q, LANES * q + QUAD_NODES)
        there = slice(QUAD_NODES * q, QUAD_NODES * (q + 1))
        for c in range(3):
            field[ROWS * c : ROWS * (c + 1), here] = velocity[c, :, there]
        nodal_wide[0:5, here] = nodal[0:5, there]
        nodal_wide[5:6, here] = jnp.ones((1, QUAD_NODES), f32)
    own = jnp.zeros((8, LANES), f32)
    for q in range(QUADS):
        own = own + jnp.where(mode[0] == q, nodal_wide[:, LANES * q : LANES * (q + 1)], 0.0)
    own_metric[...] = own
    ids_row = [
        jnp.concatenate(
            [
                ids[:, QUAD_NODES * q : QUAD_NODES * (q + 1)],
                jnp.full((1, LANES - QUAD_NODES), -1, jnp.int32),
            ],
            axis=1,
        ).astype(f32)
        for q in range(QUADS)
    ]
    ids_wide = jnp.concatenate(ids_row, axis=1)
    edge_row = [
        jnp.concatenate(
            [edges[s : s + 1, :], jnp.full((1, LANES - EDGE), -2, jnp.int32)], axis=1
        ).astype(f32)
        for s in range(2)
    ]
    edge_wide = jnp.concatenate(edge_row, axis=1)
    columns = jnp.transpose(jnp.concatenate(ids_row, axis=0))
    edge_columns = jnp.transpose(jnp.concatenate(edge_row + [edge_row[0]] * 6, axis=0))
    for q in range(QUADS):
        column = columns[:, q : q + 1]
        joins[LANES * q : LANES * (q + 1), :] = jnp.where(column == ids_wide, 1.0, 0.0).astype(bf16)
        rims[LANES * q : LANES * (q + 1), :] = jnp.where(column == edge_wide, 1.0, 0.0).astype(bf16)
    for s in range(2):
        column = edge_columns[:, s : s + 1]
        joins[WIDE + LANES * s : WIDE + LANES * (s + 1), :] = jnp.where(
            column == ids_wide, 1.0, 0.0
        ).astype(bf16)


def convect_kernel(packed, own_metric, synthesis, forward, derive, out, products):
    coefficients = packed[...].reshape(PLANES, PACK)
    high, low = split2(coefficients)
    both = jnp.concatenate([high, low], axis=1)
    metric = own_metric[...]
    lane = lax.broadcasted_iota(jnp.int32, (1, LANES), 1)
    inside = lane < QUAD_NODES
    table = (derive[0], derive[1])
    chunk = 128

    def planes(first):
        rows = pl.ds(first, chunk)
        wide = mm(synthesis[0, rows, :], both)
        return wide[:, :PACK] + wide[:, PACK:] + mm(synthesis[1, rows, :], high)

    for first in range(0, PLANES, chunk):
        value = planes(first)
        slope = planes(PLANES + first)
        speed = [unpacked(value, c) for c in range(3)]
        derived = times_table(jnp.concatenate(speed, axis=0), table)
        weight_r = speed[0] * metric[0:1] + speed[1] * metric[1:2]
        weight_s = speed[0] * metric[2:3] + speed[1] * metric[3:4]
        total = None
        for c in range(3):
            part = derived[chunk * c : chunk * (c + 1)]
            term = (
                weight_r * part[:, :LANES]
                + weight_s * part[:, LANES:]
                + speed[2] * unpacked(slope, c)
            )
            term = jnp.where(inside, -term, 0.0)
            term = jnp.concatenate([term, jnp.zeros((chunk, PACK - LANES), f32)], axis=1)
            if c:
                term = pltpu.roll(term, QUAD_NODES * c, 1)
            total = term if total is None else total + term
        products[first : first + chunk, :] = total
    spectral = table_times((forward[0], forward[1]), products[...])
    out[0 : KEPT // ROWS] = spectral.reshape(KEPT // ROWS, ROWS, PACK)
    out[KEPT // ROWS :] = jnp.zeros((QUADS - KEPT // ROWS, ROWS, PACK), f32)


def weigh_kernel(spectral, nodal, rims, share, to_prev, to_next):
    for q in range(QUADS):
        here = slice(LANES * q, LANES * (q + 1))
        mass = nodal[4:5, here]
        block = spectral[q]
        for c in range(3):
            share[ROWS * c : ROWS * (c + 1), here] = mass * jnp.where(
                mass > 0.0, unpacked(block, c), 0.0
            )
    share[3 * ROWS : 3 * ROWS + 1, :] = nodal[4:5, :]
    share[3 * ROWS + 1 : 3 * ROWS + 2, :] = nodal[5:6, :]
    share[3 * ROWS + 2 :, :] = jnp.zeros((STACK - 3 * ROWS - 2, WIDE), f32)
    rim = times_incidence(share[...], rims[...])
    to_prev[...] = rim[:, :LANES]
    to_next[...] = rim[:, LANES:]


def joined(share, from_prev, from_next, joins):
    return times_incidence(
        jnp.concatenate([share[...], from_prev[...], from_next[...]], axis=1), joins[...]
    )


def star_kernel(
    mode, share, from_prev, from_next, joins, rims, field, nodal, derive,
    star, inverse, share_out, to_prev, to_next,
):
    total = joined(share, from_prev, from_next, joins)
    metric = nodal[...]
    inside = metric[5:6] > 0.0
    scale = TIME_STEP / jnp.where(inside, total[3 * ROWS : 3 * ROWS + 1], 1.0)
    inverse[...] = jnp.where(
        inside, 1.0 / jnp.where(inside, total[3 * ROWS + 1 : 3 * ROWS + 2], 1.0), 0.0
    )
    star[...] = field[...] + scale * total[: 3 * ROWS]
    table = (derive[0], derive[1])
    star_x = gradient(star[0:ROWS], metric, table)[0]
    star_y = gradient(star[ROWS : 2 * ROWS], metric, table)[1]
    divergence = star_x + star_y + along_z(star[2 * ROWS :], mode[0])
    result = (-1.0 / TIME_STEP) * (metric[4:5] * divergence)
    share_out[...] = result
    rim = times_incidence(result, rims[...])
    to_prev[...] = rim[:, :LANES]
    to_next[...] = rim[:, LANES:]


def lane_sum(x):
    total = x[:, :LANES]
    for q in range(1, QUADS):
        total = total + x[:, LANES * q : LANES * (q + 1)]
    return jnp.sum(total, axis=1, keepdims=True)


def helmholtz_kernel(
    mode, share, from_prev, from_next, joins, rims, nodal, inverse, derive, derive_back,
    right, right_x, right_y, share_out, to_prev, to_next, sums,
):
    total = joined(share, from_prev, from_next, joins)
    metric = nodal[...]
    mass = metric[4:5]
    rate, even = rates(mode[0])
    shift = rate * rate + PENALTY
    grad_x, grad_y = gradient(total, metric, (derive[0], derive[1]))
    right[...] = total
    right_x[...] = grad_x
    right_y[...] = grad_y
    flux_x = mass * grad_x
    flux_y = mass * grad_y
    weighted = shift * (mass * total)
    part_r = metric[0:1] * flux_x + metric[1:2] * flux_y
    part_s = metric[2:3] * flux_x + metric[3:4] * flux_y
    both = jnp.concatenate([stacked(part_r), stacked(part_s)], axis=1)
    result = unstacked(times_table(both, (derive_back[0], derive_back[1]))) + weighted
    share_out[...] = result
    rim = times_incidence(result, rims[...])
    to_prev[...] = rim[:, :LANES]
    to_next[...] = rim[:, LANES:]
    square = lane_sum(total * total * inverse[...])
    energy = lane_sum(flux_x * grad_x + flux_y * grad_y + weighted * total)
    column = lax.broadcasted_iota(jnp.int32, (ROWS, LANES), 1)
    sums[...] = jnp.where(column == 0, square, jnp.where(column == 1, energy, 0.0))


def image_kernel(
    mode, share, from_prev, from_next, joins, nodal, inverse, derive, sums,
    image, image_x, image_y, spread,
):
    total = joined(share, from_prev, from_next, joins)
    metric = nodal[...]
    mass = metric[4:5]
    rate, even = rates(mode[0])
    shift = rate * rate + PENALTY
    grad_x, grad_y = gradient(total, metric, (derive[0], derive[1]))
    image[...] = total
    image_x[...] = grad_x
    image_y[...] = grad_y
    square = lane_sum(total * total * inverse[...])
    energy = lane_sum(mass * (grad_x * grad_x + grad_y * grad_y + shift * (total * total)))
    column = lax.broadcasted_iota(jnp.int32, (ROWS, LANES), 1)
    table = jnp.where(column == 2, square, jnp.where(column == 3, energy, sums[...]))
    table = jnp.concatenate([table, jnp.zeros((LANES - ROWS, LANES), f32)], axis=0)
    turned = jnp.transpose(table)
    short = jnp.concatenate(
        [
            turned[0:1] + pltpu.roll(turned[1:2], ROWS, 1),
            turned[2:3] + pltpu.roll(turned[3:4], ROWS, 1),
        ],
        axis=1,
    )
    spread[...] = jnp.broadcast_to(short, spread.shape)


def finish_kernel(
    mode, gathered, star, right, right_x, right_y, image, image_x, image_y,
    velocity_out, pressure_out,
):
    sums = jnp.sum(gathered[...], axis=0, keepdims=True)
    first = sums[:, :LANES]
    second = sums[:, LANES:]
    g0 = first
    g1 = pltpu.roll(first, ROWS, 1)
    g2 = second
    g3 = pltpu.roll(second, ROWS, 1)
    step0 = g0 / g1
    new = step0 * step0 * g2 - g0
    ratio = new / g0
    curve = (1.0 + ratio) * ((1.0 + ratio) * g1 - 2.0 * step0 * g2) + step0 * step0 * g3
    step1 = new / curve
    by_right = step0 + step1 * (1.0 + ratio)
    by_image = -step1 * step0
    pair = jnp.concatenate([by_right, by_image, jnp.zeros((6, LANES), f32)], axis=0)
    turned = jnp.transpose(pair)
    by_right = turned[:ROWS, 0:1]
    by_image = turned[:ROWS, 1:2]
    pressure = by_right * right[...] + by_image * image[...]
    outs = [
        star[0:ROWS] - TIME_STEP * (by_right * right_x[...] + by_image * image_x[...]),
        star[ROWS : 2 * ROWS] - TIME_STEP * (by_right * right_y[...] + by_image * image_y[...]),
        star[2 * ROWS :] - TIME_STEP * along_z(pressure, mode[0]),
    ]
    for q in range(QUADS):
        here = slice(QUAD_NODES * q, QUAD_NODES * (q + 1))
        there = slice(LANES * q, LANES * q + QUAD_NODES)
        for c in range(3):
            velocity_out[c, :, here] = outs[c][:, there]
        pressure_out[:, here] = pressure[:, there]


VMEM = pl.BlockSpec(memory_space=pltpu.VMEM)
SMEM = pl.BlockSpec(memory_space=pltpu.SMEM)


def call(kernel, ins, outs, scratch=(), flops=0, name=None):
    specs = [SMEM if a.dtype == jnp.int32 and a.shape == (1,) else VMEM for a in ins]
    shapes = [jax.ShapeDtypeStruct(s, d) for s, d in outs]
    size = sum(math.prod(a.shape) * a.dtype.itemsize for a in list(ins) + shapes)
    return pl.pallas_call(
        kernel,
        in_specs=specs,
        out_specs=[VMEM] * len(shapes),
        out_shape=shapes,
        scratch_shapes=list(scratch),
        name=name,
        cost_estimate=pl.CostEstimate(flops=flops, bytes_accessed=size, transcendentals=0),
        compiler_params=pltpu.CompilerParams(vmem_limit_bytes=40 * 1024 * 1024),
    )(*ins)


def on_device(velocity, metric, mass, local_ids, edge_ids):
    derive, derive_back = (jnp.asarray(t) for t in derivative_tables())
    synthesis, forward = (jnp.asarray(t) for t in fourier_tables())
    mode = lax.axis_index("mode").astype(jnp.int32).reshape(1)
    count = lax.axis_size("elem")
    onward = [(i, (i + 1) % count) for i in range(count)]
    backward = [(target, source) for source, target in onward]

    def swap(to_prev, to_next):
        return lax.ppermute(to_next, "elem", onward), lax.ppermute(to_prev, "elem", backward)

    (packed,) = call(pack_kernel, [velocity], [((QUADS, ROWS, PACK), f32)], name="pack")
    nodal = jnp.concatenate([metric, mass[None]], axis=0)
    field, nodal, own_metric, joins, rims = call(
        prepare_kernel,
        [mode, velocity, nodal, local_ids[None], edge_ids[0]],
        [
            ((3 * ROWS, WIDE), f32),
            ((8, WIDE), f32),
            ((8, LANES), f32),
            ((WIDE + 2 * LANES, WIDE), bf16),
            ((WIDE, 2 * LANES), bf16),
        ],
        flops=1 << 24,
        name="prepare",
    )
    arrived = lax.all_to_all(packed, "mode", 0, 0)
    (spectral,) = call(
        convect_kernel,
        [arrived, own_metric, synthesis, forward, derive],
        [((QUADS, ROWS, PACK), f32)],
        scratch=[pltpu.VMEM((PLANES, PACK), f32)],
        flops=1 << 30,
        name="convect",
    )
    returned = lax.all_to_all(spectral, "mode", 0, 0)
    rim_out = [((STACK, LANES), f32)] * 2
    share, to_prev, to_next = call(
        weigh_kernel, [returned, nodal, rims], [((STACK, WIDE), f32)] + rim_out,
        flops=1 << 28, name="weigh",
    )
    from_prev, from_next = swap(to_prev, to_next)
    one = ((ROWS, WIDE), f32)
    rim_out = [((ROWS, LANES), f32)] * 2
    star, inverse, share, to_prev, to_next = call(
        star_kernel,
        [mode, share, from_prev, from_next, joins, rims, field, nodal, derive],
        [((3 * ROWS, WIDE), f32), ((1, WIDE), f32), one] + rim_out,
        flops=1 << 29, name="star",
    )
    from_prev, from_next = swap(to_prev, to_next)
    right, right_x, right_y, share, to_prev, to_next, sums = call(
        helmholtz_kernel,
        [mode, share, from_prev, from_next, joins, rims, nodal, inverse, derive, derive_back],
        [one, one, one, one] + rim_out + [((ROWS, LANES), f32)],
        flops=1 << 29, name="helmholtz",
    )
    from_prev, from_next = swap(to_prev, to_next)
    image, image_x, image_y, spread = call(
        image_kernel,
        [mode, share, from_prev, from_next, joins, nodal, inverse, derive, sums],
        [one, one, one, ((count, 1, 2 * LANES), f32)],
        flops=1 << 29, name="image",
    )
    gathered = lax.all_to_all(spread, "elem", 0, 0)
    gathered = gathered.reshape(count, 2 * LANES)
    velocity_new, pressure = call(
        finish_kernel,
        [mode, gathered, star, right, right_x, right_y, image, image_x, image_y],
        [((3, ROWS, QUADS * QUAD_NODES), f32), ((ROWS, QUADS * QUAD_NODES), f32)],
        name="finish",
    )
    return velocity_new, pressure


def solution(mesh):
    in_specs = (
        P(None, "mode", "elem"),
        P(None, "elem"),
        P("elem"),
        P("elem"),
        P("elem", None, None),
    )
    out_specs = (P(None, "mode", "elem"), P("mode", "elem"))
    return jax.shard_map(
        on_device, mesh=mesh, in_specs=in_specs, out_specs=out_specs, check_vma=False
    )
```

time: 649 us -> 108 us (0.17)
  the two profiles are of different devices: /device:TPU:2 before, /device:TPU:8 now
where the time goes in v1:
time: 108 us; the launch traced here: 107 us
  blocking collectives  39.3 us (36%)
  starting transfers between devices  34.3 us (32%)
  Pallas kernels  14 us (13%)
  waiting for transfers between devices  10 us (9%)
  local copies, waits for them, and re-layouts  7.79 us (7%)
    all_to_all x1, blocking collectives, on_device(): gathered = lax.all_to_all(spread, 'elem', 0, 0)  26.5 us
    ppermute x3, starting transfers between devices, swap(): lax.ppermute(to_prev, 'elem', backward)  22.1 us
    pallas_call x8, Pallas kernels, call(): pl.pallas_call(kernel, in_specs=specs, out_specs=[VMEM] * len(shapes), ou...  14 us
    all_to_all x1, blocking collectives, on_device(): returned = lax.all_to_all(spectral, 'mode', 0, 0)  12.8 us
    ppermute x3, starting transfers between devices, swap(): lax.ppermute(to_next, 'elem', onward)  7.81 us
    unnamed x19, local copies, waits for them, and re-layouts  6.41 us
    ppermute x3, waiting for transfers between devices, swap(): lax.ppermute(to_prev, 'elem', backward)  4.66 us
    all_to_all x1, waiting for transfers between devices, on_device(): arrived = lax.all_to_all(packed, 'mode', 0, 0)  4.64 us
  transfers between devices with their start and end apart: 7, of which 5 were waited for; matrix products, arithmetic and copies ran while one was open for 2% of the time, Pallas kernels for 1%

profile of v1, /device:TPU:8, one launch (start us, length us, event | category | flops | bytes accessed | tf_op | source)
XLA Modules:
  0.0 106.9 jit_solution(12187834060670522928)
XLA Ops:
  0.6 0.0 copy-start
  0.6 1.1 copy-done
  1.7 0.0 copy-start.3
  1.7 1.2 %pack.1 = f32[8,64,256]{2,1,0:T(8,128)} custom-call(f32[3,64,648]{2,1,0:T(8,128)S(1)} %copy-done), custom_call_target="tpu_custom_call" | custom-call | bytes 1021952 | tf_op jit(solution)/shard_map/pack/pallas_call | solution.py:412
  2.9 4.3 %all-to-all-start = ((f32[8,64,256]{2,1,0:T(8,128)}), f32[8,64,256]{2,1,0:T(8,128)}, u32[]{:S(2)}, u32[]{:S(2)}) async-start(f32[8,64,256]{2,1,0:T(8,128)} %pack.1), calls=%async_computation | async-start | bytes 1048576 | tf_op jit(solution)/shard_map/all_to_all | solution.py:450
  7.2 0.7 broadcast_in_dim.6
  7.8 0.7 broadcast_in_dim.7.ids
  8.5 0.7 pad_maximum_fusion.nodal
  9.3 0.0 copy-start.1
  9.3 1.1 copy-done.1
  10.3 0.0 copy-start.8
  10.3 0.7 copy-done.8
  11.0 1.1 %prepare.1 = (f32[192,1024]{1,0:T(8,128)S(1)}, f32[8,1024]{1,0:T(8,128)S(1)}, f32[8,128]{1,0:T(8,128)S(1)}, bf16[1280,1024]{1,0:T(8,128)(2,1)S(1)}, bf16[1024,256]{1,0:T(8,128)(2,1)S(1)}) custom-call(s32[1]{0:T(128)} %bitcast.mode, f32[3,64,648]{2,1,0:T(8,128)S(1)} %copy-done.1, f32[5,648]{1,0:T(8,128)S(1)} %pad_maximum_fusion.nodal, ...), custom_call_target="tpu_custom_call" | custom-call | flops 16777216 | bytes 4482764 | tf_op jit(solution)/shard_map/prepare/pallas_call | solution.py:412
  12.1 0.0 copy-start.5
  12.1 0.9 copy-done.5
  13.0 4.6 %all-to-all-done.packed = f32[8,64,256]{2,1,0:T(8,128)} async-done(((f32[8,64,256]{2,1,0:T(8,128)}), f32[8,64,256]{2,1,0:T(8,128)}, u32[]{:S(2)}, u32[]{:S(2)}) %all-to-all-start) | async-done | bytes 524320 | tf_op jit(solution)/shard_map/all_to_all | solution.py:450
  17.6 0.0 copy-done.3
  17.6 0.0 copy-start.2
  17.6 1.6 %copy-done.2 = bf16[2,1024,512]{2,1,0:T(8,128)(2,1)S(1)} copy-done((bf16[2,1024,512]{2,1,0:T(8,128)(2,1)S(1)}, bf16[2,1024,512]{2,1,0:T(8,128)(2,1)}, u32[]{:S(2)}) %copy-start.2) | copy-done | bytes 2097176
  19.2 0.0 copy-start.4
  19.2 1.1 %copy-done.4 = bf16[2,384,512]{2,1,0:T(8,128)(2,1)S(1)} copy-done((bf16[2,384,512]{2,1,0:T(8,128)(2,1)S(1)}, bf16[2,384,512]{2,1,0:T(8,128)(2,1)}, u32[]{:S(2)}) %copy-start.4) | copy-done | bytes 786456
  20.3 0.0 copy-start.6
  20.3 4.1 %convect.1 = f32[8,64,256]{2,1,0:T(8,128)S(1)} custom-call(f32[8,64,256]{2,1,0:T(8,128)} %all-to-all-done.packed, f32[8,128]{1,0:T(8,128)S(1)} %get-tuple-element.26.own_metric, bf16[2,1024,512]{2,1,0:T(8,128)(2,1)S(1)} %copy-done.2, bf16[2,384,512]{2,1,0:T(8,128)(2,1)S(1)} %copy-done.4, bf16[2,128,256]{2,1,0:T(8,128)(2,1)S(1)} %copy-done.3), custom_call_target="tpu_custom_call" | custom-call | flops 1073741824 | bytes 4067328 | tf_op jit(solution)/shard_map/convect/pallas_call | solution.py:412
  24.4 12.8 %all_to_all.15.spectral = f32[8,64,256]{2,1,0:T(8,128)S(1)} all-to-all(f32[8,64,256]{2,1,0:T(8,128)S(1)} %convect.1), channel_id=1, replica_groups=mesh['elem'=64,'mode'=8] {'mode'}, dimensions={0} | all-to-all | bytes 1048576 | tf_op jit(solution)/shard_map/all_to_all | solution.py:459
  37.2 0.7 weigh.1
  37.9 0.0 copy-start.7
  37.9 4.0 %collective-permute-start = (f32[200,128]{1,0:T(8,128)S(1)}, f32[200,128]{1,0:T(8,128)S(1)}, u32[]{:S(2)}, u32[]{:S(2)}) collective-permute-start(f32[200,128]{1,0:T(8,128)S(1)} %get-tuple-element.30), channel_id=1, source_target_pairs={{0,8},{8,16},{16,24},{24,32},{32,40},{40,48},{48,56},{56,64},{64,7... | collective-permute-start | bytes 307208 | tf_op jit(solution)/shard_map/ppermute | solution.py:433
  41.9 9.4 %collective-permute-start.1 = (f32[200,128]{1,0:T(8,128)S(1)}, f32[200,128]{1,0:T(8,128)S(1)}, u32[]{:S(2)}, u32[]{:S(2)}) collective-permute-start(f32[200,128]{1,0:T(8,128)S(1)} %get-tuple-element.31), channel_id=1, source_target_pairs={{8,0},{16,8},{24,16},{32,24},{40,32},{48,40},{56,48},{64,56},{72,6... | collective-permute-start | bytes 307208 | tf_op jit(solution)/shard_map/ppermute | solution.py:433
  51.3 0.7 collective-permute-done.from_prev
  52.0 1.5 %collective-permute-done.1.from_next = f32[200,128]{1,0:T(8,128)S(1)} collective-permute-done((f32[200,128]{1,0:T(8,128)S(1)}, f32[200,128]{1,0:T(8,128)S(1)}, u32[]{:S(2)}, u32[]{:S(2)}) %collective-permute-start.1) | collective-permute-done | bytes 102432 | tf_op jit(solution)/shard_map/ppermute | solution.py:433
  53.5 0.0 copy-done.6
  53.5 2.6 %star.1 = (f32[192,1024]{1,0:T(8,128)S(1)}, f32[1,1024]{1,0:T(1,128)S(1)}, f32[64,1024]{1,0:T(8,128)S(1)}, f32[64,128]{1,0:T(8,128)S(1)}, f32[64,128]{1,0:T(8,128)S(1)}) custom-call(s32[1]{0:T(128)} %bitcast.mode, f32[200,1024]{1,0:T(8,128)S(1)} %get-tuple-element.29.share, f32[200,128]{1,0:T(8,128)S(1)} %collective-permute-done.from_prev, ...), custom_call_target="tpu_custom_call" | custom-call | flops 536870912 | bytes 6238212 | tf_op jit(solution)/shard_map/star/pallas_call | solution.py:412
  56.1 1.9 %collective-permute-start.2 = (f32[64,128]{1,0:T(8,128)S(1)}, f32[64,128]{1,0:T(8,128)S(1)}, u32[]{:S(2)}, u32[]{:S(2)}) collective-permute-start(f32[64,128]{1,0:T(8,128)S(1)} %get-tuple-element.35), channel_id=1, source_target_pairs={{0,8},{8,16},{16,24},{24,32},{32,40},{40,48},{48,56},{56,64},{64,7... | collective-permute-start | bytes 98312 | tf_op jit(solution)/shard_map/ppermute | solution.py:433
  58.0 6.4 %collective-permute-start.3 = (f32[64,128]{1,0:T(8,128)S(1)}, f32[64,128]{1,0:T(8,128)S(1)}, u32[]{:S(2)}, u32[]{:S(2)}) collective-permute-start(f32[64,128]{1,0:T(8,128)S(1)} %get-tuple-element.36), channel_id=1, source_target_pairs={{8,0},{16,8},{24,16},{32,24},{40,32},{48,40},{56,48},{64,56},{72,6... | collective-permute-start | bytes 98312 | tf_op jit(solution)/shard_map/ppermute | solution.py:433
  64.5 0.0 collective-permute-done.2.from_prev
  64.5 1.6 %collective-permute-done.3.from_next = f32[64,128]{1,0:T(8,128)S(1)} collective-permute-done((f32[64,128]{1,0:T(8,128)S(1)}, f32[64,128]{1,0:T(8,128)S(1)}, u32[]{:S(2)}, u32[]{:S(2)}) %collective-permute-start.3) | collective-permute-done | bytes 32800 | tf_op jit(solution)/shard_map/ppermute | solution.py:433
  66.0 0.0 copy-done.7
  66.0 1.7 %helmholtz.1 = (f32[64,1024]{1,0:T(8,128)S(1)}, f32[64,1024]{1,0:T(8,128)S(1)}, f32[64,1024]{1,0:T(8,128)S(1)}, f32[64,1024]{1,0:T(8,128)S(1)}, f32[64,128]{1,0:...) custom-call(s32[1]{0:T(128)} %bitcast.mode, f32[64,1024]{1,0:T(8,128)S(1)} %get-tuple-element.34.share, ...), custom_call_target="tpu_custom_call" | custom-call | flops 536870912 | bytes 4919300 | tf_op jit(solution)/shard_map/helmholtz/pallas_call | solution.py:412
  67.8 1.9 %collective-permute-start.4 = (f32[64,128]{1,0:T(8,128)S(1)}, f32[64,128]{1,0:T(8,128)S(1)}, u32[]{:S(2)}, u32[]{:S(2)}) collective-permute-start(f32[64,128]{1,0:T(8,128)S(1)} %get-tuple-element.39), channel_id=1, source_target_pairs={{0,8},{8,16},{16,24},{24,32},{32,40},{40,48},{48,56},{56,64},{64,7... | collective-permute-start | bytes 98312 | tf_op jit(solution)/shard_map/ppermute | solution.py:433
  69.7 6.3 %collective-permute-start.5 = (f32[64,128]{1,0:T(8,128)S(1)}, f32[64,128]{1,0:T(8,128)S(1)}, u32[]{:S(2)}, u32[]{:S(2)}) collective-permute-start(f32[64,128]{1,0:T(8,128)S(1)} %get-tuple-element.40), channel_id=1, source_target_pairs={{8,0},{16,8},{24,16},{32,24},{40,32},{48,40},{56,48},{64,56},{72,6... | collective-permute-start | bytes 98312 | tf_op jit(solution)/shard_map/ppermute | solution.py:433
  76.1 0.0 collective-permute-done.4.from_prev
  76.1 1.6 %collective-permute-done.5.from_next = f32[64,128]{1,0:T(8,128)S(1)} collective-permute-done((f32[64,128]{1,0:T(8,128)S(1)}, f32[64,128]{1,0:T(8,128)S(1)}, u32[]{:S(2)}, u32[]{:S(2)}) %collective-permute-start.5) | collective-permute-done | bytes 32800 | tf_op jit(solution)/shard_map/ppermute | solution.py:433
  77.6 1.3 %image.1 = (f32[64,1024]{1,0:T(8,128)S(1)}, f32[64,1024]{1,0:T(8,128)S(1)}, f32[64,1024]{1,0:T(8,128)S(1)}, f32[64,1,256]{2,1,0:T(1,128)S(1)}) custom-call(s32[1]{0:T(128)} %bitcast.mode, f32[64,1024]{1,0:T(8,128)S(1)} %get-tuple-element.38.share, f32[64,128]{1,0:T(8,128)S(1)} %collective-permute-done.4.from_prev, ...), custom_call_target="tpu_custom_call" | custom-call | flops 536870912 | bytes 4001796 | tf_op jit(solution)/shard_map/image/pallas_call | solution.py:412
  78.9 26.5 %all_to_all.16 = f32[64,1,256]{2,1,0:T(1,128)S(1)} all-to-all(f32[64,1,256]{2,1,0:T(1,128)S(1)} %get-tuple-element.42), channel_id=1, replica_groups=mesh['elem'=64,'mode'=8] {'elem'}, dimensions={0} | all-to-all | bytes 131072 | tf_op jit(solution)/shard_map/all_to_all | solution.py:488
  105.4 1.5 %finish.1 = (f32[3,64,648]{2,1,0:T(8,128)}, f32[64,648]{1,0:T(8,128)}) custom-call(s32[1]{0:T(128)} %bitcast.mode, f32[64,256]{1,0:T(8,128)S(1)} %bitcast.5, f32[192,1024]{1,0:T(8,128)S(1)} %get-tuple-element.43.star, f32[64,1024]{1,0:T(8,128)S(1)} %get-tuple-element.44.right, f32[64,1024]{1,0:T(8,128)S(1)} %get-tuple-element.45.right_x, ...), custom_call_target="tpu_custom_call" | custom-call | bytes 3088388 | tf_op jit(solution)/shard_map/finish/pallas_call | solution.py:412
  (1 shorter events, 0.0 us)
Async XLA Ops:
  0.6 1.1 copy-start
  1.7 15.9 %copy-start.3 = (bf16[2,128,256]{2,1,0:T(8,128)(2,1)S(1)}, bf16[2,128,256]{2,1,0:T(8,128)(2,1)}, u32[]{:S(2)}) copy-start(bf16[2,128,256]{2,1,0:T(8,128)(2,1)} %constant.12.clone.derive) | copy-start | bytes 393220
  2.9 14.8 %all-to-all-start = ((f32[8,64,256]{2,1,0:T(8,128)}), f32[8,64,256]{2,1,0:T(8,128)}, u32[]{:S(2)}, u32[]{:S(2)}) async-start(f32[8,64,256]{2,1,0:T(8,128)} %pack.1), calls=%async_computation | async-start | bytes 1048576 | tf_op jit(solution)/shard_map/all_to_all | solution.py:450
  9.3 1.1 copy-start.1
  10.3 0.7 copy-start.8
  12.1 0.9 copy-start.5
  17.6 1.6 %copy-start.2 = (bf16[2,1024,512]{2,1,0:T(8,128)(2,1)S(1)}, bf16[2,1024,512]{2,1,0:T(8,128)(2,1)}, u32[]{:S(2)}) copy-start(bf16[2,1024,512]{2,1,0:T(8,128)(2,1)} %constant.14.clone.synthesis) | copy-start | bytes 6291460
  19.2 1.1 %copy-start.4 = (bf16[2,384,512]{2,1,0:T(8,128)(2,1)S(1)}, bf16[2,384,512]{2,1,0:T(8,128)(2,1)}, u32[]{:S(2)}) copy-start(bf16[2,384,512]{2,1,0:T(8,128)(2,1)} %constant.15.clone.forward) | copy-start | bytes 2359300
  20.3 33.2 %copy-start.6 = (f32[192,1024]{1,0:T(8,128)S(1)}, f32[192,1024]{1,0:T(8,128)}, u32[]{:S(2)}) copy-start(f32[192,1024]{1,0:T(8,128)} %copy-done.5) | copy-start | bytes 2359300
  37.9 28.1 %copy-start.7 = (bf16[2,256,128]{2,1,0:T(8,128)(2,1)S(1)}, bf16[2,256,128]{2,1,0:T(8,128)(2,1)}, u32[]{:S(2)}) copy-start(bf16[2,256,128]{2,1,0:T(8,128)(2,1)} %constant.13.clone.derive_back) | copy-start | bytes 393220
  37.9 14.1 %collective-permute-start = (f32[200,128]{1,0:T(8,128)S(1)}, f32[200,128]{1,0:T(8,128)S(1)}, u32[]{:S(2)}, u32[]{:S(2)}) collective-permute-start(f32[200,128]{1,0:T(8,128)S(1)} %get-tuple-element.30), channel_id=1, source_target_pairs={{0,8},{8,16},{16,24},{24,32},{32,40},{40,48},{48,56},{56,64},{64,7... | collective-permute-start | bytes 307208 | tf_op jit(solution)/shard_map/ppermute | solution.py:433
  41.9 11.6 %collective-permute-start.1 = (f32[200,128]{1,0:T(8,128)S(1)}, f32[200,128]{1,0:T(8,128)S(1)}, u32[]{:S(2)}, u32[]{:S(2)}) collective-permute-start(f32[200,128]{1,0:T(8,128)S(1)} %get-tuple-element.31), channel_id=1, source_target_pairs={{8,0},{16,8},{24,16},{32,24},{40,32},{48,40},{56,48},{64,56},{72,6... | collective-permute-start | bytes 307208 | tf_op jit(solution)/shard_map/ppermute | solution.py:433
  56.1 8.4 %collective-permute-start.2 = (f32[64,128]{1,0:T(8,128)S(1)}, f32[64,128]{1,0:T(8,128)S(1)}, u32[]{:S(2)}, u32[]{:S(2)}) collective-permute-start(f32[64,128]{1,0:T(8,128)S(1)} %get-tuple-element.35), channel_id=1, source_target_pairs={{0,8},{8,16},{16,24},{24,32},{32,40},{40,48},{48,56},{56,64},{64,7... | collective-permute-start | bytes 98312 | tf_op jit(solution)/shard_map/ppermute | solution.py:433
  58.0 8.0 %collective-permute-start.3 = (f32[64,128]{1,0:T(8,128)S(1)}, f32[64,128]{1,0:T(8,128)S(1)}, u32[]{:S(2)}, u32[]{:S(2)}) collective-permute-start(f32[64,128]{1,0:T(8,128)S(1)} %get-tuple-element.36), channel_id=1, source_target_pairs={{8,0},{16,8},{24,16},{32,24},{40,32},{48,40},{56,48},{64,56},{72,6... | collective-permute-start | bytes 98312 | tf_op jit(solution)/shard_map/ppermute | solution.py:433
  67.8 8.3 %collective-permute-start.4 = (f32[64,128]{1,0:T(8,128)S(1)}, f32[64,128]{1,0:T(8,128)S(1)}, u32[]{:S(2)}, u32[]{:S(2)}) collective-permute-start(f32[64,128]{1,0:T(8,128)S(1)} %get-tuple-element.39), channel_id=1, source_target_pairs={{0,8},{8,16},{16,24},{24,32},{32,40},{40,48},{48,56},{56,64},{64,7... | collective-permute-start | bytes 98312 | tf_op jit(solution)/shard_map/ppermute | solution.py:433
  69.7 7.9 %collective-permute-start.5 = (f32[64,128]{1,0:T(8,128)S(1)}, f32[64,128]{1,0:T(8,128)S(1)}, u32[]{:S(2)}, u32[]{:S(2)}) collective-permute-start(f32[64,128]{1,0:T(8,128)S(1)} %get-tuple-element.40), channel_id=1, source_target_pairs={{8,0},{16,8},{24,16},{32,24},{40,32},{48,40},{56,48},{64,56},{72,6... | collective-permute-start | bytes 98312 | tf_op jit(solution)/shard_map/ppermute | solution.py:433

commit v2 on v1

--- a/solution.py
+++ b/solution.py
@@ -18,8 +18,10 @@
 WIDE = QUADS * LANES
 PACK = 256
 ROWS = 64
-KEPT = 384
+KEPT = 192
 STACK = 200
+CHUNK = 64
+HALF = 256
 
 PENALTY = 1.0
 TIME_STEP = 0.01
@@ -70,20 +72,9 @@
 
 
 def fourier_tables():
-    positions = np.arange(PLANES)
-    mode_number = positions // 2
-    frequency = np.where(positions == 1, PLANES // 2, mode_number)
-    angles = 2.0 * math.pi / PLANES * (positions[:, None] * frequency[None, :] % PLANES)
-    cosine = np.cos(angles)
-    sines = np.sin(angles)
-    cos_like = (positions % 2 == 0) | (positions == 1)
-    synthesis = np.where(cos_like[None, :], cosine, sines)
-    wavenumber = 8.0 / PLANES * mode_number
-    slope = np.where(cos_like[None, :], -wavenumber[None, :] * sines, wavenumber[None, :] * cosine)
-    weight = np.where(positions < 2, 1.0, 2.0) / PLANES
-    retained = (mode_number <= PLANES // 3) & (positions != 1)
-    forward = (synthesis * np.where(retained, weight, 0.0)[None, :]).T
-    return halves(np.concatenate([synthesis, slope])), halves(forward[:KEPT])
+    index = np.arange(HALF)
+    angles = 2.0 * math.pi / PLANES * (index[:, None] * index[None, :] % PLANES)
+    return np.stack([halves(np.cos(angles)), halves(np.sin(angles))])
 
 
 def split2(x):
@@ -160,14 +151,26 @@
 def pack_kernel(velocity, packed):
     for q in range(QUADS):
         for c in range(3):
-            packed[q, :, QUAD_NODES * c : QUAD_NODES * (c + 1)] = velocity[
-                c, :, QUAD_NODES * q : QUAD_NODES * (q + 1)
-            ]
-        packed[q, :, 3 * QUAD_NODES :] = jnp.zeros((ROWS, PACK - 3 * QUAD_NODES), f32)
-
-
-def prepare_kernel(mode, velocity, nodal, ids, edges, field, nodal_wide, own_metric, joins, rims):
+            start, stop = QUAD_NODES * c, QUAD_NODES * (c + 1)
+            for tile in range(start // LANES, (stop - 1) // LANES + 1):
+                low, high = max(start, LANES * tile), min(stop, LANES * (tile + 1))
+                node = QUAD_NODES * q - start
+                packed[q, tile, :, low - LANES * tile : high - LANES * tile] = velocity[
+                    c, :, node + low : node + high
+                ]
+        packed[q, 1, :, 3 * QUAD_NODES - LANES :] = jnp.zeros((ROWS, PACK - 3 * QUAD_NODES), f32)
+
+
+def matches(column, row):
+    return jnp.where(column == row, 1.0, 0.0)
+
+
+def prepare_kernel(
+    mode, velocity, nodal, ids, edges, fourier, derive,
+    field, nodal_wide, own_metric, joins, rims, fourier_on, derive_on,
+):
     lane = lax.broadcasted_iota(jnp.int32, (1, LANES), 1)
+    inside = lane < QUAD_NODES
     field[...] = jnp.zeros_like(field)
     nodal_wide[...] = jnp.zeros_like(nodal_wide)
     for q in range(QUADS):
@@ -198,66 +201,149 @@
         ).astype(f32)
         for s in range(2)
     ]
-    edge_wide = jnp.concatenate(edge_row, axis=1)
     columns = jnp.transpose(jnp.concatenate(ids_row, axis=0))
-    edge_columns = jnp.transpose(jnp.concatenate(edge_row + [edge_row[0]] * 6, axis=0))
-    for q in range(QUADS):
-        column = columns[:, q : q + 1]
-        joins[LANES * q : LANES * (q + 1), :] = jnp.where(column == ids_wide, 1.0, 0.0).astype(bf16)
-        rims[LANES * q : LANES * (q + 1), :] = jnp.where(column == edge_wide, 1.0, 0.0).astype(bf16)
+    column = [columns[:, q : q + 1] for q in range(QUADS)]
+    row_at = lax.broadcasted_iota(jnp.int32, (LANES, LANES), 0)
+    lane_at = lax.broadcasted_iota(jnp.int32, (LANES, LANES), 1)
+    opens = []
+    for q in range(QUADS):
+        total = jnp.zeros((LANES, LANES), f32)
+        before = jnp.zeros((LANES, LANES), f32)
+        for p in range(QUADS):
+            same = matches(column[p], ids_row[q])
+            total = total + same
+            if p < q:
+                before = before + same
+            if p == q:
+                before = before + jnp.where(row_at < lane_at, same, 0.0)
+        copies = jnp.sum(total, axis=0, keepdims=True)
+        earlier = jnp.sum(before, axis=0, keepdims=True)
+        shared = jnp.where(inside & (copies > 1.5), 1.0, 0.0)
+        opens.append(jnp.where(earlier < 0.5, shared, 0.0))
+        nodal_wide[6:7, LANES * q : LANES * (q + 1)] = jnp.where(inside, 1.0 - shared, 0.0)
+    opens = jnp.concatenate(opens, axis=0)
+    triangle = jnp.where(row_at < lane_at, 1.0, 0.0).astype(bf16)
+    rank = mm(opens.astype(bf16), triangle)
+    counts = jnp.sum(opens, axis=1, keepdims=True)
+    offset = jnp.zeros((1, 1), f32)
+    offsets = []
+    for q in range(QUADS):
+        offsets.append(offset)
+        offset = offset + counts[q : q + 1]
+    slot = jnp.where(opens > 0.5, rank + jnp.concatenate(offsets, axis=0) + float(EDGE), -1.0)
+    slots = jnp.transpose(slot)
+    lanes = lane.astype(f32)
+    hits = jnp.zeros((LANES, LANES), f32)
+    named = jnp.zeros((LANES, LANES), f32)
+    for q in range(QUADS):
+        hit = matches(slots[:, q : q + 1], lanes)
+        hits = hits + hit
+        named = named + hit * column[q]
+    hits = jnp.sum(hits, axis=0, keepdims=True)
+    named = jnp.sum(named, axis=0, keepdims=True)
+    first = jnp.where(lane < EDGE, edge_row[0], jnp.where(hits > 0.5, named, -3.0))
+    keys = [first, edge_row[1]]
+    key_columns = jnp.transpose(jnp.concatenate(keys + [first] * 6, axis=0))
+    for q in range(QUADS):
+        for s in range(2):
+            rims[LANES * q : LANES * (q + 1), LANES * s : LANES * (s + 1)] = matches(
+                column[q], keys[s]
+            ).astype(bf16)
     for s in range(2):
-        column = edge_columns[:, s : s + 1]
-        joins[WIDE + LANES * s : WIDE + LANES * (s + 1), :] = jnp.where(
-            column == ids_wide, 1.0, 0.0
+        joins[LANES * s : LANES * (s + 1), :] = matches(
+            key_columns[:, s : s + 1], ids_wide
         ).astype(bf16)
 
 
-def convect_kernel(packed, own_metric, synthesis, forward, derive, out, products):
-    coefficients = packed[...].reshape(PLANES, PACK)
-    high, low = split2(coefficients)
-    both = jnp.concatenate([high, low], axis=1)
+def convect_kernel(packed, own_metric, fourier, derive, out, even, odd, sums, differences):
+    cosine = (fourier[0, 0], fourier[0, 1])
+    sine = (fourier[1, 0], fourier[1, 1])
     metric = own_metric[...]
     lane = lax.broadcasted_iota(jnp.int32, (1, LANES), 1)
     inside = lane < QUAD_NODES
     table = (derive[0], derive[1])
-    chunk = 128
-
-    def planes(first):
-        rows = pl.ds(first, chunk)
-        wide = mm(synthesis[0, rows, :], both)
-        return wide[:, :PACK] + wide[:, PACK:] + mm(synthesis[1, rows, :], high)
-
-    for first in range(0, PLANES, chunk):
-        value = planes(first)
-        slope = planes(PLANES + first)
+    index = lax.broadcasted_iota(jnp.int32, (HALF, 1), 0)
+    rate = (8.0 / PLANES) * index.astype(f32)
+    sign = jnp.where(index % 2 == 0, 1.0, -1.0)
+    cosines, sines = (
+        jnp.concatenate(
+            [
+                jnp.concatenate(
+                    [packed[m, tile, pl.ds(parity, ROWS // 2, stride=2), :] for tile in range(2)],
+                    axis=1,
+                )
+                for m in range(QUADS)
+            ],
+            axis=0,
+        )
+        for parity in range(2)
+    )
+    highest = sines[0:1]
+    to_even = jnp.concatenate([cosines, rate * sines], axis=1)
+    to_odd = jnp.concatenate([sines, -rate * cosines], axis=1)
+    even[...] = table_times(cosine, to_even)
+    even[:, :PACK] = even[:, :PACK] + sign * highest
+    middle = jnp.sum(sign * to_even, axis=0, keepdims=True)
+    middle = middle + jnp.concatenate([highest, jnp.zeros_like(highest)], axis=1)
+    odd[...] = table_times(sine, to_odd)
+    opening = lax.broadcasted_iota(jnp.int32, (CHUNK, 1), 0) == 0
+    product_middle = None
+    for i in range(HALF // CHUNK):
+        rows = slice(CHUNK * i, CHUNK * (i + 1))
+        part_even = even[rows]
+        part_odd = odd[rows]
+        ahead = part_even + part_odd
+        if i == 0:
+            part_even = jnp.where(opening, middle, part_even)
+        wide = jnp.concatenate([ahead, part_even - part_odd], axis=0)
+        value = wide[:, :PACK]
+        slope = wide[:, PACK:]
         speed = [unpacked(value, c) for c in range(3)]
         derived = times_table(jnp.concatenate(speed, axis=0), table)
         weight_r = speed[0] * metric[0:1] + speed[1] * metric[1:2]
         weight_s = speed[0] * metric[2:3] + speed[1] * metric[3:4]
         total = None
         for c in range(3):
-            part = derived[chunk * c : chunk * (c + 1)]
+            part = derived[2 * CHUNK * c : 2 * CHUNK * (c + 1)]
             term = (
                 weight_r * part[:, :LANES]
                 + weight_s * part[:, LANES:]
                 + speed[2] * unpacked(slope, c)
             )
             term = jnp.where(inside, -term, 0.0)
-            term = jnp.concatenate([term, jnp.zeros((chunk, PACK - LANES), f32)], axis=1)
+            term = jnp.concatenate([term, jnp.zeros((2 * CHUNK, PACK - LANES), f32)], axis=1)
             if c:
                 term = pltpu.roll(term, QUAD_NODES * c, 1)
             total = term if total is None else total + term
-        products[first : first + chunk, :] = total
-    spectral = table_times((forward[0], forward[1]), products[...])
-    out[0 : KEPT // ROWS] = spectral.reshape(KEPT // ROWS, ROWS, PACK)
-    out[KEPT // ROWS :] = jnp.zeros((QUADS - KEPT // ROWS, ROWS, PACK), f32)
+        ahead = total[:CHUNK]
+        mirror = total[CHUNK:]
+        differences[rows, :] = ahead - mirror
+        if i == 0:
+            product_middle = mirror[0:1]
+            mirror = jnp.where(opening, 0.0, mirror)
+        sums[rows, :] = ahead + mirror
+    index = index[:KEPT]
+    weight = jnp.where(index <= PLANES // 3, 2.0 / PLANES, 0.0)
+    kept = [(fourier[t, 0, :KEPT], fourier[t, 1, :KEPT]) for t in range(2)]
+    result = table_times(kept[0], sums[...]) + sign[:KEPT] * product_middle
+    results = [jnp.where(index == 0, 0.5 * weight, weight) * result]
+    result = table_times(kept[1], differences[...])
+    results.append(jnp.where(index == 0, 0.0, weight) * result)
+    half = ROWS // 2
+    for m in range(KEPT // half):
+        for tile in range(2):
+            for parity in range(2):
+                out[m, tile, pl.ds(parity, half, stride=2), :] = results[parity][
+                    half * m : half * (m + 1), LANES * tile : LANES * (tile + 1)
+                ]
+    out[KEPT // half :] = jnp.zeros((QUADS - KEPT // half, 2, ROWS, LANES), f32)
 
 
 def weigh_kernel(spectral, nodal, rims, share, to_prev, to_next):
     for q in range(QUADS):
         here = slice(LANES * q, LANES * (q + 1))
         mass = nodal[4:5, here]
-        block = spectral[q]
+        block = jnp.concatenate([spectral[q, 0], spectral[q, 1]], axis=1)
         for c in range(3):
             share[ROWS * c : ROWS * (c + 1), here] = mass * jnp.where(
                 mass > 0.0, unpacked(block, c), 0.0
@@ -270,18 +356,19 @@
     to_next[...] = rim[:, LANES:]
 
 
-def joined(share, from_prev, from_next, joins):
-    return times_incidence(
-        jnp.concatenate([share[...], from_prev[...], from_next[...]], axis=1), joins[...]
-    )
+def joined(share, own, from_prev, from_next, joins, single):
+    lane = lax.broadcasted_iota(jnp.int32, (1, LANES), 1)
+    near = jnp.where(lane < EDGE, from_prev[...], own[...])
+    sums = jnp.concatenate([near, from_next[...]], axis=1)
+    return share[...] * single + times_incidence(sums, joins[...])
 
 
 def star_kernel(
-    mode, share, from_prev, from_next, joins, rims, field, nodal, derive,
+    mode, share, own, from_prev, from_next, joins, rims, field, nodal, derive,
     star, inverse, share_out, to_prev, to_next,
 ):
-    total = joined(share, from_prev, from_next, joins)
     metric = nodal[...]
+    total = joined(share, own, from_prev, from_next, joins, metric[6:7])
     inside = metric[5:6] > 0.0
     scale = TIME_STEP / jnp.where(inside, total[3 * ROWS : 3 * ROWS + 1], 1.0)
     inverse[...] = jnp.where(
@@ -307,11 +394,11 @@
 
 
 def helmholtz_kernel(
-    mode, share, from_prev, from_next, joins, rims, nodal, inverse, derive, derive_back,
+    mode, share, own, from_prev, from_next, joins, rims, nodal, inverse, derive, derive_back,
     right, right_x, right_y, share_out, to_prev, to_next, sums,
 ):
-    total = joined(share, from_prev, from_next, joins)
     metric = nodal[...]
+    total = joined(share, own, from_prev, from_next, joins, metric[6:7])
     mass = metric[4:5]
     rate, even = rates(mode[0])
     shift = rate * rate + PENALTY
@@ -337,11 +424,11 @@
 
 
 def image_kernel(
-    mode, share, from_prev, from_next, joins, nodal, inverse, derive, sums,
+    mode, share, own, from_prev, from_next, joins, nodal, inverse, derive, sums,
     image, image_x, image_y, spread,
 ):
-    total = joined(share, from_prev, from_next, joins)
     metric = nodal[...]
+    total = joined(share, own, from_prev, from_next, joins, metric[6:7])
     mass = metric[4:5]
     rate, even = rates(mode[0])
     shift = rate * rate + PENALTY
@@ -388,11 +475,12 @@
     by_right = turned[:ROWS, 0:1]
     by_image = turned[:ROWS, 1:2]
     pressure = by_right * right[...] + by_image * image[...]
-    outs = [
-        star[0:ROWS] - TIME_STEP * (by_right * right_x[...] + by_image * image_x[...]),
-        star[ROWS : 2 * ROWS] - TIME_STEP * (by_right * right_y[...] + by_image * image_y[...]),
-        star[2 * ROWS :] - TIME_STEP * along_z(pressure, mode[0]),
+    slopes = [
+        by_right * right_x[...] + by_image * image_x[...],
+        by_right * right_y[...] + by_image * image_y[...],
+        along_z(pressure, mode[0]),
     ]
+    outs = [star[ROWS * c : ROWS * (c + 1)] - TIME_STEP * slopes[c] for c in range(3)]
     for q in range(QUADS):
         here = slice(QUAD_NODES * q, QUAD_NODES * (q + 1))
         there = slice(LANES * q, LANES * q + QUAD_NODES)
@@ -403,18 +491,21 @@
 
 VMEM = pl.BlockSpec(memory_space=pltpu.VMEM)
 SMEM = pl.BlockSpec(memory_space=pltpu.SMEM)
-
-
-def call(kernel, ins, outs, scratch=(), flops=0, name=None):
+ANY = pl.BlockSpec(memory_space=pl.ANY)
+
+
+def call(kernel, ins, outs, scratch=(), flops=0, name=None, aliases={}):
     specs = [SMEM if a.dtype == jnp.int32 and a.shape == (1,) else VMEM for a in ins]
+    specs = [ANY if i in aliases else spec for i, spec in enumerate(specs)]
     shapes = [jax.ShapeDtypeStruct(s, d) for s, d in outs]
     size = sum(math.prod(a.shape) * a.dtype.itemsize for a in list(ins) + shapes)
     return pl.pallas_call(
         kernel,
         in_specs=specs,
-        out_specs=[VMEM] * len(shapes),
+        out_specs=[ANY if i in aliases.values() else VMEM for i in range(len(shapes))],
         out_shape=shapes,
         scratch_shapes=list(scratch),
+        input_output_aliases=aliases,
         name=name,
         cost_estimate=pl.CostEstimate(flops=flops, bytes_accessed=size, transcendentals=0),
         compiler_params=pltpu.CompilerParams(vmem_limit_bytes=40 * 1024 * 1024),
@@ -423,7 +514,7 @@
 
 def on_device(velocity, metric, mass, local_ids, edge_ids):
     derive, derive_back = (jnp.asarray(t) for t in derivative_tables())
-    synthesis, forward = (jnp.asarray(t) for t in fourier_tables())
+    fourier = jnp.asarray(fourier_tables())
     mode = lax.axis_index("mode").astype(jnp.int32).reshape(1)
     count = lax.axis_size("elem")
     onward = [(i, (i + 1) % count) for i in range(count)]
@@ -432,27 +523,34 @@
     def swap(to_prev, to_next):
         return lax.ppermute(to_next, "elem", onward), lax.ppermute(to_prev, "elem", backward)
 
-    (packed,) = call(pack_kernel, [velocity], [((QUADS, ROWS, PACK), f32)], name="pack")
+    block = (QUADS, 2, ROWS, LANES)
+    (packed,) = call(
+        pack_kernel, [velocity], [(block, f32)],
+        name="pack",
+    )
     nodal = jnp.concatenate([metric, mass[None]], axis=0)
-    field, nodal, own_metric, joins, rims = call(
+    tables = [fourier, derive]
+    field, nodal, own_metric, joins, rims, fourier, derive = call(
         prepare_kernel,
-        [mode, velocity, nodal, local_ids[None], edge_ids[0]],
+        [mode, velocity, nodal, local_ids[None], edge_ids[0]] + tables,
         [
             ((3 * ROWS, WIDE), f32),
             ((8, WIDE), f32),
             ((8, LANES), f32),
-            ((WIDE + 2 * LANES, WIDE), bf16),
+            ((2 * LANES, WIDE), bf16),
             ((WIDE, 2 * LANES), bf16),
-        ],
+        ]
+        + [(t.shape, bf16) for t in tables],
         flops=1 << 24,
         name="prepare",
+        aliases={5: 5, 6: 6},
     )
     arrived = lax.all_to_all(packed, "mode", 0, 0)
     (spectral,) = call(
         convect_kernel,
-        [arrived, own_metric, synthesis, forward, derive],
-        [((QUADS, ROWS, PACK), f32)],
-        scratch=[pltpu.VMEM((PLANES, PACK), f32)],
+        [arrived, own_metric, fourier, derive],
+        [(block, f32)],
+        scratch=[pltpu.VMEM((HALF, 2 * PACK), f32)] * 2 + [pltpu.VMEM((HALF, PACK), f32)] * 2,
         flops=1 << 30,
         name="convect",
     )
@@ -467,21 +565,21 @@
     rim_out = [((ROWS, LANES), f32)] * 2
     star, inverse, share, to_prev, to_next = call(
         star_kernel,
-        [mode, share, from_prev, from_next, joins, rims, field, nodal, derive],
+        [mode, share, to_prev, from_prev, from_next, joins, rims, field, nodal, derive],
         [((3 * ROWS, WIDE), f32), ((1, WIDE), f32), one] + rim_out,
         flops=1 << 29, name="star",
     )
     from_prev, from_next = swap(to_prev, to_next)
     right, right_x, right_y, share, to_prev, to_next, sums = call(
         helmholtz_kernel,
-        [mode, share, from_prev, from_next, joins, rims, nodal, inverse, derive, derive_back],
+        [mode, share, to_prev, from_prev, from_next, joins, rims, nodal, inverse, derive, derive_back],
         [one, one, one, one] + rim_out + [((ROWS, LANES), f32)],
         flops=1 << 29, name="helmholtz",
     )
     from_prev, from_next = swap(to_prev, to_next)
     image, image_x, image_y, spread = call(
         image_kernel,
-        [mode, share, from_prev, from_next, joins, nodal, inverse, derive, sums],
+        [mode, share, to_prev, from_prev, from_next, joins, nodal, inverse, derive, sums],
         [one, one, one, ((count, 1, 2 * LANES), f32)],
         flops=1 << 29, name="image",
     )

time: 108 us -> 100 us (0.926)
  local copies, waits for them, and re-layouts: 7.79 us -> 3.18 us
  Pallas kernels: 14 us -> 10.4 us
  waiting for transfers between devices: 10 us -> 11.7 us
    pallas_call x8, Pallas kernels: 14 us -> 10.4 us  [call(): pl.pallas_call(kernel, in_specs=specs, out_specs=[ANY if i in aliases.val...]
    unnamed x19 -> x21, local copies, waits for them, and re-layouts: 6.41 us -> 3.17 us
    all_to_all x1, waiting for transfers between devices: 4.64 us -> 6.35 us  [on_device(): arrived = lax.all_to_all(packed, 'mode', 0, 0)]
  transfers between devices with their start and end apart: 7 -> 7, of which waited for: 5 -> 5; matrix products, arithmetic and copies ran while one was open for 2% -> 0% of each run, Pallas kernels for 1% -> 2%
where the time goes in v2:
time: 100 us; the launch traced here: 99.7 us
  blocking collectives  39.3 us (39%)
  starting transfers between devices  34.2 us (34%)
  waiting for transfers between devices  11.7 us (12%)
  Pallas kernels  10.4 us (10%)
  local copies, waits for them, and re-layouts  3.18 us (3%)
    all_to_all x1, blocking collectives, on_device(): gathered = lax.all_to_all(spread, 'elem', 0, 0)  26.5 us
    ppermute x3, starting transfers between devices, swap(): lax.ppermute(to_prev, 'elem', backward)  22.1 us
    all_to_all x1, blocking collectives, on_device(): returned = lax.all_to_all(spectral, 'mode', 0, 0)  12.8 us
    pallas_call x8, Pallas kernels, call(): pl.pallas_call(kernel, in_specs=specs, out_specs=[ANY if i in aliases.val...  10.4 us
    ppermute x3, starting transfers between devices, swap(): lax.ppermute(to_next, 'elem', onward)  7.66 us
    all_to_all x1, waiting for transfers between devices, on_device(): arrived = lax.all_to_all(packed, 'mode', 0, 0)  6.35 us
    ppermute x3, waiting for transfers between devices, swap(): lax.ppermute(to_prev, 'elem', backward)  4.66 us
    all_to_all x1, starting transfers between devices, on_device(): arrived = lax.all_to_all(packed, 'mode', 0, 0)  4.43 us
  transfers between devices with their start and end apart: 7, of which 5 were waited for; matrix products, arithmetic and copies ran while one was open for 0% of the time, Pallas kernels for 2%

profile of v2, /device:TPU:8, one launch (start us, length us, event | category | flops | bytes accessed | tf_op | source)
XLA Modules:
  0.0 99.7 jit_solution(14321468575843212359)
XLA Ops:
  0.6 0.0 copy-start
  0.6 1.1 %copy-done = f32[3,64,648]{2,1,0:T(8,128)S(1)} copy-done((f32[3,64,648]{2,1,0:T(8,128)S(1)}, f32[3,64,648]{2,1,0:T(8,128)}, u32[]{:S(2)}) %copy-start) | copy-done | bytes 497688
  1.7 1.2 %pack.1 = f32[8,2,64,128]{3,2,1,0:T(8,128)} custom-call(f32[3,64,648]{2,1,0:T(8,128)S(1)} %copy-done), custom_call_target="tpu_custom_call" | custom-call | bytes 1021952 | tf_op jit(solution)/shard_map/pack/pallas_call | solution.py:502
  2.9 0.0 copy-start.5
  2.9 0.0 copy-start.4
  2.9 4.4 %all-to-all-start = ((f32[8,2,64,128]{3,2,1,0:T(8,128)}), f32[8,2,64,128]{3,2,1,0:T(8,128)S(1)}, u32[]{:S(2)}, u32[]{:S(2)}) async-start(f32[8,2,64,128]{3,2,1,0:T(8,128)} %pack.1), calls=%async_computation | async-start | bytes 1048576 | tf_op jit(solution)/shard_map/all_to_all | solution.py:548
  7.3 0.0 copy-start.7
  7.4 0.0 copy-start.8
  7.4 0.7 copy-done.7
  8.0 0.0 copy-done.8
  8.1 0.0 copy-done.5
  8.1 0.0 copy-done.4
  8.1 0.0 copy-start.6
  8.1 0.0 copy-start.1
  8.2 0.6 copy-done.6
  8.8 0.0 copy-start.2
  8.8 0.3 copy-done.1
  9.2 0.4 copy-done.2
  9.5 1.8 %prepare.1 = (f32[192,1024]{1,0:T(8,128)S(1)}, f32[8,1024]{1,0:T(8,128)S(1)}, f32[8,128]{1,0:T(8,128)S(1)}, bf16[256,1024]{1,0:T(8,128)(2,1)S(1)}, bf16[1024,256...) custom-call(s32[1]{0:T(128)} %bitcast.mode, ...), custom_call_target="tpu_custom_call", output_to_operand_aliasing={{5}: (5, {}), {6}: (6, {})} | custom-call | flops 16777216 | bytes 3696332 | tf_op jit(solution)/shard_map/prepare/pallas_call | solution.py:502
  11.3 6.4 %all-to-all-done.packed = f32[8,2,64,128]{3,2,1,0:T(8,128)S(1)} async-done(((f32[8,2,64,128]{3,2,1,0:T(8,128)}), f32[8,2,64,128]{3,2,1,0:T(8,128)S(1)}, u32[]{:S(2)}, u32[]{:S(2)}) %all-to-all-start) | async-done | bytes 524320 | tf_op jit(solution)/shard_map/all_to_all | solution.py:548
  17.7 1.8 %convect.1 = f32[8,2,64,128]{3,2,1,0:T(8,128)S(1)} custom-call(f32[8,2,64,128]{3,2,1,0:T(8,128)S(1)} %all-to-all-done.packed, f32[8,128]{1,0:T(8,128)S(1)} %get-tuple-element.28.own_metric, bf16[2,2,256,256]{3,2,1,0:T(8,128)(2,1)S(1)} %get-tuple-element.29.fourier, bf16[2,128,256]{2,1,0:T(8,128)(2,1)S(1)} %get-tuple-element.30.derive), custom_call_target="tpu_custom_call" | custom-call | flops 1073741824 | bytes 1708032 | tf_op jit(solution)/shard_map/convect/pallas_call | solution.py:502
  19.5 12.8 %all_to_all.15.spectral = f32[8,2,64,128]{3,2,1,0:T(8,128)S(1)} all-to-all(f32[8,2,64,128]{3,2,1,0:T(8,128)S(1)} %convect.1), channel_id=1, replica_groups=mesh['elem'=64,'mode'=8] {'mode'}, dimensions={0} | all-to-all | bytes 1048576 | tf_op jit(solution)/shard_map/all_to_all | solution.py:557
  32.3 0.7 weigh.1
  32.9 3.8 %collective-permute-start = (f32[200,128]{1,0:T(8,128)S(1)}, f32[200,128]{1,0:T(8,128)S(1)}, u32[]{:S(2)}, u32[]{:S(2)}) collective-permute-start(f32[200,128]{1,0:T(8,128)S(1)} %get-tuple-element.35), channel_id=1, source_target_pairs={{0,8},{8,16},{16,24},{24,32},{32,40},{40,48},{48,56},{56,64},{64,7... | collective-permute-start | bytes 307208 | tf_op jit(solution)/shard_map/ppermute | solution.py:524
  36.8 9.4 %collective-permute-start.1 = (f32[200,128]{1,0:T(8,128)S(1)}, f32[200,128]{1,0:T(8,128)S(1)}, u32[]{:S(2)}, u32[]{:S(2)}) collective-permute-start(f32[200,128]{1,0:T(8,128)S(1)} %get-tuple-element.34.own), channel_id=1, source_target_pairs={{8,0},{16,8},{24,16},{32,24},{40,32},{48,40},{56,48},{64,56},{72,6... | collective-permute-start | bytes 307208 | tf_op jit(solution)/shard_map/ppermute | solution.py:524
  46.2 0.7 collective-permute-done.from_prev
  46.9 1.5 %collective-permute-done.1.from_next = f32[200,128]{1,0:T(8,128)S(1)} collective-permute-done((f32[200,128]{1,0:T(8,128)S(1)}, f32[200,128]{1,0:T(8,128)S(1)}, u32[]{:S(2)}, u32[]{:S(2)}) %collective-permute-start.1) | collective-permute-done | bytes 102432 | tf_op jit(solution)/shard_map/ppermute | solution.py:524
  48.4 0.0 copy-start.3
  48.4 1.3 %star.1 = (f32[192,1024]{1,0:T(8,128)S(1)}, f32[1,1024]{1,0:T(1,128)S(1)}, f32[64,1024]{1,0:T(8,128)S(1)}, f32[64,128]{1,0:T(8,128)S(1)}, f32[64,128]{1,0:T(8,128)S(1)}) custom-call(s32[1]{0:T(128)} %bitcast.mode, f32[200,1024]{1,0:T(8,128)S(1)} %get-tuple-element.33.share, f32[200,128]{1,0:T(8,128)S(1)} %get-tuple-element.34.own, ...), custom_call_target="tpu_custom_call" | custom-call | flops 536870912 | bytes 4243460 | tf_op jit(solution)/shard_map/star/pallas_call | solution.py:502
  49.7 1.9 %collective-permute-start.2 = (f32[64,128]{1,0:T(8,128)S(1)}, f32[64,128]{1,0:T(8,128)S(1)}, u32[]{:S(2)}, u32[]{:S(2)}) collective-permute-start(f32[64,128]{1,0:T(8,128)S(1)} %get-tuple-element.40), channel_id=1, source_target_pairs={{0,8},{8,16},{16,24},{24,32},{32,40},{40,48},{48,56},{56,64},{64,7... | collective-permute-start | bytes 98312 | tf_op jit(solution)/shard_map/ppermute | solution.py:524
  51.7 6.4 %collective-permute-start.3 = (f32[64,128]{1,0:T(8,128)S(1)}, f32[64,128]{1,0:T(8,128)S(1)}, u32[]{:S(2)}, u32[]{:S(2)}) collective-permute-start(f32[64,128]{1,0:T(8,128)S(1)} %get-tuple-element.39.own), channel_id=1, source_target_pairs={{8,0},{16,8},{24,16},{32,24},{40,32},{48,40},{56,48},{64,56},{72,6... | collective-permute-start | bytes 98312 | tf_op jit(solution)/shard_map/ppermute | solution.py:524
  58.1 0.0 collective-permute-done.2.from_prev
  58.1 1.6 %collective-permute-done.3.from_next = f32[64,128]{1,0:T(8,128)S(1)} collective-permute-done((f32[64,128]{1,0:T(8,128)S(1)}, f32[64,128]{1,0:T(8,128)S(1)}, u32[]{:S(2)}, u32[]{:S(2)}) %collective-permute-start.3) | collective-permute-done | bytes 32800 | tf_op jit(solution)/shard_map/ppermute | solution.py:524
  59.7 0.0 copy-done.3
  59.7 1.3 %helmholtz.1 = (f32[64,1024]{1,0:T(8,128)S(1)}, f32[64,1024]{1,0:T(8,128)S(1)}, f32[64,1024]{1,0:T(8,128)S(1)}, f32[64,1024]{1,0:T(8,128)S(1)}, f32[64,128]{1,0:...) custom-call(s32[1]{0:T(128)} %bitcast.mode, f32[64,1024]{1,0:T(8,128)S(1)} %get-tuple-element.38.share, ...), custom_call_target="tpu_custom_call" | custom-call | flops 536870912 | bytes 2854916 | tf_op jit(solution)/shard_map/helmholtz/pallas_call | solution.py:502
  61.0 1.9 %collective-permute-start.4 = (f32[64,128]{1,0:T(8,128)S(1)}, f32[64,128]{1,0:T(8,128)S(1)}, u32[]{:S(2)}, u32[]{:S(2)}) collective-permute-start(f32[64,128]{1,0:T(8,128)S(1)} %get-tuple-element.44), channel_id=1, source_target_pairs={{0,8},{8,16},{16,24},{24,32},{32,40},{40,48},{48,56},{56,64},{64,7... | collective-permute-start | bytes 98312 | tf_op jit(solution)/shard_map/ppermute | solution.py:524
  62.9 6.3 %collective-permute-start.5 = (f32[64,128]{1,0:T(8,128)S(1)}, f32[64,128]{1,0:T(8,128)S(1)}, u32[]{:S(2)}, u32[]{:S(2)}) collective-permute-start(f32[64,128]{1,0:T(8,128)S(1)} %get-tuple-element.43.own), channel_id=1, source_target_pairs={{8,0},{16,8},{24,16},{32,24},{40,32},{48,40},{56,48},{64,56},{72,6... | collective-permute-start | bytes 98312 | tf_op jit(solution)/shard_map/ppermute | solution.py:524
  69.3 0.0 collective-permute-done.4.from_prev
  69.3 1.6 %collective-permute-done.5.from_next = f32[64,128]{1,0:T(8,128)S(1)} collective-permute-done((f32[64,128]{1,0:T(8,128)S(1)}, f32[64,128]{1,0:T(8,128)S(1)}, u32[]{:S(2)}, u32[]{:S(2)}) %collective-permute-start.5) | collective-permute-done | bytes 32800 | tf_op jit(solution)/shard_map/ppermute | solution.py:524
  70.9 0.8 image.1
  71.7 26.5 %all_to_all.16 = f32[64,1,256]{2,1,0:T(1,128)S(1)} all-to-all(f32[64,1,256]{2,1,0:T(1,128)S(1)} %get-tuple-element.46), channel_id=1, replica_groups=mesh['elem'=64,'mode'=8] {'elem'}, dimensions={0} | all-to-all | bytes 131072 | tf_op jit(solution)/shard_map/all_to_all | solution.py:586
  98.2 1.5 %finish.1 = (f32[3,64,648]{2,1,0:T(8,128)}, f32[64,648]{1,0:T(8,128)}) custom-call(s32[1]{0:T(128)} %bitcast.mode, f32[64,256]{1,0:T(8,128)S(1)} %bitcast.5, f32[192,1024]{1,0:T(8,128)S(1)} %get-tuple-element.47.star, f32[64,1024]{1,0:T(8,128)S(1)} %get-tuple-element.48.right, f32[64,1024]{1,0:T(8,128)S(1)} %get-tuple-element.49.right_x, ...), custom_call_target="tpu_custom_call" | custom-call | bytes 3088388 | tf_op jit(solution)/shard_map/finish/pallas_call | solution.py:502
  (6 shorter events, 0.1 us)
Async XLA Ops:
  0.6 1.1 %copy-start = (f32[3,64,648]{2,1,0:T(8,128)S(1)}, f32[3,64,648]{2,1,0:T(8,128)}, u32[]{:S(2)}) copy-start(f32[3,64,648]{2,1,0:T(8,128)} %velocity.3) | copy-start | bytes 1492996
  2.9 5.1 %copy-start.5 = (bf16[2,128,256]{2,1,0:T(8,128)(2,1)S(1)}, bf16[2,128,256]{2,1,0:T(8,128)(2,1)}, u32[]{:S(2)}) copy-start(bf16[2,128,256]{2,1,0:T(8,128)(2,1)} %constant.10.clone) | copy-start | bytes 393220
  2.9 5.2 %copy-start.4 = (bf16[2,2,256,256]{3,2,1,0:T(8,128)(2,1)S(1)}, bf16[2,2,256,256]{3,2,1,0:T(8,128)(2,1)}, u32[]{:S(2)}) copy-start(bf16[2,2,256,256]{3,2,1,0:T(8,128)(2,1)} %constant.12.clone) | copy-start | bytes 1572868
  2.9 14.8 %all-to-all-start = ((f32[8,2,64,128]{3,2,1,0:T(8,128)}), f32[8,2,64,128]{3,2,1,0:T(8,128)S(1)}, u32[]{:S(2)}, u32[]{:S(2)}) async-start(f32[8,2,64,128]{3,2,1,0:T(8,128)} %pack.1), calls=%async_computation | async-start | bytes 1048576 | tf_op jit(solution)/shard_map/all_to_all | solution.py:548
  7.3 0.7 copy-start.7
  7.4 0.7 copy-start.8
  8.1 0.7 copy-start.6
  8.1 1.1 %copy-start.1 = (f32[3,64,648]{2,1,0:T(8,128)S(1)}, f32[3,64,648]{2,1,0:T(8,128)}, u32[]{:S(2)}) copy-start(f32[3,64,648]{2,1,0:T(8,128)} %velocity.3) | copy-start | bytes 1492996
  8.8 0.7 copy-start.2
  32.9 13.9 %collective-permute-start = (f32[200,128]{1,0:T(8,128)S(1)}, f32[200,128]{1,0:T(8,128)S(1)}, u32[]{:S(2)}, u32[]{:S(2)}) collective-permute-start(f32[200,128]{1,0:T(8,128)S(1)} %get-tuple-element.35), channel_id=1, source_target_pairs={{0,8},{8,16},{16,24},{24,32},{32,40},{40,48},{48,56},{56,64},{64,7... | collective-permute-start | bytes 307208 | tf_op jit(solution)/shard_map/ppermute | solution.py:524
  36.8 11.6 %collective-permute-start.1 = (f32[200,128]{1,0:T(8,128)S(1)}, f32[200,128]{1,0:T(8,128)S(1)}, u32[]{:S(2)}, u32[]{:S(2)}) collective-permute-start(f32[200,128]{1,0:T(8,128)S(1)} %get-tuple-element.34.own), channel_id=1, source_target_pairs={{8,0},{16,8},{24,16},{32,24},{40,32},{48,40},{56,48},{64,56},{72,6... | collective-permute-start | bytes 307208 | tf_op jit(solution)/shard_map/ppermute | solution.py:524
  48.4 11.3 %copy-start.3 = (bf16[2,256,128]{2,1,0:T(8,128)(2,1)S(1)}, bf16[2,256,128]{2,1,0:T(8,128)(2,1)}, u32[]{:S(2)}) copy-start(bf16[2,256,128]{2,1,0:T(8,128)(2,1)} %constant.11.clone.derive_back) | copy-start | bytes 393220
  49.7 8.4 %collective-permute-start.2 = (f32[64,128]{1,0:T(8,128)S(1)}, f32[64,128]{1,0:T(8,128)S(1)}, u32[]{:S(2)}, u32[]{:S(2)}) collective-permute-start(f32[64,128]{1,0:T(8,128)S(1)} %get-tuple-element.40), channel_id=1, source_target_pairs={{0,8},{8,16},{16,24},{24,32},{32,40},{40,48},{48,56},{56,64},{64,7... | collective-permute-start | bytes 98312 | tf_op jit(solution)/shard_map/ppermute | solution.py:524
  51.7 8.0 %collective-permute-start.3 = (f32[64,128]{1,0:T(8,128)S(1)}, f32[64,128]{1,0:T(8,128)S(1)}, u32[]{:S(2)}, u32[]{:S(2)}) collective-permute-start(f32[64,128]{1,0:T(8,128)S(1)} %get-tuple-element.39.own), channel_id=1, source_target_pairs={{8,0},{16,8},{24,16},{32,24},{40,32},{48,40},{56,48},{64,56},{72,6... | collective-permute-start | bytes 98312 | tf_op jit(solution)/shard_map/ppermute | solution.py:524
  61.0 8.3 %collective-permute-start.4 = (f32[64,128]{1,0:T(8,128)S(1)}, f32[64,128]{1,0:T(8,128)S(1)}, u32[]{:S(2)}, u32[]{:S(2)}) collective-permute-start(f32[64,128]{1,0:T(8,128)S(1)} %get-tuple-element.44), channel_id=1, source_target_pairs={{0,8},{8,16},{16,24},{24,32},{32,40},{40,48},{48,56},{56,64},{64,7... | collective-permute-start | bytes 98312 | tf_op jit(solution)/shard_map/ppermute | solution.py:524
  62.9 7.9 %collective-permute-start.5 = (f32[64,128]{1,0:T(8,128)S(1)}, f32[64,128]{1,0:T(8,128)S(1)}, u32[]{:S(2)}, u32[]{:S(2)}) collective-permute-start(f32[64,128]{1,0:T(8,128)S(1)} %get-tuple-element.43.own), channel_id=1, source_target_pairs={{8,0},{16,8},{24,16},{32,24},{40,32},{48,40},{56,48},{64,56},{72,6... | collective-permute-start | bytes 98312 | tf_op jit(solution)/shard_map/ppermute | solution.py:524

commit v3 on v2

--- a/solution.py
+++ b/solution.py
@@ -59,7 +59,17 @@
 def halves(table):
     high = table.astype(np.float32).astype(jnp.bfloat16)
     low = (table - high.astype(np.float64)).astype(np.float32).astype(jnp.bfloat16)
-    return np.stack([high, low])
+    return high, low
+
+
+def as_right(table):
+    high, low = halves(table)
+    return np.concatenate([high, high, low], axis=0)
+
+
+def as_left(table):
+    high, low = halves(table)
+    return np.concatenate([high, high, low], axis=1)
 
 
 def derivative_tables():
@@ -68,13 +78,13 @@
     table[:QUAD_NODES, :QUAD_NODES] = np.kron(matrix, np.eye(SIDE)).T
     table[:QUAD_NODES, LANES : LANES + QUAD_NODES] = np.kron(np.eye(SIDE), matrix).T
     table = table.astype(np.float32).astype(np.float64)
-    return halves(table), halves(table.T.copy())
+    return as_right(table), as_right(table.T.copy())
 
 
 def fourier_tables():
     index = np.arange(HALF)
     angles = 2.0 * math.pi / PLANES * (index[:, None] * index[None, :] % PLANES)
-    return np.stack([halves(np.cos(angles)), halves(np.sin(angles))])
+    return np.stack([as_left(np.cos(angles)), as_left(np.sin(angles))])
 
 
 def split2(x):
@@ -94,17 +104,13 @@
 
 
 def times_table(x, table):
-    rows = x.shape[0]
     high, low = split2(x)
-    both = mm(jnp.concatenate([high, low], axis=0), table[0])
-    return both[:rows] + both[rows:] + mm(high, table[1])
+    return mm(jnp.concatenate([high, low, high], axis=1), table)
 
 
 def table_times(table, x):
     high, low = split2(x)
-    cols = x.shape[1]
-    both = mm(table[0], jnp.concatenate([high, low], axis=1))
-    return both[:, :cols] + both[:, cols:] + mm(table[1], high)
+    return mm(table, jnp.concatenate([high, low, high], axis=0))
 
 
 def times_incidence(x, incidence):
@@ -166,7 +172,7 @@
 
 
 def prepare_kernel(
-    mode, velocity, nodal, ids, edges, fourier, derive,
+    mode, parity, velocity, nodal, ids, edges, fourier, derive,
     field, nodal_wide, own_metric, joins, rims, fourier_on, derive_on,
 ):
     lane = lax.broadcasted_iota(jnp.int32, (1, LANES), 1)
@@ -195,9 +201,14 @@
         for q in range(QUADS)
     ]
     ids_wide = jnp.concatenate(ids_row, axis=1)
+    odd = parity[0] > 0
     edge_row = [
         jnp.concatenate(
-            [edges[s : s + 1, :], jnp.full((1, LANES - EDGE), -2, jnp.int32)], axis=1
+            [
+                jnp.where(odd, edges[1 - s : 2 - s, :], edges[s : s + 1, :]),
+                jnp.full((1, LANES - EDGE), -2, jnp.int32),
+            ],
+            axis=1,
         ).astype(f32)
         for s in range(2)
     ]
@@ -256,12 +267,10 @@
 
 
 def convect_kernel(packed, own_metric, fourier, derive, out, even, odd, sums, differences):
-    cosine = (fourier[0, 0], fourier[0, 1])
-    sine = (fourier[1, 0], fourier[1, 1])
     metric = own_metric[...]
     lane = lax.broadcasted_iota(jnp.int32, (1, LANES), 1)
     inside = lane < QUAD_NODES
-    table = (derive[0], derive[1])
+    table = derive[...]
     index = lax.broadcasted_iota(jnp.int32, (HALF, 1), 0)
     rate = (8.0 / PLANES) * index.astype(f32)
     sign = jnp.where(index % 2 == 0, 1.0, -1.0)
@@ -281,11 +290,11 @@
     highest = sines[0:1]
     to_even = jnp.concatenate([cosines, rate * sines], axis=1)
     to_odd = jnp.concatenate([sines, -rate * cosines], axis=1)
-    even[...] = table_times(cosine, to_even)
+    even[...] = table_times(fourier[0], to_even)
     even[:, :PACK] = even[:, :PACK] + sign * highest
     middle = jnp.sum(sign * to_even, axis=0, keepdims=True)
     middle = middle + jnp.concatenate([highest, jnp.zeros_like(highest)], axis=1)
-    odd[...] = table_times(sine, to_odd)
+    odd[...] = table_times(fourier[1], to_odd)
     opening = lax.broadcasted_iota(jnp.int32, (CHUNK, 1), 0) == 0
     product_middle = None
     for i in range(HALF // CHUNK):
@@ -324,10 +333,9 @@
         sums[rows, :] = ahead + mirror
     index = index[:KEPT]
     weight = jnp.where(index <= PLANES // 3, 2.0 / PLANES, 0.0)
-    kept = [(fourier[t, 0, :KEPT], fourier[t, 1, :KEPT]) for t in range(2)]
-    result = table_times(kept[0], sums[...]) + sign[:KEPT] * product_middle
+    result = table_times(fourier[0, :KEPT], sums[...]) + sign[:KEPT] * product_middle
     results = [jnp.where(index == 0, 0.5 * weight, weight) * result]
-    result = table_times(kept[1], differences[...])
+    result = table_times(fourier[1, :KEPT], differences[...])
     results.append(jnp.where(index == 0, 0.0, weight) * result)
     half = ROWS // 2
     for m in range(KEPT // half):
@@ -339,7 +347,7 @@
     out[KEPT // half :] = jnp.zeros((QUADS - KEPT // half, 2, ROWS, LANES), f32)
 
 
-def weigh_kernel(spectral, nodal, rims, share, to_prev, to_next):
+def weigh_kernel(spectral, nodal, rims, share, first_out, second_out):
     for q in range(QUADS):
         here = slice(LANES * q, LANES * (q + 1))
         mass = nodal[4:5, here]
@@ -352,38 +360,38 @@
     share[3 * ROWS + 1 : 3 * ROWS + 2, :] = nodal[5:6, :]
     share[3 * ROWS + 2 :, :] = jnp.zeros((STACK - 3 * ROWS - 2, WIDE), f32)
     rim = times_incidence(share[...], rims[...])
-    to_prev[...] = rim[:, :LANES]
-    to_next[...] = rim[:, LANES:]
-
-
-def joined(share, own, from_prev, from_next, joins, single):
+    first_out[...] = rim[:, :LANES]
+    second_out[...] = rim[:, LANES:]
+
+
+def joined(share, own, first_in, second_in, joins, single):
     lane = lax.broadcasted_iota(jnp.int32, (1, LANES), 1)
-    near = jnp.where(lane < EDGE, from_prev[...], own[...])
-    sums = jnp.concatenate([near, from_next[...]], axis=1)
+    near = jnp.where(lane < EDGE, first_in[...], own[...])
+    sums = jnp.concatenate([near, second_in[...]], axis=1)
     return share[...] * single + times_incidence(sums, joins[...])
 
 
 def star_kernel(
-    mode, share, own, from_prev, from_next, joins, rims, field, nodal, derive,
-    star, inverse, share_out, to_prev, to_next,
+    mode, share, own, first_in, second_in, joins, rims, field, nodal, derive,
+    star, inverse, share_out, first_out, second_out,
 ):
     metric = nodal[...]
-    total = joined(share, own, from_prev, from_next, joins, metric[6:7])
+    total = joined(share, own, first_in, second_in, joins, metric[6:7])
     inside = metric[5:6] > 0.0
     scale = TIME_STEP / jnp.where(inside, total[3 * ROWS : 3 * ROWS + 1], 1.0)
     inverse[...] = jnp.where(
         inside, 1.0 / jnp.where(inside, total[3 * ROWS + 1 : 3 * ROWS + 2], 1.0), 0.0
     )
     star[...] = field[...] + scale * total[: 3 * ROWS]
-    table = (derive[0], derive[1])
+    table = derive[...]
     star_x = gradient(star[0:ROWS], metric, table)[0]
     star_y = gradient(star[ROWS : 2 * ROWS], metric, table)[1]
     divergence = star_x + star_y + along_z(star[2 * ROWS :], mode[0])
     result = (-1.0 / TIME_STEP) * (metric[4:5] * divergence)
     share_out[...] = result
     rim = times_incidence(result, rims[...])
-    to_prev[...] = rim[:, :LANES]
-    to_next[...] = rim[:, LANES:]
+    first_out[...] = rim[:, :LANES]
+    second_out[...] = rim[:, LANES:]
 
 
 def lane_sum(x):
@@ -394,15 +402,15 @@
 
 
 def helmholtz_kernel(
-    mode, share, own, from_prev, from_next, joins, rims, nodal, inverse, derive, derive_back,
-    right, right_x, right_y, share_out, to_prev, to_next, sums,
+    mode, share, own, first_in, second_in, joins, rims, nodal, inverse, derive, derive_back,
+    right, right_x, right_y, share_out, first_out, second_out, sums,
 ):
     metric = nodal[...]
-    total = joined(share, own, from_prev, from_next, joins, metric[6:7])
+    total = joined(share, own, first_in, second_in, joins, metric[6:7])
     mass = metric[4:5]
     rate, even = rates(mode[0])
     shift = rate * rate + PENALTY
-    grad_x, grad_y = gradient(total, metric, (derive[0], derive[1]))
+    grad_x, grad_y = gradient(total, metric, derive[...])
     right[...] = total
     right_x[...] = grad_x
     right_y[...] = grad_y
@@ -412,11 +420,11 @@
     part_r = metric[0:1] * flux_x + metric[1:2] * flux_y
     part_s = metric[2:3] * flux_x + metric[3:4] * flux_y
     both = jnp.concatenate([stacked(part_r), stacked(part_s)], axis=1)
-    result = unstacked(times_table(both, (derive_back[0], derive_back[1]))) + weighted
+    result = unstacked(times_table(both, derive_back[...])) + weighted
     share_out[...] = result
     rim = times_incidence(result, rims[...])
-    to_prev[...] = rim[:, :LANES]
-    to_next[...] = rim[:, LANES:]
+    first_out[...] = rim[:, :LANES]
+    second_out[...] = rim[:, LANES:]
     square = lane_sum(total * total * inverse[...])
     energy = lane_sum(flux_x * grad_x + flux_y * grad_y + weighted * total)
     column = lax.broadcasted_iota(jnp.int32, (ROWS, LANES), 1)
@@ -424,15 +432,15 @@
 
 
 def image_kernel(
-    mode, share, own, from_prev, from_next, joins, nodal, inverse, derive, sums,
+    mode, share, own, first_in, second_in, joins, nodal, inverse, derive, sums,
     image, image_x, image_y, spread,
 ):
     metric = nodal[...]
-    total = joined(share, own, from_prev, from_next, joins, metric[6:7])
+    total = joined(share, own, first_in, second_in, joins, metric[6:7])
     mass = metric[4:5]
     rate, even = rates(mode[0])
     shift = rate * rate + PENALTY
-    grad_x, grad_y = gradient(total, metric, (derive[0], derive[1]))
+    grad_x, grad_y = gradient(total, metric, derive[...])
     image[...] = total
     image_x[...] = grad_x
     image_y[...] = grad_y
@@ -516,12 +524,13 @@
     derive, derive_back = (jnp.asarray(t) for t in derivative_tables())
     fourier = jnp.asarray(fourier_tables())
     mode = lax.axis_index("mode").astype(jnp.int32).reshape(1)
+    parity = (lax.axis_index("elem") % 2).astype(jnp.int32).reshape(1)
     count = lax.axis_size("elem")
-    onward = [(i, (i + 1) % count) for i in range(count)]
-    backward = [(target, source) for source, target in onward]
-
-    def swap(to_prev, to_next):
-        return lax.ppermute(to_next, "elem", onward), lax.ppermute(to_prev, "elem", backward)
+    pairs = [[(i, (i + 1) % count) for i in range(start, count, 2)] for start in (1, 0)]
+    pairs = [some + [(target, source) for source, target in some] for some in pairs]
+
+    def swap(first, second):
+        return lax.ppermute(first, "elem", pairs[0]), lax.ppermute(second, "elem", pairs[1])
 
     block = (QUADS, 2, ROWS, LANES)
     (packed,) = call(
@@ -532,7 +541,7 @@
     tables = [fourier, derive]
     field, nodal, own_metric, joins, rims, fourier, derive = call(
         prepare_kernel,
-        [mode, velocity, nodal, local_ids[None], edge_ids[0]] + tables,
+        [mode, parity, velocity, nodal, local_ids[None], edge_ids[0]] + tables,
         [
             ((3 * ROWS, WIDE), f32),
             ((8, WIDE), f32),
@@ -543,7 +552,7 @@
         + [(t.shape, bf16) for t in tables],
         flops=1 << 24,
         name="prepare",
-        aliases={5: 5, 6: 6},
+        aliases={6: 5, 7: 6},
     )
     arrived = lax.all_to_all(packed, "mode", 0, 0)
     (spectral,) = call(
@@ -556,30 +565,30 @@
     )
     returned = lax.all_to_all(spectral, "mode", 0, 0)
     rim_out = [((STACK, LANES), f32)] * 2
-    share, to_prev, to_next = call(
+    share, first_out, second_out = call(
         weigh_kernel, [returned, nodal, rims], [((STACK, WIDE), f32)] + rim_out,
         flops=1 << 28, name="weigh",
     )
-    from_prev, from_next = swap(to_prev, to_next)
+    first_in, second_in = swap(first_out, second_out)
     one = ((ROWS, WIDE), f32)
     rim_out = [((ROWS, LANES), f32)] * 2
-    star, inverse, share, to_prev, to_next = call(
+    star, inverse, share, first_out, second_out = call(
         star_kernel,
-        [mode, share, to_prev, from_prev, from_next, joins, rims, field, nodal, derive],
+        [mode, share, first_out, first_in, second_in, joins, rims, field, nodal, derive],
         [((3 * ROWS, WIDE), f32), ((1, WIDE), f32), one] + rim_out,
         flops=1 << 29, name="star",
     )
-    from_prev, from_next = swap(to_prev, to_next)
-    right, right_x, right_y, share, to_prev, to_next, sums = call(
+    first_in, second_in = swap(first_out, second_out)
+    right, right_x, right_y, share, first_out, second_out, sums = call(
         helmholtz_kernel,
-        [mode, share, to_prev, from_prev, from_next, joins, rims, nodal, inverse, derive, derive_back],
+        [mode, share, first_out, first_in, second_in, joins, rims, nodal, inverse, derive, derive_back],
         [one, one, one, one] + rim_out + [((ROWS, LANES), f32)],
         flops=1 << 29, name="helmholtz",
     )
-    from_prev, from_next = swap(to_prev, to_next)
+    first_in, second_in = swap(first_out, second_out)
     image, image_x, image_y, spread = call(
         image_kernel,
-        [mode, share, to_prev, from_prev, from_next, joins, nodal, inverse, derive, sums],
+        [mode, share, first_out, first_in, second_in, joins, nodal, inverse, derive, sums],
         [one, one, one, ((count, 1, 2 * LANES), f32)],
         flops=1 << 29, name="image",
     )

time: 100 us -> 98 us (0.980)
  waiting for transfers between devices: 11.7 us -> 17.1 us
  starting transfers between devices: 34.2 us -> 29.4 us
  blocking collectives: 39.3 us -> 35.4 us
  local copies, waits for them, and re-layouts: 3.18 us -> 4.82 us
    ppermute x6, waiting for transfers between devices: 5.37 us -> 12.4 us  [the longest x3 7.68 us: swap(): lax.ppermute(second, 'elem', pairs[1])]
    ppermute x6, starting transfers between devices: 29.8 us -> 25 us  [the longest x3 19.2 us: swap(): lax.ppermute(first, 'elem', pairs[0])]
    all_to_all x1, blocking collectives: 26.5 us -> 22.6 us  [on_device(): gathered = lax.all_to_all(spread, 'elem', 0, 0)]
    all_to_all x1, waiting for transfers between devices: 6.35 us -> 4.71 us  [on_device(): arrived = lax.all_to_all(packed, 'mode', 0, 0)]
    unnamed x21 -> x25, local copies, waits for them, and re-layouts: 3.17 us -> 4.81 us
  transfers between devices with their start and end apart: 7 -> 7, of which waited for: 5 -> 6; matrix products, arithmetic and copies ran while one was open for 0% -> 0% of each run, Pallas kernels for 2% -> 2%
where the time goes in v3:
time: 98 us; the launch traced here: 97.4 us
  blocking collectives  35.4 us (36%)
  starting transfers between devices  29.4 us (30%)
  waiting for transfers between devices  17.1 us (17%)
  Pallas kernels  9.86 us (10%)
  local copies, waits for them, and re-layouts  4.82 us (5%)
    all_to_all x1, blocking collectives, on_device(): gathered = lax.all_to_all(spread, 'elem', 0, 0)  22.6 us
    ppermute x3, starting transfers between devices, swap(): lax.ppermute(first, 'elem', pairs[0])  19.2 us
    all_to_all x1, blocking collectives, on_device(): returned = lax.all_to_all(spectral, 'mode', 0, 0)  12.8 us
    pallas_call x8, Pallas kernels, call(): pl.pallas_call(kernel, in_specs=specs, out_specs=[ANY if i in aliases.val...  9.86 us
    ppermute x3, waiting for transfers between devices, swap(): lax.ppermute(second, 'elem', pairs[1])  7.68 us
    ppermute x3, starting transfers between devices, swap(): lax.ppermute(second, 'elem', pairs[1])  5.76 us
    unnamed x25, local copies, waits for them, and re-layouts  4.81 us
    all_to_all x1, waiting for transfers between devices, on_device(): arrived = lax.all_to_all(packed, 'mode', 0, 0)  4.71 us
  transfers between devices with their start and end apart: 7, of which 6 were waited for; matrix products, arithmetic and copies ran while one was open for 0% of the time, Pallas kernels for 2%

profile of v3, /device:TPU:8, one launch (start us, length us, event | category | flops | bytes accessed | tf_op | source)
XLA Modules:
  0.0 97.4 jit_solution(6840758774520254171)
XLA Ops:
  0.6 0.0 copy-start
  0.6 1.1 %copy-done = f32[3,64,648]{2,1,0:T(8,128)S(1)} copy-done((f32[3,64,648]{2,1,0:T(8,128)S(1)}, f32[3,64,648]{2,1,0:T(8,128)}, u32[]{:S(2)}) %copy-start) | copy-done | bytes 497688
  1.7 1.2 %pack.1 = f32[8,2,64,128]{3,2,1,0:T(8,128)} custom-call(f32[3,64,648]{2,1,0:T(8,128)S(1)} %copy-done), custom_call_target="tpu_custom_call" | custom-call | bytes 1021952 | tf_op jit(solution)/shard_map/pack/pallas_call | solution.py:510
  2.9 0.0 copy-start.6
  2.9 4.4 %all-to-all-start = ((f32[8,2,64,128]{3,2,1,0:T(8,128)}), f32[8,2,64,128]{3,2,1,0:T(8,128)S(1)}, u32[]{:S(2)}, u32[]{:S(2)}) async-start(f32[8,2,64,128]{3,2,1,0:T(8,128)} %pack.1), calls=%async_computation | async-start | bytes 1048576 | tf_op jit(solution)/shard_map/all_to_all | solution.py:557
  7.3 0.0 copy-done.6
  7.3 0.0 copy-start.7
  7.4 0.0 copy-start.1
  7.4 0.1 copy.21.fourier
  7.4 0.8 copy-done.7
  8.3 0.0 copy-start.9
  8.3 0.0 copy-start.10
  8.3 0.7 copy-done.9
  9.0 0.0 copy-start.8
  9.0 0.0 copy-done.10
  9.0 0.7 copy-done.8
  9.7 0.0 copy-start.4
  9.7 0.0 copy-done.1
  9.7 0.7 copy-done.4
  10.4 1.8 %prepare.1 = (f32[192,1024]{1,0:T(8,128)S(1)}, f32[8,1024]{1,0:T(8,128)S(1)}, f32[8,128]{1,0:T(8,128)S(1)}, bf16[256,1024]{1,0:T(8,128)(2,1)S(1)}, bf16[1024,256...) custom-call(s32[1]{0:T(128)} %bitcast.mode, ...), custom_call_target="tpu_custom_call", output_to_operand_aliasing={{5}: (6, {}), {6}: (7, {})} | custom-call | flops 16777216 | bytes 4351696 | tf_op jit(solution)/shard_map/prepare/pallas_call | solution.py:510
  12.2 0.0 copy-start.2
  12.2 0.8 copy-done.2
  13.0 4.7 %all-to-all-done.packed = f32[8,2,64,128]{3,2,1,0:T(8,128)S(1)} async-done(((f32[8,2,64,128]{3,2,1,0:T(8,128)}), f32[8,2,64,128]{3,2,1,0:T(8,128)S(1)}, u32[]{:S(2)}, u32[]{:S(2)}) %all-to-all-start) | async-done | bytes 524320 | tf_op jit(solution)/shard_map/all_to_all | solution.py:557
  17.7 1.7 %convect.1 = f32[8,2,64,128]{3,2,1,0:T(8,128)S(1)} custom-call(f32[8,2,64,128]{3,2,1,0:T(8,128)S(1)} %all-to-all-done.packed, f32[8,128]{1,0:T(8,128)S(1)} %get-tuple-element.28.own_metric, bf16[2,256,768]{2,1,0:T(8,128)(2,1)S(1)} %get-tuple-element.29.fourier, bf16[384,256]{1,0:T(8,128)(2,1)S(1)} %get-tuple-element.30.derive), custom_call_target="tpu_custom_call" | custom-call | flops 1073741824 | bytes 2035712 | tf_op jit(solution)/shard_map/convect/pallas_call | solution.py:510
  19.4 12.8 %all_to_all.15.spectral = f32[8,2,64,128]{3,2,1,0:T(8,128)S(1)} all-to-all(f32[8,2,64,128]{3,2,1,0:T(8,128)S(1)} %convect.1), channel_id=1, replica_groups=mesh['elem'=64,'mode'=8] {'mode'}, dimensions={0} | all-to-all | bytes 1048576 | tf_op jit(solution)/shard_map/all_to_all | solution.py:566
  32.2 0.0 copy-start.3
  32.2 0.7 weigh.1
  32.9 11.3 %collective-permute-start = (f32[200,128]{1,0:T(8,128)S(1)}, f32[200,128]{1,0:T(8,128)S(1)}, u32[]{:S(2)}, u32[]{:S(2)}) collective-permute-start(f32[200,128]{1,0:T(8,128)S(1)} %get-tuple-element.34.own), channel_id=1, source_target_pairs={{8,16},{24,32},{40,48},{56,64},{72,80},{88,96},{104,112},{120,128}... | collective-permute-start | bytes 307208 | tf_op jit(solution)/shard_map/ppermute | solution.py:533
  44.2 1.9 %collective-permute-start.1 = (f32[200,128]{1,0:T(8,128)S(1)}, f32[200,128]{1,0:T(8,128)S(1)}, u32[]{:S(2)}, u32[]{:S(2)}) collective-permute-start(f32[200,128]{1,0:T(8,128)S(1)} %get-tuple-element.35), channel_id=1, source_target_pairs={{0,8},{16,24},{32,40},{48,56},{64,72},{80,88},{96,104},{112,120},{... | collective-permute-start | bytes 307208 | tf_op jit(solution)/shard_map/ppermute | solution.py:533
  46.1 0.7 collective-permute-done.first_in
  46.8 3.9 %collective-permute-done.1.second_in = f32[200,128]{1,0:T(8,128)S(1)} collective-permute-done((f32[200,128]{1,0:T(8,128)S(1)}, f32[200,128]{1,0:T(8,128)S(1)}, u32[]{:S(2)}, u32[]{:S(2)}) %collective-permute-start.1) | collective-permute-done | bytes 102432 | tf_op jit(solution)/shard_map/ppermute | solution.py:533
  50.7 0.0 copy-done.3
  50.7 0.0 copy-start.5
  50.7 1.2 %star.1 = (f32[192,1024]{1,0:T(8,128)S(1)}, f32[1,1024]{1,0:T(1,128)S(1)}, f32[64,1024]{1,0:T(8,128)S(1)}, f32[64,128]{1,0:T(8,128)S(1)}, f32[64,128]{1,0:T(8,128)S(1)}) custom-call(s32[1]{0:T(128)} %bitcast.mode, f32[200,1024]{1,0:T(8,128)S(1)} %get-tuple-element.33.share, f32[200,128]{1,0:T(8,128)S(1)} %get-tuple-element.34.own, ...), custom_call_target="tpu_custom_call" | custom-call | flops 536870912 | bytes 4308996 | tf_op jit(solution)/shard_map/star/pallas_call | solution.py:510
  51.9 2.1 %collective-permute-start.2 = (f32[64,128]{1,0:T(8,128)S(1)}, f32[64,128]{1,0:T(8,128)S(1)}, u32[]{:S(2)}, u32[]{:S(2)}) collective-permute-start(f32[64,128]{1,0:T(8,128)S(1)} %get-tuple-element.39.own), channel_id=1, source_target_pairs={{8,16},{24,32},{40,48},{56,64},{72,80},{88,96},{104,112},{120,128}... | collective-permute-start | bytes 98312 | tf_op jit(solution)/shard_map/ppermute | solution.py:533
  54.1 1.9 %collective-permute-start.3 = (f32[64,128]{1,0:T(8,128)S(1)}, f32[64,128]{1,0:T(8,128)S(1)}, u32[]{:S(2)}, u32[]{:S(2)}) collective-permute-start(f32[64,128]{1,0:T(8,128)S(1)} %get-tuple-element.40), channel_id=1, source_target_pairs={{0,8},{16,24},{32,40},{48,56},{64,72},{80,88},{96,104},{112,120},{... | collective-permute-start | bytes 98312 | tf_op jit(solution)/shard_map/ppermute | solution.py:533
  56.0 3.9 %collective-permute-done.2.first_in = f32[64,128]{1,0:T(8,128)S(1)} collective-permute-done((f32[64,128]{1,0:T(8,128)S(1)}, f32[64,128]{1,0:T(8,128)S(1)}, u32[]{:S(2)}, u32[]{:S(2)}) %collective-permute-start.2) | collective-permute-done | bytes 32800 | tf_op jit(solution)/shard_map/ppermute | solution.py:533
  59.9 0.0 collective-permute-done.3.second_in
  59.9 0.0 copy-done.5
  59.9 1.1 %helmholtz.1 = (f32[64,1024]{1,0:T(8,128)S(1)}, f32[64,1024]{1,0:T(8,128)S(1)}, f32[64,1024]{1,0:T(8,128)S(1)}, f32[64,1024]{1,0:T(8,128)S(1)}, f32[64,128]{1,0:...) custom-call(s32[1]{0:T(128)} %bitcast.mode, f32[64,1024]{1,0:T(8,128)S(1)} %get-tuple-element.38.share, ...), custom_call_target="tpu_custom_call" | custom-call | flops 536870912 | bytes 2985988 | tf_op jit(solution)/shard_map/helmholtz/pallas_call | solution.py:510
  61.0 5.8 %collective-permute-start.4 = (f32[64,128]{1,0:T(8,128)S(1)}, f32[64,128]{1,0:T(8,128)S(1)}, u32[]{:S(2)}, u32[]{:S(2)}) collective-permute-start(f32[64,128]{1,0:T(8,128)S(1)} %get-tuple-element.43.own), channel_id=1, source_target_pairs={{8,16},{24,32},{40,48},{56,64},{72,80},{88,96},{104,112},{120,128}... | collective-permute-start | bytes 98312 | tf_op jit(solution)/shard_map/ppermute | solution.py:533
  66.8 1.9 %collective-permute-start.5 = (f32[64,128]{1,0:T(8,128)S(1)}, f32[64,128]{1,0:T(8,128)S(1)}, u32[]{:S(2)}, u32[]{:S(2)}) collective-permute-start(f32[64,128]{1,0:T(8,128)S(1)} %get-tuple-element.44), channel_id=1, source_target_pairs={{0,8},{16,24},{32,40},{48,56},{64,72},{80,88},{96,104},{112,120},{... | collective-permute-start | bytes 98312 | tf_op jit(solution)/shard_map/ppermute | solution.py:533
  68.8 0.1 collective-permute-done.4.first_in
  68.9 3.7 %collective-permute-done.5.second_in = f32[64,128]{1,0:T(8,128)S(1)} collective-permute-done((f32[64,128]{1,0:T(8,128)S(1)}, f32[64,128]{1,0:T(8,128)S(1)}, u32[]{:S(2)}, u32[]{:S(2)}) %collective-permute-start.5) | collective-permute-done | bytes 32800 | tf_op jit(solution)/shard_map/ppermute | solution.py:533
  72.7 0.7 image.1
  73.4 22.6 %all_to_all.16 = f32[64,1,256]{2,1,0:T(1,128)S(1)} all-to-all(f32[64,1,256]{2,1,0:T(1,128)S(1)} %get-tuple-element.46), channel_id=1, replica_groups=mesh['elem'=64,'mode'=8] {'elem'}, dimensions={0} | all-to-all | bytes 131072 | tf_op jit(solution)/shard_map/all_to_all | solution.py:595
  96.0 1.5 %finish.1 = (f32[3,64,648]{2,1,0:T(8,128)}, f32[64,648]{1,0:T(8,128)}) custom-call(s32[1]{0:T(128)} %bitcast.mode, f32[64,256]{1,0:T(8,128)S(1)} %bitcast.6, f32[192,1024]{1,0:T(8,128)S(1)} %get-tuple-element.47.star, f32[64,1024]{1,0:T(8,128)S(1)} %get-tuple-element.48.right, f32[64,1024]{1,0:T(8,128)S(1)} %get-tuple-element.49.right_x, ...), custom_call_target="tpu_custom_call" | custom-call | bytes 3088388 | tf_op jit(solution)/shard_map/finish/pallas_call | solution.py:510
  (5 shorter events, 0.0 us)
Async XLA Ops:
  0.6 1.1 %copy-start = (f32[3,64,648]{2,1,0:T(8,128)S(1)}, f32[3,64,648]{2,1,0:T(8,128)}, u32[]{:S(2)}) copy-start(f32[3,64,648]{2,1,0:T(8,128)} %velocity.3) | copy-start | bytes 1492996
  2.9 4.4 %copy-start.6 = (bf16[2,256,768]{2,1,0:T(8,128)(2,1)S(1)}, bf16[2,256,768]{2,1,0:T(8,128)(2,1)}, u32[]{:S(2)}) copy-start(bf16[2,256,768]{2,1,0:T(8,128)(2,1)} %constant.30.clone) | copy-start | bytes 2359300
  2.9 14.8 %all-to-all-start = ((f32[8,2,64,128]{3,2,1,0:T(8,128)}), f32[8,2,64,128]{3,2,1,0:T(8,128)S(1)}, u32[]{:S(2)}, u32[]{:S(2)}) async-start(f32[8,2,64,128]{3,2,1,0:T(8,128)} %pack.1), calls=%async_computation | async-start | bytes 1048576 | tf_op jit(solution)/shard_map/all_to_all | solution.py:557
  7.3 0.9 copy-start.7
  7.4 2.3 %copy-start.1 = (f32[3,64,648]{2,1,0:T(8,128)S(1)}, f32[3,64,648]{2,1,0:T(8,128)}, u32[]{:S(2)}) copy-start(f32[3,64,648]{2,1,0:T(8,128)} %velocity.3) | copy-start | bytes 1492996
  8.3 0.7 copy-start.9
  8.3 0.7 copy-start.10
  9.0 0.7 copy-start.8
  9.7 0.7 copy-start.4
  12.2 0.8 copy-start.2
  32.2 18.5 %copy-start.3 = (bf16[256,1024]{1,0:T(8,128)(2,1)S(1)}, bf16[256,1024]{1,0:T(8,128)(2,1)}, u32[]{:S(2)}) copy-start(bf16[256,1024]{1,0:T(8,128)(2,1)} %copy-done.2) | copy-start | bytes 1572868
  32.9 13.9 %collective-permute-start = (f32[200,128]{1,0:T(8,128)S(1)}, f32[200,128]{1,0:T(8,128)S(1)}, u32[]{:S(2)}, u32[]{:S(2)}) collective-permute-start(f32[200,128]{1,0:T(8,128)S(1)} %get-tuple-element.34.own), channel_id=1, source_target_pairs={{8,16},{24,32},{40,48},{56,64},{72,80},{88,96},{104,112},{120,128}... | collective-permute-start | bytes 307208 | tf_op jit(solution)/shard_map/ppermute | solution.py:533
  44.2 6.6 %collective-permute-start.1 = (f32[200,128]{1,0:T(8,128)S(1)}, f32[200,128]{1,0:T(8,128)S(1)}, u32[]{:S(2)}, u32[]{:S(2)}) collective-permute-start(f32[200,128]{1,0:T(8,128)S(1)} %get-tuple-element.35), channel_id=1, source_target_pairs={{0,8},{16,24},{32,40},{48,56},{64,72},{80,88},{96,104},{112,120},{... | collective-permute-start | bytes 307208 | tf_op jit(solution)/shard_map/ppermute | solution.py:533
  50.7 9.2 %copy-start.5 = (bf16[768,128]{1,0:T(8,128)(2,1)S(1)}, bf16[768,128]{1,0:T(8,128)(2,1)}, u32[]{:S(2)}) copy-start(bf16[768,128]{1,0:T(8,128)(2,1)} %constant.29.clone.derive_back) | copy-start | bytes 589828
  51.9 7.9 %collective-permute-start.2 = (f32[64,128]{1,0:T(8,128)S(1)}, f32[64,128]{1,0:T(8,128)S(1)}, u32[]{:S(2)}, u32[]{:S(2)}) collective-permute-start(f32[64,128]{1,0:T(8,128)S(1)} %get-tuple-element.39.own), channel_id=1, source_target_pairs={{8,16},{24,32},{40,48},{56,64},{72,80},{88,96},{104,112},{120,128}... | collective-permute-start | bytes 98312 | tf_op jit(solution)/shard_map/ppermute | solution.py:533
  54.1 5.8 %collective-permute-start.3 = (f32[64,128]{1,0:T(8,128)S(1)}, f32[64,128]{1,0:T(8,128)S(1)}, u32[]{:S(2)}, u32[]{:S(2)}) collective-permute-start(f32[64,128]{1,0:T(8,128)S(1)} %get-tuple-element.40), channel_id=1, source_target_pairs={{0,8},{16,24},{32,40},{48,56},{64,72},{80,88},{96,104},{112,120},{... | collective-permute-start | bytes 98312 | tf_op jit(solution)/shard_map/ppermute | solution.py:533
  61.0 7.9 %collective-permute-start.4 = (f32[64,128]{1,0:T(8,128)S(1)}, f32[64,128]{1,0:T(8,128)S(1)}, u32[]{:S(2)}, u32[]{:S(2)}) collective-permute-start(f32[64,128]{1,0:T(8,128)S(1)} %get-tuple-element.43.own), channel_id=1, source_target_pairs={{8,16},{24,32},{40,48},{56,64},{72,80},{88,96},{104,112},{120,128}... | collective-permute-start | bytes 98312 | tf_op jit(solution)/shard_map/ppermute | solution.py:533
  66.8 5.8 %collective-permute-start.5 = (f32[64,128]{1,0:T(8,128)S(1)}, f32[64,128]{1,0:T(8,128)S(1)}, u32[]{:S(2)}, u32[]{:S(2)}) collective-permute-start(f32[64,128]{1,0:T(8,128)S(1)} %get-tuple-element.44), channel_id=1, source_target_pairs={{0,8},{16,24},{32,40},{48,56},{64,72},{80,88},{96,104},{112,120},{... | collective-permute-start | bytes 98312 | tf_op jit(solution)/shard_map/ppermute | solution.py:533

commit v4 on v3

--- a/solution.py
+++ b/solution.py
@@ -364,19 +364,20 @@
     second_out[...] = rim[:, LANES:]
 
 
-def joined(share, own, first_in, second_in, joins, single):
+def joined(parity, share, own, first_in, second_in, joins, single):
     lane = lax.broadcasted_iota(jnp.int32, (1, LANES), 1)
     near = jnp.where(lane < EDGE, first_in[...], own[...])
-    sums = jnp.concatenate([near, second_in[...]], axis=1)
+    other = jnp.where(parity[0] > 0, second_in[0], second_in[1])
+    sums = jnp.concatenate([near, other], axis=1)
     return share[...] * single + times_incidence(sums, joins[...])
 
 
 def star_kernel(
-    mode, share, own, first_in, second_in, joins, rims, field, nodal, derive,
+    mode, parity, share, own, first_in, second_in, joins, rims, field, nodal, derive,
     star, inverse, share_out, first_out, second_out,
 ):
     metric = nodal[...]
-    total = joined(share, own, first_in, second_in, joins, metric[6:7])
+    total = joined(parity, share, own, first_in, second_in, joins, metric[6:7])
     inside = metric[5:6] > 0.0
     scale = TIME_STEP / jnp.where(inside, total[3 * ROWS : 3 * ROWS + 1], 1.0)
     inverse[...] = jnp.where(
@@ -402,11 +403,11 @@
 
 
 def helmholtz_kernel(
-    mode, share, own, first_in, second_in, joins, rims, nodal, inverse, derive, derive_back,
+    mode, parity, share, own, first_in, second_in, joins, rims, nodal, inverse, derive, derive_back,
     right, right_x, right_y, share_out, first_out, second_out, sums,
 ):
     metric = nodal[...]
-    total = joined(share, own, first_in, second_in, joins, metric[6:7])
+    total = joined(parity, share, own, first_in, second_in, joins, metric[6:7])
     mass = metric[4:5]
     rate, even = rates(mode[0])
     shift = rate * rate + PENALTY
@@ -432,11 +433,11 @@
 
 
 def image_kernel(
-    mode, share, own, first_in, second_in, joins, nodal, inverse, derive, sums,
+    mode, parity, share, own, first_in, second_in, joins, nodal, inverse, derive, sums,
     image, image_x, image_y, spread,
 ):
     metric = nodal[...]
-    total = joined(share, own, first_in, second_in, joins, metric[6:7])
+    total = joined(parity, share, own, first_in, second_in, joins, metric[6:7])
     mass = metric[4:5]
     rate, even = rates(mode[0])
     shift = rate * rate + PENALTY
@@ -526,11 +527,15 @@
     mode = lax.axis_index("mode").astype(jnp.int32).reshape(1)
     parity = (lax.axis_index("elem") % 2).astype(jnp.int32).reshape(1)
     count = lax.axis_size("elem")
-    pairs = [[(i, (i + 1) % count) for i in range(start, count, 2)] for start in (1, 0)]
-    pairs = [some + [(target, source) for source, target in some] for some in pairs]
+    across = [(i, (i + 1) % count) for i in range(1, count, 2)]
+    across = across + [(target, source) for source, target in across]
+    beside = [[i, i + 1] for i in range(0, count, 2)]
 
     def swap(first, second):
-        return lax.ppermute(first, "elem", pairs[0]), lax.ppermute(second, "elem", pairs[1])
+        return (
+            lax.ppermute(first, "elem", across),
+            lax.all_gather(second, "elem", axis_index_groups=beside),
+        )
 
     block = (QUADS, 2, ROWS, LANES)
     (packed,) = call(
@@ -574,21 +579,21 @@
     rim_out = [((ROWS, LANES), f32)] * 2
     star, inverse, share, first_out, second_out = call(
         star_kernel,
-        [mode, share, first_out, first_in, second_in, joins, rims, field, nodal, derive],
+        [mode, parity, share, first_out, first_in, second_in, joins, rims, field, nodal, derive],
         [((3 * ROWS, WIDE), f32), ((1, WIDE), f32), one] + rim_out,
         flops=1 << 29, name="star",
     )
     first_in, second_in = swap(first_out, second_out)
     right, right_x, right_y, share, first_out, second_out, sums = call(
         helmholtz_kernel,
-        [mode, share, first_out, first_in, second_in, joins, rims, nodal, inverse, derive, derive_back],
+        [mode, parity, share, first_out, first_in, second_in, joins, rims, nodal, inverse, derive, derive_back],
         [one, one, one, one] + rim_out + [((ROWS, LANES), f32)],
         flops=1 << 29, name="helmholtz",
     )
     first_in, second_in = swap(first_out, second_out)
     image, image_x, image_y, spread = call(
         image_kernel,
-        [mode, share, first_out, first_in, second_in, joins, nodal, inverse, derive, sums],
+        [mode, parity, share, first_out, first_in, second_in, joins, nodal, inverse, derive, sums],
         [one, one, one, ((count, 1, 2 * LANES), f32)],
         flops=1 << 29, name="image",
     )

time: 98 us -> 94.3 us (0.962)
  blocking collectives: 35.4 us -> 49.9 us
  waiting for transfers between devices: 17.1 us -> 5.58 us
  starting transfers between devices: 29.4 us -> 23.7 us
    all_gather x0 -> x3, blocking collectives: none -> 14.5 us  [swap(): lax.all_gather(second, 'elem', axis_index_groups=beside)]
    ppermute x6 -> x3, waiting for transfers between devices: 12.4 us -> 0.02 us  [swap(): lax.ppermute(first, 'elem', across)]
    ppermute x6 -> x3, starting transfers between devices: 25 us -> 19.2 us  [swap(): lax.ppermute(first, 'elem', across)]
  transfers between devices with their start and end apart: 7 -> 4, of which waited for: 6 -> 1; matrix products, arithmetic and copies ran while one was open for 0% -> 0% of each run, Pallas kernels for 2% -> 2%
where the time goes in v4:
time: 94.3 us; the launch traced here: 93.8 us
  blocking collectives  49.9 us (53%)
  starting transfers between devices  23.7 us (25%)
  Pallas kernels  9.86 us (10%)
  waiting for transfers between devices  5.58 us (6%)
  local copies, waits for them, and re-layouts  3.97 us (4%)
    all_to_all x1, blocking collectives, on_device(): gathered = lax.all_to_all(spread, 'elem', 0, 0)  22.6 us
    ppermute x3, starting transfers between devices, swap(): lax.ppermute(first, 'elem', across)  19.2 us
    all_gather x3, blocking collectives, swap(): lax.all_gather(second, 'elem', axis_index_groups=beside)  14.5 us
    all_to_all x1, blocking collectives, on_device(): returned = lax.all_to_all(spectral, 'mode', 0, 0)  12.8 us
    pallas_call x8, Pallas kernels, call(): pl.pallas_call(kernel, in_specs=specs, out_specs=[ANY if i in aliases.val...  9.86 us
    all_to_all x1, waiting for transfers between devices, on_device(): arrived = lax.all_to_all(packed, 'mode', 0, 0)  5.56 us
    all_to_all x1, starting transfers between devices, on_device(): arrived = lax.all_to_all(packed, 'mode', 0, 0)  4.43 us
    unnamed x25, local copies, waits for them, and re-layouts  3.96 us
  transfers between devices with their start and end apart: 4, of which 1 were waited for; matrix products, arithmetic and copies ran while one was open for 0% of the time, Pallas kernels for 2%

profile of v4, /device:TPU:8, one launch (start us, length us, event | category | flops | bytes accessed | tf_op | source)
XLA Modules:
  0.0 93.8 jit_solution(16639133646297253922)
XLA Ops:
  0.6 0.0 copy-start
  0.6 1.1 %copy-done = f32[3,64,648]{2,1,0:T(8,128)S(1)} copy-done((f32[3,64,648]{2,1,0:T(8,128)S(1)}, f32[3,64,648]{2,1,0:T(8,128)}, u32[]{:S(2)}) %copy-start) | copy-done | bytes 497688
  1.7 1.2 %pack.1 = f32[8,2,64,128]{3,2,1,0:T(8,128)} custom-call(f32[3,64,648]{2,1,0:T(8,128)S(1)} %copy-done), custom_call_target="tpu_custom_call" | custom-call | bytes 1021952 | tf_op jit(solution)/shard_map/pack/pallas_call | solution.py:511
  2.9 0.0 copy-start.7
  2.9 0.0 copy-start.6
  2.9 4.4 %all-to-all-start = ((f32[8,2,64,128]{3,2,1,0:T(8,128)}), f32[8,2,64,128]{3,2,1,0:T(8,128)S(1)}, u32[]{:S(2)}, u32[]{:S(2)}) async-start(f32[8,2,64,128]{3,2,1,0:T(8,128)} %pack.1), calls=%async_computation | async-start | bytes 1048576 | tf_op jit(solution)/shard_map/all_to_all | solution.py:562
  7.3 0.0 copy-start.9
  7.4 0.0 copy-start.10
  7.4 0.7 copy-done.9
  8.0 0.0 copy-done.10
  8.1 0.0 copy-done.7
  8.1 0.0 copy-done.6
  8.1 0.0 copy-start.8
  8.1 0.0 copy-start.1
  8.1 0.1 copy.21.fourier
  8.2 0.6 copy-done.8
  8.8 0.0 copy-start.4
  8.8 0.3 copy-done.1
  9.2 0.4 copy-done.4
  9.5 1.8 %prepare.1 = (f32[192,1024]{1,0:T(8,128)S(1)}, f32[8,1024]{1,0:T(8,128)S(1)}, f32[8,128]{1,0:T(8,128)S(1)}, bf16[256,1024]{1,0:T(8,128)(2,1)S(1)}, bf16[1024,256...) custom-call(s32[1]{0:T(128)} %bitcast.mode, ...), custom_call_target="tpu_custom_call", output_to_operand_aliasing={{5}: (6, {}), {6}: (7, {})} | custom-call | flops 16777216 | bytes 4351696 | tf_op jit(solution)/shard_map/prepare/pallas_call | solution.py:511
  11.3 0.0 copy-start.2
  11.4 0.8 copy-done.2
  12.1 5.6 %all-to-all-done.packed = f32[8,2,64,128]{3,2,1,0:T(8,128)S(1)} async-done(((f32[8,2,64,128]{3,2,1,0:T(8,128)}), f32[8,2,64,128]{3,2,1,0:T(8,128)S(1)}, u32[]{:S(2)}, u32[]{:S(2)}) %all-to-all-start) | async-done | bytes 524320 | tf_op jit(solution)/shard_map/all_to_all | solution.py:562
  17.7 1.7 %convect.1 = f32[8,2,64,128]{3,2,1,0:T(8,128)S(1)} custom-call(f32[8,2,64,128]{3,2,1,0:T(8,128)S(1)} %all-to-all-done.packed, f32[8,128]{1,0:T(8,128)S(1)} %get-tuple-element.28.own_metric, bf16[2,256,768]{2,1,0:T(8,128)(2,1)S(1)} %get-tuple-element.29.fourier, bf16[384,256]{1,0:T(8,128)(2,1)S(1)} %get-tuple-element.30.derive), custom_call_target="tpu_custom_call" | custom-call | flops 1073741824 | bytes 2035712 | tf_op jit(solution)/shard_map/convect/pallas_call | solution.py:511
  19.4 12.8 %all_to_all.15.spectral = f32[8,2,64,128]{3,2,1,0:T(8,128)S(1)} all-to-all(f32[8,2,64,128]{3,2,1,0:T(8,128)S(1)} %convect.1), channel_id=1, replica_groups=mesh['elem'=64,'mode'=8] {'mode'}, dimensions={0} | all-to-all | bytes 1048576 | tf_op jit(solution)/shard_map/all_to_all | solution.py:571
  32.2 0.0 copy-start.3
  32.2 0.7 weigh.1
  32.9 11.3 %collective-permute-start = (f32[200,128]{1,0:T(8,128)S(1)}, f32[200,128]{1,0:T(8,128)S(1)}, u32[]{:S(2)}, u32[]{:S(2)}) collective-permute-start(f32[200,128]{1,0:T(8,128)S(1)} %get-tuple-element.34.own), channel_id=1, source_target_pairs={{8,16},{24,32},{40,48},{56,64},{72,80},{88,96},{104,112},{120,128}... | collective-permute-start | bytes 307208 | tf_op jit(solution)/shard_map/ppermute | solution.py:536
  44.2 5.3 %all-gather = f32[400,128]{1,0:T(8,128)S(1)} all-gather(f32[200,128]{1,0:T(8,128)S(1)} %get-tuple-element.35), channel_id=2, replica_groups={{0,8},{16,24},{32,40},{48,56},{64,72},{80,88},{96,104},{112,120},{128,1..., dimensions={0}, use_global_device_ids=true | all-gather | bytes 307200 | tf_op jit(solution)/shard_map/all_gather | solution.py:537
  49.5 0.0 collective-permute-done.first_in
  49.5 0.0 copy-done.3
  49.5 0.0 copy-start.5
  49.5 1.2 %star.1 = (f32[192,1024]{1,0:T(8,128)S(1)}, f32[1,1024]{1,0:T(1,128)S(1)}, f32[64,1024]{1,0:T(8,128)S(1)}, f32[64,128]{1,0:T(8,128)S(1)}, f32[64,128]{1,0:T(8,128)S(1)}) custom-call(s32[1]{0:T(128)} %bitcast.mode, s32[1]{0:T(128)} %bitcast.1.parity, f32[200,1024]{1,0:T(8,128)S(1)} %get-tuple-element.33.share, f32[200,128]{1,0:T(8,128)S(1)} %get-tuple-element.34.own, ...), custom_call_target="tpu_custom_call" | custom-call | flops 536870912 | bytes 4411400 | tf_op jit(solution)/shard_map/star/pallas_call | solution.py:511
  50.7 3.3 %collective-permute-start.1 = (f32[64,128]{1,0:T(8,128)S(1)}, f32[64,128]{1,0:T(8,128)S(1)}, u32[]{:S(2)}, u32[]{:S(2)}) collective-permute-start(f32[64,128]{1,0:T(8,128)S(1)} %get-tuple-element.39.own), channel_id=1, source_target_pairs={{8,16},{24,32},{40,48},{56,64},{72,80},{88,96},{104,112},{120,128}... | collective-permute-start | bytes 98312 | tf_op jit(solution)/shard_map/ppermute | solution.py:536
  54.0 4.6 %all-gather.1 = f32[128,128]{1,0:T(8,128)S(1)} all-gather(f32[64,128]{1,0:T(8,128)S(1)} %get-tuple-element.40), channel_id=3, replica_groups={{0,8},{16,24},{32,40},{48,56},{64,72},{80,88},{96,104},{112,120},{128,1..., dimensions={0}, use_global_device_ids=true | all-gather | bytes 98304 | tf_op jit(solution)/shard_map/all_gather | solution.py:537
  58.6 0.0 collective-permute-done.1.first_in
  58.6 0.0 copy-done.5
  58.6 1.1 %helmholtz.1 = (f32[64,1024]{1,0:T(8,128)S(1)}, f32[64,1024]{1,0:T(8,128)S(1)}, f32[64,1024]{1,0:T(8,128)S(1)}, f32[64,1024]{1,0:T(8,128)S(1)}, f32[64,128]{1,0:...) custom-call(s32[1]{0:T(128)} %bitcast.mode, s32[1]{0:T(128)} %bitcast.1.parity, ...), custom_call_target="tpu_custom_call" | custom-call | flops 536870912 | bytes 3018760 | tf_op jit(solution)/shard_map/helmholtz/pallas_call | solution.py:511
  59.8 4.6 %collective-permute-start.2 = (f32[64,128]{1,0:T(8,128)S(1)}, f32[64,128]{1,0:T(8,128)S(1)}, u32[]{:S(2)}, u32[]{:S(2)}) collective-permute-start(f32[64,128]{1,0:T(8,128)S(1)} %get-tuple-element.43.own), channel_id=1, source_target_pairs={{8,16},{24,32},{40,48},{56,64},{72,80},{88,96},{104,112},{120,128}... | collective-permute-start | bytes 98312 | tf_op jit(solution)/shard_map/ppermute | solution.py:536
  64.4 4.6 %all-gather.2 = f32[128,128]{1,0:T(8,128)S(1)} all-gather(f32[64,128]{1,0:T(8,128)S(1)} %get-tuple-element.44), channel_id=4, replica_groups={{0,8},{16,24},{32,40},{48,56},{64,72},{80,88},{96,104},{112,120},{128,1..., dimensions={0}, use_global_device_ids=true | all-gather | bytes 98304 | tf_op jit(solution)/shard_map/all_gather | solution.py:537
  69.0 0.0 collective-permute-done.2.first_in
  69.0 0.7 image.1
  69.7 22.6 %all_to_all.16 = f32[64,1,256]{2,1,0:T(1,128)S(1)} all-to-all(f32[64,1,256]{2,1,0:T(1,128)S(1)} %get-tuple-element.46), channel_id=1, replica_groups=mesh['elem'=64,'mode'=8] {'elem'}, dimensions={0} | all-to-all | bytes 131072 | tf_op jit(solution)/shard_map/all_to_all | solution.py:600
  92.3 1.5 %finish.1 = (f32[3,64,648]{2,1,0:T(8,128)}, f32[64,648]{1,0:T(8,128)}) custom-call(s32[1]{0:T(128)} %bitcast.mode, f32[64,256]{1,0:T(8,128)S(1)} %bitcast.10, f32[192,1024]{1,0:T(8,128)S(1)} %get-tuple-element.47.star, f32[64,1024]{1,0:T(8,128)S(1)} %get-tuple-element.48.right, f32[64,1024]{1,0:T(8,128)S(1)} %get-tuple-element.49.right_x, ...), custom_call_target="tpu_custom_call" | custom-call | bytes 3088388 | tf_op jit(solution)/shard_map/finish/pallas_call | solution.py:511
  (5 shorter events, 0.0 us)
Async XLA Ops:
  0.6 1.1 %copy-start = (f32[3,64,648]{2,1,0:T(8,128)S(1)}, f32[3,64,648]{2,1,0:T(8,128)}, u32[]{:S(2)}) copy-start(f32[3,64,648]{2,1,0:T(8,128)} %velocity.3) | copy-start | bytes 1492996
  2.9 5.1 %copy-start.7 = (bf16[384,256]{1,0:T(8,128)(2,1)S(1)}, bf16[384,256]{1,0:T(8,128)(2,1)}, u32[]{:S(2)}) copy-start(bf16[384,256]{1,0:T(8,128)(2,1)} %constant.28.clone) | copy-start | bytes 589828
  2.9 5.2 %copy-start.6 = (bf16[2,256,768]{2,1,0:T(8,128)(2,1)S(1)}, bf16[2,256,768]{2,1,0:T(8,128)(2,1)}, u32[]{:S(2)}) copy-start(bf16[2,256,768]{2,1,0:T(8,128)(2,1)} %constant.30.clone) | copy-start | bytes 2359300
  2.9 14.8 %all-to-all-start = ((f32[8,2,64,128]{3,2,1,0:T(8,128)}), f32[8,2,64,128]{3,2,1,0:T(8,128)S(1)}, u32[]{:S(2)}, u32[]{:S(2)}) async-start(f32[8,2,64,128]{3,2,1,0:T(8,128)} %pack.1), calls=%async_computation | async-start | bytes 1048576 | tf_op jit(solution)/shard_map/all_to_all | solution.py:562
  7.3 0.7 copy-start.9
  7.4 0.7 copy-start.10
  8.1 0.7 copy-start.8
  8.1 1.1 %copy-start.1 = (f32[3,64,648]{2,1,0:T(8,128)S(1)}, f32[3,64,648]{2,1,0:T(8,128)}, u32[]{:S(2)}) copy-start(f32[3,64,648]{2,1,0:T(8,128)} %velocity.3) | copy-start | bytes 1492996
  8.8 0.7 copy-start.4
  11.3 0.8 copy-start.2
  32.2 17.3 %copy-start.3 = (bf16[256,1024]{1,0:T(8,128)(2,1)S(1)}, bf16[256,1024]{1,0:T(8,128)(2,1)}, u32[]{:S(2)}) copy-start(bf16[256,1024]{1,0:T(8,128)(2,1)} %copy-done.2) | copy-start | bytes 1572868
  32.9 16.6 %collective-permute-start = (f32[200,128]{1,0:T(8,128)S(1)}, f32[200,128]{1,0:T(8,128)S(1)}, u32[]{:S(2)}, u32[]{:S(2)}) collective-permute-start(f32[200,128]{1,0:T(8,128)S(1)} %get-tuple-element.34.own), channel_id=1, source_target_pairs={{8,16},{24,32},{40,48},{56,64},{72,80},{88,96},{104,112},{120,128}... | collective-permute-start | bytes 307208 | tf_op jit(solution)/shard_map/ppermute | solution.py:536
  49.5 9.1 %copy-start.5 = (bf16[768,128]{1,0:T(8,128)(2,1)S(1)}, bf16[768,128]{1,0:T(8,128)(2,1)}, u32[]{:S(2)}) copy-start(bf16[768,128]{1,0:T(8,128)(2,1)} %constant.29.clone.derive_back) | copy-start | bytes 589828
  50.7 7.9 %collective-permute-start.1 = (f32[64,128]{1,0:T(8,128)S(1)}, f32[64,128]{1,0:T(8,128)S(1)}, u32[]{:S(2)}, u32[]{:S(2)}) collective-permute-start(f32[64,128]{1,0:T(8,128)S(1)} %get-tuple-element.39.own), channel_id=1, source_target_pairs={{8,16},{24,32},{40,48},{56,64},{72,80},{88,96},{104,112},{120,128}... | collective-permute-start | bytes 98312 | tf_op jit(solution)/shard_map/ppermute | solution.py:536
  59.8 9.2 %collective-permute-start.2 = (f32[64,128]{1,0:T(8,128)S(1)}, f32[64,128]{1,0:T(8,128)S(1)}, u32[]{:S(2)}, u32[]{:S(2)}) collective-permute-start(f32[64,128]{1,0:T(8,128)S(1)} %get-tuple-element.43.own), channel_id=1, source_target_pairs={{8,16},{24,32},{40,48},{56,64},{72,80},{88,96},{104,112},{120,128}... | collective-permute-start | bytes 98312 | tf_op jit(solution)/shard_map/ppermute | solution.py:536

commit v5 on v4

--- a/solution.py
+++ b/solution.py
@@ -92,13 +92,6 @@
     return high, (x - high.astype(f32)).astype(bf16)
 
 
-def split3(x):
-    high = x.astype(bf16)
-    rest = x - high.astype(f32)
-    middle = rest.astype(bf16)
-    return high, middle, (rest - middle.astype(f32)).astype(bf16)
-
-
 def mm(a, b):
     return jnp.dot(a, b, preferred_element_type=f32)
 
@@ -115,8 +108,8 @@
 
 def times_incidence(x, incidence):
     rows = x.shape[0]
-    out = mm(jnp.concatenate(split3(x), axis=0), incidence)
-    return out[:rows] + (out[rows : 2 * rows] + out[2 * rows :])
+    out = mm(jnp.concatenate(split2(x), axis=0), incidence)
+    return out[:rows] + out[rows:]
 
 
 def stacked(x):
@@ -148,10 +141,29 @@
     return rate * jnp.where(even, pltpu.roll(x, ROWS - 1, 0), -pltpu.roll(x, 1, 0))
 
 
+def lanes_at():
+    return lax.broadcasted_iota(jnp.int32, (1, LANES), 1)
+
+
 def unpacked(x, field):
-    if field:
-        x = pltpu.roll(x, PACK - QUAD_NODES * field, 1)
-    return x[:, :LANES]
+    first, second = x[:, :LANES], x[:, LANES:]
+    if field == 0:
+        return first
+    if field == 1:
+        both = jnp.where(lanes_at() < QUAD_NODES, second, first)
+        return pltpu.roll(both, LANES - QUAD_NODES, 1)
+    return pltpu.roll(second, 2 * (LANES - QUAD_NODES), 1)
+
+
+def repacked(fields):
+    lane = lanes_at()
+    second_at = 2 * QUAD_NODES - LANES
+    middle = pltpu.roll(fields[1], QUAD_NODES, 1)
+    last = jnp.where(lane < second_at + QUAD_NODES, pltpu.roll(fields[2], second_at, 1), 0.0)
+    return jnp.concatenate(
+        [jnp.where(lane < QUAD_NODES, fields[0], middle), jnp.where(lane < second_at, middle, last)],
+        axis=1,
+    )
 
 
 def pack_kernel(velocity, packed):
@@ -268,8 +280,6 @@
 
 def convect_kernel(packed, own_metric, fourier, derive, out, even, odd, sums, differences):
     metric = own_metric[...]
-    lane = lax.broadcasted_iota(jnp.int32, (1, LANES), 1)
-    inside = lane < QUAD_NODES
     table = derive[...]
     index = lax.broadcasted_iota(jnp.int32, (HALF, 1), 0)
     rate = (8.0 / PLANES) * index.astype(f32)
@@ -311,19 +321,15 @@
         derived = times_table(jnp.concatenate(speed, axis=0), table)
         weight_r = speed[0] * metric[0:1] + speed[1] * metric[1:2]
         weight_s = speed[0] * metric[2:3] + speed[1] * metric[3:4]
-        total = None
+        terms = []
         for c in range(3):
             part = derived[2 * CHUNK * c : 2 * CHUNK * (c + 1)]
-            term = (
+            terms.append(
                 weight_r * part[:, :LANES]
                 + weight_s * part[:, LANES:]
                 + speed[2] * unpacked(slope, c)
             )
-            term = jnp.where(inside, -term, 0.0)
-            term = jnp.concatenate([term, jnp.zeros((2 * CHUNK, PACK - LANES), f32)], axis=1)
-            if c:
-                term = pltpu.roll(term, QUAD_NODES * c, 1)
-            total = term if total is None else total + term
+        total = repacked(terms)
         ahead = total[:CHUNK]
         mirror = total[CHUNK:]
         differences[rows, :] = ahead - mirror
@@ -332,7 +338,7 @@
             mirror = jnp.where(opening, 0.0, mirror)
         sums[rows, :] = ahead + mirror
     index = index[:KEPT]
-    weight = jnp.where(index <= PLANES // 3, 2.0 / PLANES, 0.0)
+    weight = jnp.where(index <= PLANES // 3, -2.0 / PLANES, 0.0)
     result = table_times(fourier[0, :KEPT], sums[...]) + sign[:KEPT] * product_middle
     results = [jnp.where(index == 0, 0.5 * weight, weight) * result]
     result = table_times(fourier[1, :KEPT], differences[...])

time: 94.3 us -> 93.6 us (level)
  no operation moved by 1% of the time
where the time goes in v5:
time: 93.6 us; the launch traced here: 93.1 us
  blocking collectives  49.9 us (53%)
  starting transfers between devices  23.7 us (25%)
  Pallas kernels  9.14 us (10%)
  waiting for transfers between devices  5.57 us (6%)
  local copies, waits for them, and re-layouts  3.97 us (4%)
    all_to_all x1, blocking collectives, on_device(): gathered = lax.all_to_all(spread, 'elem', 0, 0)  22.6 us
    ppermute x3, starting transfers between devices, swap(): lax.ppermute(first, 'elem', across)  19.2 us
    all_gather x3, blocking collectives, swap(): lax.all_gather(second, 'elem', axis_index_groups=beside)  14.5 us
    all_to_all x1, blocking collectives, on_device(): returned = lax.all_to_all(spectral, 'mode', 0, 0)  12.8 us
    pallas_call x8, Pallas kernels, call(): pl.pallas_call(kernel, in_specs=specs, out_specs=[ANY if i in aliases.val...  9.14 us
    all_to_all x1, waiting for transfers between devices, on_device(): arrived = lax.all_to_all(packed, 'mode', 0, 0)  5.56 us
    all_to_all x1, starting transfers between devices, on_device(): arrived = lax.all_to_all(packed, 'mode', 0, 0)  4.43 us
    unnamed x25, local copies, waits for them, and re-layouts  3.96 us
  transfers between devices with their start and end apart: 4, of which 1 were waited for; matrix products, arithmetic and copies ran while one was open for 0% of the time, Pallas kernels for 2%

profile of v5, /device:TPU:8, one launch (start us, length us, event | category | flops | bytes accessed | tf_op | source)
XLA Modules:
  0.0 93.1 jit_solution(4510619363324732157)
XLA Ops:
  0.6 0.0 copy-start
  0.6 1.1 %copy-done = f32[3,64,648]{2,1,0:T(8,128)S(1)} copy-done((f32[3,64,648]{2,1,0:T(8,128)S(1)}, f32[3,64,648]{2,1,0:T(8,128)}, u32[]{:S(2)}) %copy-start) | copy-done | bytes 497688
  1.7 1.2 %pack.1 = f32[8,2,64,128]{3,2,1,0:T(8,128)} custom-call(f32[3,64,648]{2,1,0:T(8,128)S(1)} %copy-done), custom_call_target="tpu_custom_call" | custom-call | bytes 1021952 | tf_op jit(solution)/shard_map/pack/pallas_call | solution.py:517
  2.9 0.0 copy-start.7
  2.9 0.0 copy-start.6
  2.9 4.4 %all-to-all-start = ((f32[8,2,64,128]{3,2,1,0:T(8,128)}), f32[8,2,64,128]{3,2,1,0:T(8,128)S(1)}, u32[]{:S(2)}, u32[]{:S(2)}) async-start(f32[8,2,64,128]{3,2,1,0:T(8,128)} %pack.1), calls=%async_computation | async-start | bytes 1048576 | tf_op jit(solution)/shard_map/all_to_all | solution.py:568
  7.3 0.0 copy-start.9
  7.4 0.0 copy-start.10
  7.4 0.7 copy-done.9
  8.0 0.0 copy-done.10
  8.1 0.0 copy-done.7
  8.1 0.0 copy-done.6
  8.1 0.0 copy-start.8
  8.1 0.0 copy-start.1
  8.1 0.1 copy.21.fourier
  8.2 0.6 copy-done.8
  8.8 0.0 copy-start.4
  8.8 0.3 copy-done.1
  9.2 0.4 copy-done.4
  9.5 1.8 %prepare.1 = (f32[192,1024]{1,0:T(8,128)S(1)}, f32[8,1024]{1,0:T(8,128)S(1)}, f32[8,128]{1,0:T(8,128)S(1)}, bf16[256,1024]{1,0:T(8,128)(2,1)S(1)}, bf16[1024,256...) custom-call(s32[1]{0:T(128)} %bitcast.mode, ...), custom_call_target="tpu_custom_call", output_to_operand_aliasing={{5}: (6, {}), {6}: (7, {})} | custom-call | flops 16777216 | bytes 4351696 | tf_op jit(solution)/shard_map/prepare/pallas_call | solution.py:517
  11.3 0.0 copy-start.2
  11.4 0.8 copy-done.2
  12.1 5.6 %all-to-all-done.packed = f32[8,2,64,128]{3,2,1,0:T(8,128)S(1)} async-done(((f32[8,2,64,128]{3,2,1,0:T(8,128)}), f32[8,2,64,128]{3,2,1,0:T(8,128)S(1)}, u32[]{:S(2)}, u32[]{:S(2)}) %all-to-all-start) | async-done | bytes 524320 | tf_op jit(solution)/shard_map/all_to_all | solution.py:568
  17.7 1.5 %convect.1 = f32[8,2,64,128]{3,2,1,0:T(8,128)S(1)} custom-call(f32[8,2,64,128]{3,2,1,0:T(8,128)S(1)} %all-to-all-done.packed, f32[8,128]{1,0:T(8,128)S(1)} %get-tuple-element.28.own_metric, bf16[2,256,768]{2,1,0:T(8,128)(2,1)S(1)} %get-tuple-element.29.fourier, bf16[384,256]{1,0:T(8,128)(2,1)S(1)} %get-tuple-element.30.derive), custom_call_target="tpu_custom_call" | custom-call | flops 1073741824 | bytes 2035712 | tf_op jit(solution)/shard_map/convect/pallas_call | solution.py:517
  19.2 12.8 %all_to_all.15.spectral = f32[8,2,64,128]{3,2,1,0:T(8,128)S(1)} all-to-all(f32[8,2,64,128]{3,2,1,0:T(8,128)S(1)} %convect.1), channel_id=1, replica_groups=mesh['elem'=64,'mode'=8] {'mode'}, dimensions={0} | all-to-all | bytes 1048576 | tf_op jit(solution)/shard_map/all_to_all | solution.py:577
  32.0 0.0 copy-start.3
  32.0 0.4 weigh.1
  32.5 11.3 %collective-permute-start = (f32[200,128]{1,0:T(8,128)S(1)}, f32[200,128]{1,0:T(8,128)S(1)}, u32[]{:S(2)}, u32[]{:S(2)}) collective-permute-start(f32[200,128]{1,0:T(8,128)S(1)} %get-tuple-element.34.own), channel_id=1, source_target_pairs={{8,16},{24,32},{40,48},{56,64},{72,80},{88,96},{104,112},{120,128}... | collective-permute-start | bytes 307208 | tf_op jit(solution)/shard_map/ppermute | solution.py:542
  43.8 5.3 %all-gather = f32[400,128]{1,0:T(8,128)S(1)} all-gather(f32[200,128]{1,0:T(8,128)S(1)} %get-tuple-element.35), channel_id=2, replica_groups={{0,8},{16,24},{32,40},{48,56},{64,72},{80,88},{96,104},{112,120},{128,1..., dimensions={0}, use_global_device_ids=true | all-gather | bytes 307200 | tf_op jit(solution)/shard_map/all_gather | solution.py:543
  49.1 0.0 collective-permute-done.first_in
  49.1 0.0 copy-done.3
  49.1 0.0 copy-start.5
  49.1 1.0 %star.1 = (f32[192,1024]{1,0:T(8,128)S(1)}, f32[1,1024]{1,0:T(1,128)S(1)}, f32[64,1024]{1,0:T(8,128)S(1)}, f32[64,128]{1,0:T(8,128)S(1)}, f32[64,128]{1,0:T(8,128)S(1)}) custom-call(s32[1]{0:T(128)} %bitcast.mode, s32[1]{0:T(128)} %bitcast.1.parity, f32[200,1024]{1,0:T(8,128)S(1)} %get-tuple-element.33.share, f32[200,128]{1,0:T(8,128)S(1)} %get-tuple-element.34.own, ...), custom_call_target="tpu_custom_call" | custom-call | flops 536870912 | bytes 4411400 | tf_op jit(solution)/shard_map/star/pallas_call | solution.py:517
  50.1 3.3 %collective-permute-start.1 = (f32[64,128]{1,0:T(8,128)S(1)}, f32[64,128]{1,0:T(8,128)S(1)}, u32[]{:S(2)}, u32[]{:S(2)}) collective-permute-start(f32[64,128]{1,0:T(8,128)S(1)} %get-tuple-element.39.own), channel_id=1, source_target_pairs={{8,16},{24,32},{40,48},{56,64},{72,80},{88,96},{104,112},{120,128}... | collective-permute-start | bytes 98312 | tf_op jit(solution)/shard_map/ppermute | solution.py:542
  53.4 4.6 %all-gather.1 = f32[128,128]{1,0:T(8,128)S(1)} all-gather(f32[64,128]{1,0:T(8,128)S(1)} %get-tuple-element.40), channel_id=3, replica_groups={{0,8},{16,24},{32,40},{48,56},{64,72},{80,88},{96,104},{112,120},{128,1..., dimensions={0}, use_global_device_ids=true | all-gather | bytes 98304 | tf_op jit(solution)/shard_map/all_gather | solution.py:543
  58.0 0.0 collective-permute-done.1.first_in
  58.0 0.0 copy-done.5
  58.0 1.0 %helmholtz.1 = (f32[64,1024]{1,0:T(8,128)S(1)}, f32[64,1024]{1,0:T(8,128)S(1)}, f32[64,1024]{1,0:T(8,128)S(1)}, f32[64,1024]{1,0:T(8,128)S(1)}, f32[64,128]{1,0:...) custom-call(s32[1]{0:T(128)} %bitcast.mode, s32[1]{0:T(128)} %bitcast.1.parity, ...), custom_call_target="tpu_custom_call" | custom-call | flops 536870912 | bytes 3018760 | tf_op jit(solution)/shard_map/helmholtz/pallas_call | solution.py:517
  59.1 4.6 %collective-permute-start.2 = (f32[64,128]{1,0:T(8,128)S(1)}, f32[64,128]{1,0:T(8,128)S(1)}, u32[]{:S(2)}, u32[]{:S(2)}) collective-permute-start(f32[64,128]{1,0:T(8,128)S(1)} %get-tuple-element.43.own), channel_id=1, source_target_pairs={{8,16},{24,32},{40,48},{56,64},{72,80},{88,96},{104,112},{120,128}... | collective-permute-start | bytes 98312 | tf_op jit(solution)/shard_map/ppermute | solution.py:542
  63.7 4.6 %all-gather.2 = f32[128,128]{1,0:T(8,128)S(1)} all-gather(f32[64,128]{1,0:T(8,128)S(1)} %get-tuple-element.44), channel_id=4, replica_groups={{0,8},{16,24},{32,40},{48,56},{64,72},{80,88},{96,104},{112,120},{128,1..., dimensions={0}, use_global_device_ids=true | all-gather | bytes 98304 | tf_op jit(solution)/shard_map/all_gather | solution.py:543
  68.3 0.0 collective-permute-done.2.first_in
  68.3 0.7 image.1
  69.0 22.6 %all_to_all.16 = f32[64,1,256]{2,1,0:T(1,128)S(1)} all-to-all(f32[64,1,256]{2,1,0:T(1,128)S(1)} %get-tuple-element.46), channel_id=1, replica_groups=mesh['elem'=64,'mode'=8] {'elem'}, dimensions={0} | all-to-all | bytes 131072 | tf_op jit(solution)/shard_map/all_to_all | solution.py:606
  91.6 1.5 %finish.1 = (f32[3,64,648]{2,1,0:T(8,128)}, f32[64,648]{1,0:T(8,128)}) custom-call(s32[1]{0:T(128)} %bitcast.mode, f32[64,256]{1,0:T(8,128)S(1)} %bitcast.10, f32[192,1024]{1,0:T(8,128)S(1)} %get-tuple-element.47.star, f32[64,1024]{1,0:T(8,128)S(1)} %get-tuple-element.48.right, f32[64,1024]{1,0:T(8,128)S(1)} %get-tuple-element.49.right_x, ...), custom_call_target="tpu_custom_call" | custom-call | bytes 3088388 | tf_op jit(solution)/shard_map/finish/pallas_call | solution.py:517
  (5 shorter events, 0.0 us)
Async XLA Ops:
  0.6 1.1 %copy-start = (f32[3,64,648]{2,1,0:T(8,128)S(1)}, f32[3,64,648]{2,1,0:T(8,128)}, u32[]{:S(2)}) copy-start(f32[3,64,648]{2,1,0:T(8,128)} %velocity.3) | copy-start | bytes 1492996
  2.9 5.1 %copy-start.7 = (bf16[384,256]{1,0:T(8,128)(2,1)S(1)}, bf16[384,256]{1,0:T(8,128)(2,1)}, u32[]{:S(2)}) copy-start(bf16[384,256]{1,0:T(8,128)(2,1)} %constant.28.clone) | copy-start | bytes 589828
  2.9 5.2 %copy-start.6 = (bf16[2,256,768]{2,1,0:T(8,128)(2,1)S(1)}, bf16[2,256,768]{2,1,0:T(8,128)(2,1)}, u32[]{:S(2)}) copy-start(bf16[2,256,768]{2,1,0:T(8,128)(2,1)} %constant.30.clone) | copy-start | bytes 2359300
  2.9 14.8 %all-to-all-start = ((f32[8,2,64,128]{3,2,1,0:T(8,128)}), f32[8,2,64,128]{3,2,1,0:T(8,128)S(1)}, u32[]{:S(2)}, u32[]{:S(2)}) async-start(f32[8,2,64,128]{3,2,1,0:T(8,128)} %pack.1), calls=%async_computation | async-start | bytes 1048576 | tf_op jit(solution)/shard_map/all_to_all | solution.py:568
  7.3 0.7 copy-start.9
  7.4 0.7 copy-start.10
  8.1 0.7 copy-start.8
  8.1 1.1 %copy-start.1 = (f32[3,64,648]{2,1,0:T(8,128)S(1)}, f32[3,64,648]{2,1,0:T(8,128)}, u32[]{:S(2)}) copy-start(f32[3,64,648]{2,1,0:T(8,128)} %velocity.3) | copy-start | bytes 1492996
  8.8 0.7 copy-start.4
  11.3 0.8 copy-start.2
  32.0 17.1 %copy-start.3 = (bf16[256,1024]{1,0:T(8,128)(2,1)S(1)}, bf16[256,1024]{1,0:T(8,128)(2,1)}, u32[]{:S(2)}) copy-start(bf16[256,1024]{1,0:T(8,128)(2,1)} %copy-done.2) | copy-start | bytes 1572868
  32.5 16.6 %collective-permute-start = (f32[200,128]{1,0:T(8,128)S(1)}, f32[200,128]{1,0:T(8,128)S(1)}, u32[]{:S(2)}, u32[]{:S(2)}) collective-permute-start(f32[200,128]{1,0:T(8,128)S(1)} %get-tuple-element.34.own), channel_id=1, source_target_pairs={{8,16},{24,32},{40,48},{56,64},{72,80},{88,96},{104,112},{120,128}... | collective-permute-start | bytes 307208 | tf_op jit(solution)/shard_map/ppermute | solution.py:542
  49.1 8.9 %copy-start.5 = (bf16[768,128]{1,0:T(8,128)(2,1)S(1)}, bf16[768,128]{1,0:T(8,128)(2,1)}, u32[]{:S(2)}) copy-start(bf16[768,128]{1,0:T(8,128)(2,1)} %constant.29.clone.derive_back) | copy-start | bytes 589828
  50.1 7.9 %collective-permute-start.1 = (f32[64,128]{1,0:T(8,128)S(1)}, f32[64,128]{1,0:T(8,128)S(1)}, u32[]{:S(2)}, u32[]{:S(2)}) collective-permute-start(f32[64,128]{1,0:T(8,128)S(1)} %get-tuple-element.39.own), channel_id=1, source_target_pairs={{8,16},{24,32},{40,48},{56,64},{72,80},{88,96},{104,112},{120,128}... | collective-permute-start | bytes 98312 | tf_op jit(solution)/shard_map/ppermute | solution.py:542
  59.1 9.2 %collective-permute-start.2 = (f32[64,128]{1,0:T(8,128)S(1)}, f32[64,128]{1,0:T(8,128)S(1)}, u32[]{:S(2)}, u32[]{:S(2)}) collective-permute-start(f32[64,128]{1,0:T(8,128)S(1)} %get-tuple-element.43.own), channel_id=1, source_target_pairs={{8,16},{24,32},{40,48},{56,64},{72,80},{88,96},{104,112},{120,128}... | collective-permute-start | bytes 98312 | tf_op jit(solution)/shard_map/ppermute | solution.py:542

commit v6 on v5

--- a/solution.py
+++ b/solution.py
@@ -23,6 +23,7 @@
 CHUNK = 64
 HALF = 256
 
+SCALE = 2.0**-12
 PENALTY = 1.0
 TIME_STEP = 0.01
 
@@ -433,7 +434,7 @@
     first_out[...] = rim[:, :LANES]
     second_out[...] = rim[:, LANES:]
     square = lane_sum(total * total * inverse[...])
-    energy = lane_sum(flux_x * grad_x + flux_y * grad_y + weighted * total)
+    energy = SCALE * lane_sum(flux_x * grad_x + flux_y * grad_y + weighted * total)
     column = lax.broadcasted_iota(jnp.int32, (ROWS, LANES), 1)
     sums[...] = jnp.where(column == 0, square, jnp.where(column == 1, energy, 0.0))
 
@@ -451,8 +452,9 @@
     image[...] = total
     image_x[...] = grad_x
     image_y[...] = grad_y
-    square = lane_sum(total * total * inverse[...])
-    energy = lane_sum(mass * (grad_x * grad_x + grad_y * grad_y + shift * (total * total)))
+    square = lane_sum(total * total * (SCALE**2 * inverse[...]))
+    energy = grad_x * grad_x + grad_y * grad_y + shift * (total * total)
+    energy = lane_sum((SCALE**3 * mass) * energy)
     column = lax.broadcasted_iota(jnp.int32, (ROWS, LANES), 1)
     table = jnp.where(column == 2, square, jnp.where(column == 3, energy, sums[...]))
     table = jnp.concatenate([table, jnp.zeros((LANES - ROWS, LANES), f32)], axis=0)
@@ -483,8 +485,8 @@
     ratio = new / g0
     curve = (1.0 + ratio) * ((1.0 + ratio) * g1 - 2.0 * step0 * g2) + step0 * step0 * g3
     step1 = new / curve
-    by_right = step0 + step1 * (1.0 + ratio)
-    by_image = -step1 * step0
+    by_right = SCALE * (step0 + step1 * (1.0 + ratio))
+    by_image = -(SCALE * step1) * (SCALE * step0)
     pair = jnp.concatenate([by_right, by_image, jnp.zeros((6, LANES), f32)], axis=0)
     turned = jnp.transpose(pair)
     by_right = turned[:ROWS, 0:1]

time: 93.6 us -> 93.6 us (level)
  no operation moved by 1% of the time
where the time goes in v6:
time: 93.6 us; the launch traced here: 93.1 us
  blocking collectives  49.9 us (53%)
  starting transfers between devices  23.7 us (25%)
  Pallas kernels  9.14 us (10%)
  waiting for transfers between devices  5.57 us (6%)
  local copies, waits for them, and re-layouts  3.97 us (4%)
    all_to_all x1, blocking collectives, on_device(): gathered = lax.all_to_all(spread, 'elem', 0, 0)  22.6 us
    ppermute x3, starting transfers between devices, swap(): lax.ppermute(first, 'elem', across)  19.2 us
    all_gather x3, blocking collectives, swap(): lax.all_gather(second, 'elem', axis_index_groups=beside)  14.5 us
    all_to_all x1, blocking collectives, on_device(): returned = lax.all_to_all(spectral, 'mode', 0, 0)  12.8 us
    pallas_call x8, Pallas kernels, call(): pl.pallas_call(kernel, in_specs=specs, out_specs=[ANY if i in aliases.val...  9.14 us
    all_to_all x1, waiting for transfers between devices, on_device(): arrived = lax.all_to_all(packed, 'mode', 0, 0)  5.56 us
    all_to_all x1, starting transfers between devices, on_device(): arrived = lax.all_to_all(packed, 'mode', 0, 0)  4.43 us
    unnamed x25, local copies, waits for them, and re-layouts  3.96 us
  transfers between devices with their start and end apart: 4, of which 1 were waited for; matrix products, arithmetic and copies ran while one was open for 0% of the time, Pallas kernels for 2%

profile of v6, /device:TPU:8, one launch (start us, length us, event | category | flops | bytes accessed | tf_op | source)
XLA Modules:
  0.0 93.1 jit_solution(15898527993696653194)
XLA Ops:
  0.6 0.0 copy-start
  0.6 1.1 %copy-done = f32[3,64,648]{2,1,0:T(8,128)S(1)} copy-done((f32[3,64,648]{2,1,0:T(8,128)S(1)}, f32[3,64,648]{2,1,0:T(8,128)}, u32[]{:S(2)}) %copy-start) | copy-done | bytes 497688
  1.7 1.2 %pack.1 = f32[8,2,64,128]{3,2,1,0:T(8,128)} custom-call(f32[3,64,648]{2,1,0:T(8,128)S(1)} %copy-done), custom_call_target="tpu_custom_call" | custom-call | bytes 1021952 | tf_op jit(solution)/shard_map/pack/pallas_call | solution.py:519
  2.9 0.0 copy-start.7
  2.9 0.0 copy-start.6
  2.9 4.4 %all-to-all-start = ((f32[8,2,64,128]{3,2,1,0:T(8,128)}), f32[8,2,64,128]{3,2,1,0:T(8,128)S(1)}, u32[]{:S(2)}, u32[]{:S(2)}) async-start(f32[8,2,64,128]{3,2,1,0:T(8,128)} %pack.1), calls=%async_computation | async-start | bytes 1048576 | tf_op jit(solution)/shard_map/all_to_all | solution.py:570
  7.3 0.0 copy-start.9
  7.4 0.0 copy-start.10
  7.4 0.7 copy-done.9
  8.0 0.0 copy-done.10
  8.1 0.0 copy-done.7
  8.1 0.0 copy-done.6
  8.1 0.0 copy-start.8
  8.1 0.0 copy-start.1
  8.1 0.1 copy.21.fourier
  8.2 0.6 copy-done.8
  8.8 0.0 copy-start.4
  8.8 0.3 copy-done.1
  9.2 0.4 copy-done.4
  9.5 1.8 %prepare.1 = (f32[192,1024]{1,0:T(8,128)S(1)}, f32[8,1024]{1,0:T(8,128)S(1)}, f32[8,128]{1,0:T(8,128)S(1)}, bf16[256,1024]{1,0:T(8,128)(2,1)S(1)}, bf16[1024,256...) custom-call(s32[1]{0:T(128)} %bitcast.mode, ...), custom_call_target="tpu_custom_call", output_to_operand_aliasing={{5}: (6, {}), {6}: (7, {})} | custom-call | flops 16777216 | bytes 4351696 | tf_op jit(solution)/shard_map/prepare/pallas_call | solution.py:519
  11.3 0.0 copy-start.2
  11.4 0.8 copy-done.2
  12.1 5.6 %all-to-all-done.packed = f32[8,2,64,128]{3,2,1,0:T(8,128)S(1)} async-done(((f32[8,2,64,128]{3,2,1,0:T(8,128)}), f32[8,2,64,128]{3,2,1,0:T(8,128)S(1)}, u32[]{:S(2)}, u32[]{:S(2)}) %all-to-all-start) | async-done | bytes 524320 | tf_op jit(solution)/shard_map/all_to_all | solution.py:570
  17.7 1.5 %convect.1 = f32[8,2,64,128]{3,2,1,0:T(8,128)S(1)} custom-call(f32[8,2,64,128]{3,2,1,0:T(8,128)S(1)} %all-to-all-done.packed, f32[8,128]{1,0:T(8,128)S(1)} %get-tuple-element.28.own_metric, bf16[2,256,768]{2,1,0:T(8,128)(2,1)S(1)} %get-tuple-element.29.fourier, bf16[384,256]{1,0:T(8,128)(2,1)S(1)} %get-tuple-element.30.derive), custom_call_target="tpu_custom_call" | custom-call | flops 1073741824 | bytes 2035712 | tf_op jit(solution)/shard_map/convect/pallas_call | solution.py:519
  19.2 12.8 %all_to_all.15.spectral = f32[8,2,64,128]{3,2,1,0:T(8,128)S(1)} all-to-all(f32[8,2,64,128]{3,2,1,0:T(8,128)S(1)} %convect.1), channel_id=1, replica_groups=mesh['elem'=64,'mode'=8] {'mode'}, dimensions={0} | all-to-all | bytes 1048576 | tf_op jit(solution)/shard_map/all_to_all | solution.py:579
  32.0 0.0 copy-start.3
  32.0 0.4 weigh.1
  32.5 11.3 %collective-permute-start = (f32[200,128]{1,0:T(8,128)S(1)}, f32[200,128]{1,0:T(8,128)S(1)}, u32[]{:S(2)}, u32[]{:S(2)}) collective-permute-start(f32[200,128]{1,0:T(8,128)S(1)} %get-tuple-element.34.own), channel_id=1, source_target_pairs={{8,16},{24,32},{40,48},{56,64},{72,80},{88,96},{104,112},{120,128}... | collective-permute-start | bytes 307208 | tf_op jit(solution)/shard_map/ppermute | solution.py:544
  43.8 5.3 %all-gather = f32[400,128]{1,0:T(8,128)S(1)} all-gather(f32[200,128]{1,0:T(8,128)S(1)} %get-tuple-element.35), channel_id=2, replica_groups={{0,8},{16,24},{32,40},{48,56},{64,72},{80,88},{96,104},{112,120},{128,1..., dimensions={0}, use_global_device_ids=true | all-gather | bytes 307200 | tf_op jit(solution)/shard_map/all_gather | solution.py:545
  49.1 0.0 collective-permute-done.first_in
  49.1 0.0 copy-done.3
  49.1 0.0 copy-start.5
  49.1 1.0 %star.1 = (f32[192,1024]{1,0:T(8,128)S(1)}, f32[1,1024]{1,0:T(1,128)S(1)}, f32[64,1024]{1,0:T(8,128)S(1)}, f32[64,128]{1,0:T(8,128)S(1)}, f32[64,128]{1,0:T(8,128)S(1)}) custom-call(s32[1]{0:T(128)} %bitcast.mode, s32[1]{0:T(128)} %bitcast.1.parity, f32[200,1024]{1,0:T(8,128)S(1)} %get-tuple-element.33.share, f32[200,128]{1,0:T(8,128)S(1)} %get-tuple-element.34.own, ...), custom_call_target="tpu_custom_call" | custom-call | flops 536870912 | bytes 4411400 | tf_op jit(solution)/shard_map/star/pallas_call | solution.py:519
  50.1 3.3 %collective-permute-start.1 = (f32[64,128]{1,0:T(8,128)S(1)}, f32[64,128]{1,0:T(8,128)S(1)}, u32[]{:S(2)}, u32[]{:S(2)}) collective-permute-start(f32[64,128]{1,0:T(8,128)S(1)} %get-tuple-element.39.own), channel_id=1, source_target_pairs={{8,16},{24,32},{40,48},{56,64},{72,80},{88,96},{104,112},{120,128}... | collective-permute-start | bytes 98312 | tf_op jit(solution)/shard_map/ppermute | solution.py:544
  53.4 4.6 %all-gather.1 = f32[128,128]{1,0:T(8,128)S(1)} all-gather(f32[64,128]{1,0:T(8,128)S(1)} %get-tuple-element.40), channel_id=3, replica_groups={{0,8},{16,24},{32,40},{48,56},{64,72},{80,88},{96,104},{112,120},{128,1..., dimensions={0}, use_global_device_ids=true | all-gather | bytes 98304 | tf_op jit(solution)/shard_map/all_gather | solution.py:545
  58.0 0.0 collective-permute-done.1.first_in
  58.0 0.0 copy-done.5
  58.0 1.0 %helmholtz.1 = (f32[64,1024]{1,0:T(8,128)S(1)}, f32[64,1024]{1,0:T(8,128)S(1)}, f32[64,1024]{1,0:T(8,128)S(1)}, f32[64,1024]{1,0:T(8,128)S(1)}, f32[64,128]{1,0:...) custom-call(s32[1]{0:T(128)} %bitcast.mode, s32[1]{0:T(128)} %bitcast.1.parity, ...), custom_call_target="tpu_custom_call" | custom-call | flops 536870912 | bytes 3018760 | tf_op jit(solution)/shard_map/helmholtz/pallas_call | solution.py:519
  59.1 4.6 %collective-permute-start.2 = (f32[64,128]{1,0:T(8,128)S(1)}, f32[64,128]{1,0:T(8,128)S(1)}, u32[]{:S(2)}, u32[]{:S(2)}) collective-permute-start(f32[64,128]{1,0:T(8,128)S(1)} %get-tuple-element.43.own), channel_id=1, source_target_pairs={{8,16},{24,32},{40,48},{56,64},{72,80},{88,96},{104,112},{120,128}... | collective-permute-start | bytes 98312 | tf_op jit(solution)/shard_map/ppermute | solution.py:544
  63.7 4.6 %all-gather.2 = f32[128,128]{1,0:T(8,128)S(1)} all-gather(f32[64,128]{1,0:T(8,128)S(1)} %get-tuple-element.44), channel_id=4, replica_groups={{0,8},{16,24},{32,40},{48,56},{64,72},{80,88},{96,104},{112,120},{128,1..., dimensions={0}, use_global_device_ids=true | all-gather | bytes 98304 | tf_op jit(solution)/shard_map/all_gather | solution.py:545
  68.3 0.0 collective-permute-done.2.first_in
  68.3 0.7 image.1
  69.0 22.6 %all_to_all.16 = f32[64,1,256]{2,1,0:T(1,128)S(1)} all-to-all(f32[64,1,256]{2,1,0:T(1,128)S(1)} %get-tuple-element.46), channel_id=1, replica_groups=mesh['elem'=64,'mode'=8] {'elem'}, dimensions={0} | all-to-all | bytes 131072 | tf_op jit(solution)/shard_map/all_to_all | solution.py:608
  91.6 1.5 %finish.1 = (f32[3,64,648]{2,1,0:T(8,128)}, f32[64,648]{1,0:T(8,128)}) custom-call(s32[1]{0:T(128)} %bitcast.mode, f32[64,256]{1,0:T(8,128)S(1)} %bitcast.10, f32[192,1024]{1,0:T(8,128)S(1)} %get-tuple-element.47.star, f32[64,1024]{1,0:T(8,128)S(1)} %get-tuple-element.48.right, f32[64,1024]{1,0:T(8,128)S(1)} %get-tuple-element.49.right_x, ...), custom_call_target="tpu_custom_call" | custom-call | bytes 3088388 | tf_op jit(solution)/shard_map/finish/pallas_call | solution.py:519
  (5 shorter events, 0.0 us)
Async XLA Ops:
  0.6 1.1 %copy-start = (f32[3,64,648]{2,1,0:T(8,128)S(1)}, f32[3,64,648]{2,1,0:T(8,128)}, u32[]{:S(2)}) copy-start(f32[3,64,648]{2,1,0:T(8,128)} %velocity.3) | copy-start | bytes 1492996
  2.9 5.1 %copy-start.7 = (bf16[384,256]{1,0:T(8,128)(2,1)S(1)}, bf16[384,256]{1,0:T(8,128)(2,1)}, u32[]{:S(2)}) copy-start(bf16[384,256]{1,0:T(8,128)(2,1)} %constant.28.clone) | copy-start | bytes 589828
  2.9 5.2 %copy-start.6 = (bf16[2,256,768]{2,1,0:T(8,128)(2,1)S(1)}, bf16[2,256,768]{2,1,0:T(8,128)(2,1)}, u32[]{:S(2)}) copy-start(bf16[2,256,768]{2,1,0:T(8,128)(2,1)} %constant.30.clone) | copy-start | bytes 2359300
  2.9 14.8 %all-to-all-start = ((f32[8,2,64,128]{3,2,1,0:T(8,128)}), f32[8,2,64,128]{3,2,1,0:T(8,128)S(1)}, u32[]{:S(2)}, u32[]{:S(2)}) async-start(f32[8,2,64,128]{3,2,1,0:T(8,128)} %pack.1), calls=%async_computation | async-start | bytes 1048576 | tf_op jit(solution)/shard_map/all_to_all | solution.py:570
  7.3 0.7 copy-start.9
  7.4 0.7 copy-start.10
  8.1 0.7 copy-start.8
  8.1 1.1 %copy-start.1 = (f32[3,64,648]{2,1,0:T(8,128)S(1)}, f32[3,64,648]{2,1,0:T(8,128)}, u32[]{:S(2)}) copy-start(f32[3,64,648]{2,1,0:T(8,128)} %velocity.3) | copy-start | bytes 1492996
  8.8 0.7 copy-start.4
  11.3 0.8 copy-start.2
  32.0 17.1 %copy-start.3 = (bf16[256,1024]{1,0:T(8,128)(2,1)S(1)}, bf16[256,1024]{1,0:T(8,128)(2,1)}, u32[]{:S(2)}) copy-start(bf16[256,1024]{1,0:T(8,128)(2,1)} %copy-done.2) | copy-start | bytes 1572868
  32.5 16.6 %collective-permute-start = (f32[200,128]{1,0:T(8,128)S(1)}, f32[200,128]{1,0:T(8,128)S(1)}, u32[]{:S(2)}, u32[]{:S(2)}) collective-permute-start(f32[200,128]{1,0:T(8,128)S(1)} %get-tuple-element.34.own), channel_id=1, source_target_pairs={{8,16},{24,32},{40,48},{56,64},{72,80},{88,96},{104,112},{120,128}... | collective-permute-start | bytes 307208 | tf_op jit(solution)/shard_map/ppermute | solution.py:544
  49.1 8.9 %copy-start.5 = (bf16[768,128]{1,0:T(8,128)(2,1)S(1)}, bf16[768,128]{1,0:T(8,128)(2,1)}, u32[]{:S(2)}) copy-start(bf16[768,128]{1,0:T(8,128)(2,1)} %constant.29.clone.derive_back) | copy-start | bytes 589828
  50.1 7.9 %collective-permute-start.1 = (f32[64,128]{1,0:T(8,128)S(1)}, f32[64,128]{1,0:T(8,128)S(1)}, u32[]{:S(2)}, u32[]{:S(2)}) collective-permute-start(f32[64,128]{1,0:T(8,128)S(1)} %get-tuple-element.39.own), channel_id=1, source_target_pairs={{8,16},{24,32},{40,48},{56,64},{72,80},{88,96},{104,112},{120,128}... | collective-permute-start | bytes 98312 | tf_op jit(solution)/shard_map/ppermute | solution.py:544
  59.1 9.2 %collective-permute-start.2 = (f32[64,128]{1,0:T(8,128)S(1)}, f32[64,128]{1,0:T(8,128)S(1)}, u32[]{:S(2)}, u32[]{:S(2)}) collective-permute-start(f32[64,128]{1,0:T(8,128)S(1)} %get-tuple-element.43.own), channel_id=1, source_target_pairs={{8,16},{24,32},{40,48},{56,64},{72,80},{88,96},{104,112},{120,128}... | collective-permute-start | bytes 98312 | tf_op jit(solution)/shard_map/ppermute | solution.py:544

commit v7 on v6

--- a/solution.py
+++ b/solution.py
@@ -64,13 +64,13 @@
 
 
 def as_right(table):
-    high, low = halves(table)
-    return np.concatenate([high, high, low], axis=0)
+    high, middle = halves(table)
+    rest = table - high.astype(np.float64) - middle.astype(np.float64)
+    return np.concatenate([high, middle, rest.astype(np.float32).astype(jnp.bfloat16)], axis=0)
 
 
 def as_left(table):
-    high, low = halves(table)
-    return np.concatenate([high, high, low], axis=1)
+    return np.concatenate(halves(table), axis=1)
 
 
 def derivative_tables():
@@ -97,14 +97,32 @@
     return jnp.dot(a, b, preferred_element_type=f32)
 
 
+def split3(x):
+    high = x.astype(bf16)
+    rest = x - high.astype(f32)
+    middle = rest.astype(bf16)
+    return high, middle, (rest - middle.astype(f32)).astype(bf16)
+
+
 def times_table(x, table):
+    inner = x.shape[1]
     high, low = split2(x)
-    return mm(jnp.concatenate([high, low, high], axis=1), table)
+    table = jnp.concatenate([table[:inner], table[: 2 * inner]], axis=0)
+    return mm(jnp.concatenate([low, high, high], axis=1), table)
+
+
+def times_fine(x, table):
+    inner = x.shape[1]
+    high, middle, low = split3(x)
+    table = jnp.concatenate([table[:inner], table[: 2 * inner], table], axis=0)
+    return mm(jnp.concatenate([low, middle, middle, high, high, high], axis=1), table)
 
 
 def table_times(table, x):
+    inner = x.shape[0]
     high, low = split2(x)
-    return mm(table, jnp.concatenate([high, low, high], axis=0))
+    table = jnp.concatenate([table[:, :inner], table], axis=1)
+    return mm(table, jnp.concatenate([low, high, high], axis=0))
 
 
 def times_incidence(x, incidence):
@@ -122,8 +140,8 @@
     return jnp.concatenate([x[rows * q : rows * (q + 1)] for q in range(QUADS)], axis=1)
 
 
-def gradient(x, metric, table):
-    derived = times_table(stacked(x), table)
+def gradient(x, metric, table, times=times_table):
+    derived = times(stacked(x), table)
     along_r = unstacked(derived[:, :LANES])
     along_s = unstacked(derived[:, LANES:])
     return (
@@ -319,7 +337,7 @@
         value = wide[:, :PACK]
         slope = wide[:, PACK:]
         speed = [unpacked(value, c) for c in range(3)]
-        derived = times_table(jnp.concatenate(speed, axis=0), table)
+        derived = times_fine(jnp.concatenate(speed, axis=0), table)
         weight_r = speed[0] * metric[0:1] + speed[1] * metric[1:2]
         weight_s = speed[0] * metric[2:3] + speed[1] * metric[3:4]
         terms = []
@@ -392,8 +410,8 @@
     )
     star[...] = field[...] + scale * total[: 3 * ROWS]
     table = derive[...]
-    star_x = gradient(star[0:ROWS], metric, table)[0]
-    star_y = gradient(star[ROWS : 2 * ROWS], metric, table)[1]
+    star_x = gradient(star[0:ROWS], metric, table, times_fine)[0]
+    star_y = gradient(star[ROWS : 2 * ROWS], metric, table, times_fine)[1]
     divergence = star_x + star_y + along_z(star[2 * ROWS :], mode[0])
     result = (-1.0 / TIME_STEP) * (metric[4:5] * divergence)
     share_out[...] = result

time: 93.6 us -> 94 us (level)
  no operation moved by 1% of the time
where the time goes in v7:
time: 94 us; the launch traced here: 93.5 us
  blocking collectives  49.9 us (53%)
  starting transfers between devices  23.7 us (25%)
  Pallas kernels  9.56 us (10%)
  waiting for transfers between devices  5.57 us (6%)
  local copies, waits for them, and re-layouts  3.97 us (4%)
    all_to_all x1, blocking collectives, on_device(): gathered = lax.all_to_all(spread, 'elem', 0, 0)  22.6 us
    ppermute x3, starting transfers between devices, swap(): lax.ppermute(first, 'elem', across)  19.2 us
    all_gather x3, blocking collectives, swap(): lax.all_gather(second, 'elem', axis_index_groups=beside)  14.5 us
    all_to_all x1, blocking collectives, on_device(): returned = lax.all_to_all(spectral, 'mode', 0, 0)  12.8 us
    pallas_call x8, Pallas kernels, call(): pl.pallas_call(kernel, in_specs=specs, out_specs=[ANY if i in aliases.val...  9.56 us
    all_to_all x1, waiting for transfers between devices, on_device(): arrived = lax.all_to_all(packed, 'mode', 0, 0)  5.56 us
    all_to_all x1, starting transfers between devices, on_device(): arrived = lax.all_to_all(packed, 'mode', 0, 0)  4.43 us
    unnamed x25, local copies, waits for them, and re-layouts  3.96 us
  transfers between devices with their start and end apart: 4, of which 1 were waited for; matrix products, arithmetic and copies ran while one was open for 0% of the time, Pallas kernels for 2%

profile of v7, /device:TPU:8, one launch (start us, length us, event | category | flops | bytes accessed | tf_op | source)
XLA Modules:
  0.0 93.5 jit_solution(12163845406023084959)
XLA Ops:
  0.6 0.0 copy-start
  0.6 1.1 %copy-done = f32[3,64,648]{2,1,0:T(8,128)S(1)} copy-done((f32[3,64,648]{2,1,0:T(8,128)S(1)}, f32[3,64,648]{2,1,0:T(8,128)}, u32[]{:S(2)}) %copy-start) | copy-done | bytes 497688
  1.7 1.2 %pack.1 = f32[8,2,64,128]{3,2,1,0:T(8,128)} custom-call(f32[3,64,648]{2,1,0:T(8,128)S(1)} %copy-done), custom_call_target="tpu_custom_call" | custom-call | bytes 1021952 | tf_op jit(solution)/shard_map/pack/pallas_call | solution.py:537
  2.9 0.0 copy-start.7
  2.9 0.0 copy-start.6
  2.9 4.4 %all-to-all-start = ((f32[8,2,64,128]{3,2,1,0:T(8,128)}), f32[8,2,64,128]{3,2,1,0:T(8,128)S(1)}, u32[]{:S(2)}, u32[]{:S(2)}) async-start(f32[8,2,64,128]{3,2,1,0:T(8,128)} %pack.1), calls=%async_computation | async-start | bytes 1048576 | tf_op jit(solution)/shard_map/all_to_all | solution.py:588
  7.3 0.0 copy-start.9
  7.4 0.0 copy-start.10
  7.4 0.7 copy-done.9
  8.0 0.0 copy-done.10
  8.1 0.0 copy-done.7
  8.1 0.0 copy-done.6
  8.1 0.0 copy-start.8
  8.1 0.0 copy-start.1
  8.2 0.6 copy-done.8
  8.8 0.0 copy-start.4
  8.8 0.3 copy-done.1
  9.2 0.4 copy-done.4
  9.5 1.8 %prepare.1 = (f32[192,1024]{1,0:T(8,128)S(1)}, f32[8,1024]{1,0:T(8,128)S(1)}, f32[8,128]{1,0:T(8,128)S(1)}, bf16[256,1024]{1,0:T(8,128)(2,1)S(1)}, bf16[1024,256...) custom-call(s32[1]{0:T(128)} %bitcast.mode, ...), custom_call_target="tpu_custom_call", output_to_operand_aliasing={{5}: (6, {}), {6}: (7, {})} | custom-call | flops 16777216 | bytes 3827408 | tf_op jit(solution)/shard_map/prepare/pallas_call | solution.py:537
  11.3 0.0 copy-start.2
  11.4 0.8 copy-done.2
  12.1 5.6 %all-to-all-done.packed = f32[8,2,64,128]{3,2,1,0:T(8,128)S(1)} async-done(((f32[8,2,64,128]{3,2,1,0:T(8,128)}), f32[8,2,64,128]{3,2,1,0:T(8,128)S(1)}, u32[]{:S(2)}, u32[]{:S(2)}) %all-to-all-start) | async-done | bytes 524320 | tf_op jit(solution)/shard_map/all_to_all | solution.py:588
  17.7 1.8 %convect.1 = f32[8,2,64,128]{3,2,1,0:T(8,128)S(1)} custom-call(f32[8,2,64,128]{3,2,1,0:T(8,128)S(1)} %all-to-all-done.packed, f32[8,128]{1,0:T(8,128)S(1)} %get-tuple-element.28.own_metric, bf16[2,256,512]{2,1,0:T(8,128)(2,1)S(1)} %get-tuple-element.29.fourier, bf16[384,256]{1,0:T(8,128)(2,1)S(1)} %get-tuple-element.30.derive), custom_call_target="tpu_custom_call" | custom-call | flops 1073741824 | bytes 1773568 | tf_op jit(solution)/shard_map/convect/pallas_call | solution.py:537
  19.5 12.8 %all_to_all.15.spectral = f32[8,2,64,128]{3,2,1,0:T(8,128)S(1)} all-to-all(f32[8,2,64,128]{3,2,1,0:T(8,128)S(1)} %convect.1), channel_id=1, replica_groups=mesh['elem'=64,'mode'=8] {'mode'}, dimensions={0} | all-to-all | bytes 1048576 | tf_op jit(solution)/shard_map/all_to_all | solution.py:597
  32.3 0.0 copy-start.3
  32.3 0.4 weigh.1
  32.7 11.3 %collective-permute-start = (f32[200,128]{1,0:T(8,128)S(1)}, f32[200,128]{1,0:T(8,128)S(1)}, u32[]{:S(2)}, u32[]{:S(2)}) collective-permute-start(f32[200,128]{1,0:T(8,128)S(1)} %get-tuple-element.34.own), channel_id=1, source_target_pairs={{8,16},{24,32},{40,48},{56,64},{72,80},{88,96},{104,112},{120,128}... | collective-permute-start | bytes 307208 | tf_op jit(solution)/shard_map/ppermute | solution.py:562
  44.0 5.3 %all-gather = f32[400,128]{1,0:T(8,128)S(1)} all-gather(f32[200,128]{1,0:T(8,128)S(1)} %get-tuple-element.35), channel_id=2, replica_groups={{0,8},{16,24},{32,40},{48,56},{64,72},{80,88},{96,104},{112,120},{128,1..., dimensions={0}, use_global_device_ids=true | all-gather | bytes 307200 | tf_op jit(solution)/shard_map/all_gather | solution.py:563
  49.4 0.0 collective-permute-done.first_in
  49.4 0.0 copy-done.3
  49.4 0.0 copy-start.5
  49.4 1.1 %star.1 = (f32[192,1024]{1,0:T(8,128)S(1)}, f32[1,1024]{1,0:T(1,128)S(1)}, f32[64,1024]{1,0:T(8,128)S(1)}, f32[64,128]{1,0:T(8,128)S(1)}, f32[64,128]{1,0:T(8,128)S(1)}) custom-call(s32[1]{0:T(128)} %bitcast.mode, s32[1]{0:T(128)} %bitcast.1.parity, f32[200,1024]{1,0:T(8,128)S(1)} %get-tuple-element.33.share, f32[200,128]{1,0:T(8,128)S(1)} %get-tuple-element.34.own, ...), custom_call_target="tpu_custom_call" | custom-call | flops 536870912 | bytes 4411400 | tf_op jit(solution)/shard_map/star/pallas_call | solution.py:537
  50.5 3.3 %collective-permute-start.1 = (f32[64,128]{1,0:T(8,128)S(1)}, f32[64,128]{1,0:T(8,128)S(1)}, u32[]{:S(2)}, u32[]{:S(2)}) collective-permute-start(f32[64,128]{1,0:T(8,128)S(1)} %get-tuple-element.39.own), channel_id=1, source_target_pairs={{8,16},{24,32},{40,48},{56,64},{72,80},{88,96},{104,112},{120,128}... | collective-permute-start | bytes 98312 | tf_op jit(solution)/shard_map/ppermute | solution.py:562
  53.8 4.6 %all-gather.1 = f32[128,128]{1,0:T(8,128)S(1)} all-gather(f32[64,128]{1,0:T(8,128)S(1)} %get-tuple-element.40), channel_id=3, replica_groups={{0,8},{16,24},{32,40},{48,56},{64,72},{80,88},{96,104},{112,120},{128,1..., dimensions={0}, use_global_device_ids=true | all-gather | bytes 98304 | tf_op jit(solution)/shard_map/all_gather | solution.py:563
  58.4 0.0 collective-permute-done.1.first_in
  58.4 0.0 copy-done.5
  58.4 1.1 %helmholtz.1 = (f32[64,1024]{1,0:T(8,128)S(1)}, f32[64,1024]{1,0:T(8,128)S(1)}, f32[64,1024]{1,0:T(8,128)S(1)}, f32[64,1024]{1,0:T(8,128)S(1)}, f32[64,128]{1,0:...) custom-call(s32[1]{0:T(128)} %bitcast.mode, s32[1]{0:T(128)} %bitcast.1.parity, ...), custom_call_target="tpu_custom_call" | custom-call | flops 536870912 | bytes 3018760 | tf_op jit(solution)/shard_map/helmholtz/pallas_call | solution.py:537
  59.5 4.6 %collective-permute-start.2 = (f32[64,128]{1,0:T(8,128)S(1)}, f32[64,128]{1,0:T(8,128)S(1)}, u32[]{:S(2)}, u32[]{:S(2)}) collective-permute-start(f32[64,128]{1,0:T(8,128)S(1)} %get-tuple-element.43.own), channel_id=1, source_target_pairs={{8,16},{24,32},{40,48},{56,64},{72,80},{88,96},{104,112},{120,128}... | collective-permute-start | bytes 98312 | tf_op jit(solution)/shard_map/ppermute | solution.py:562
  64.1 4.6 %all-gather.2 = f32[128,128]{1,0:T(8,128)S(1)} all-gather(f32[64,128]{1,0:T(8,128)S(1)} %get-tuple-element.44), channel_id=4, replica_groups={{0,8},{16,24},{32,40},{48,56},{64,72},{80,88},{96,104},{112,120},{128,1..., dimensions={0}, use_global_device_ids=true | all-gather | bytes 98304 | tf_op jit(solution)/shard_map/all_gather | solution.py:563
  68.7 0.0 collective-permute-done.2.first_in
  68.7 0.7 image.1
  69.4 22.6 %all_to_all.16 = f32[64,1,256]{2,1,0:T(1,128)S(1)} all-to-all(f32[64,1,256]{2,1,0:T(1,128)S(1)} %get-tuple-element.46), channel_id=1, replica_groups=mesh['elem'=64,'mode'=8] {'elem'}, dimensions={0} | all-to-all | bytes 131072 | tf_op jit(solution)/shard_map/all_to_all | solution.py:626
  92.0 1.5 %finish.1 = (f32[3,64,648]{2,1,0:T(8,128)}, f32[64,648]{1,0:T(8,128)}) custom-call(s32[1]{0:T(128)} %bitcast.mode, f32[64,256]{1,0:T(8,128)S(1)} %bitcast.10, f32[192,1024]{1,0:T(8,128)S(1)} %get-tuple-element.47.star, f32[64,1024]{1,0:T(8,128)S(1)} %get-tuple-element.48.right, f32[64,1024]{1,0:T(8,128)S(1)} %get-tuple-element.49.right_x, ...), custom_call_target="tpu_custom_call" | custom-call | bytes 3088388 | tf_op jit(solution)/shard_map/finish/pallas_call | solution.py:537
  (6 shorter events, 0.1 us)
Async XLA Ops:
  0.6 1.1 %copy-start = (f32[3,64,648]{2,1,0:T(8,128)S(1)}, f32[3,64,648]{2,1,0:T(8,128)}, u32[]{:S(2)}) copy-start(f32[3,64,648]{2,1,0:T(8,128)} %velocity.3) | copy-start | bytes 1492996
  2.9 5.1 %copy-start.7 = (bf16[384,256]{1,0:T(8,128)(2,1)S(1)}, bf16[384,256]{1,0:T(8,128)(2,1)}, u32[]{:S(2)}) copy-start(bf16[384,256]{1,0:T(8,128)(2,1)} %constant.28.clone) | copy-start | bytes 589828
  2.9 5.2 %copy-start.6 = (bf16[2,256,512]{2,1,0:T(8,128)(2,1)S(1)}, bf16[2,256,512]{2,1,0:T(8,128)(2,1)}, u32[]{:S(2)}) copy-start(bf16[2,256,512]{2,1,0:T(8,128)(2,1)} %constant.30.clone) | copy-start | bytes 1572868
  2.9 14.8 %all-to-all-start = ((f32[8,2,64,128]{3,2,1,0:T(8,128)}), f32[8,2,64,128]{3,2,1,0:T(8,128)S(1)}, u32[]{:S(2)}, u32[]{:S(2)}) async-start(f32[8,2,64,128]{3,2,1,0:T(8,128)} %pack.1), calls=%async_computation | async-start | bytes 1048576 | tf_op jit(solution)/shard_map/all_to_all | solution.py:588
  7.3 0.7 copy-start.9
  7.4 0.7 copy-start.10
  8.1 0.7 copy-start.8
  8.1 1.1 %copy-start.1 = (f32[3,64,648]{2,1,0:T(8,128)S(1)}, f32[3,64,648]{2,1,0:T(8,128)}, u32[]{:S(2)}) copy-start(f32[3,64,648]{2,1,0:T(8,128)} %velocity.3) | copy-start | bytes 1492996
  8.8 0.7 copy-start.4
  11.3 0.8 copy-start.2
  32.3 17.1 %copy-start.3 = (bf16[256,1024]{1,0:T(8,128)(2,1)S(1)}, bf16[256,1024]{1,0:T(8,128)(2,1)}, u32[]{:S(2)}) copy-start(bf16[256,1024]{1,0:T(8,128)(2,1)} %copy-done.2) | copy-start | bytes 1572868
  32.7 16.6 %collective-permute-start = (f32[200,128]{1,0:T(8,128)S(1)}, f32[200,128]{1,0:T(8,128)S(1)}, u32[]{:S(2)}, u32[]{:S(2)}) collective-permute-start(f32[200,128]{1,0:T(8,128)S(1)} %get-tuple-element.34.own), channel_id=1, source_target_pairs={{8,16},{24,32},{40,48},{56,64},{72,80},{88,96},{104,112},{120,128}... | collective-permute-start | bytes 307208 | tf_op jit(solution)/shard_map/ppermute | solution.py:562
  49.4 9.1 %copy-start.5 = (bf16[768,128]{1,0:T(8,128)(2,1)S(1)}, bf16[768,128]{1,0:T(8,128)(2,1)}, u32[]{:S(2)}) copy-start(bf16[768,128]{1,0:T(8,128)(2,1)} %constant.29.clone.derive_back) | copy-start | bytes 589828
  50.5 7.9 %collective-permute-start.1 = (f32[64,128]{1,0:T(8,128)S(1)}, f32[64,128]{1,0:T(8,128)S(1)}, u32[]{:S(2)}, u32[]{:S(2)}) collective-permute-start(f32[64,128]{1,0:T(8,128)S(1)} %get-tuple-element.39.own), channel_id=1, source_target_pairs={{8,16},{24,32},{40,48},{56,64},{72,80},{88,96},{104,112},{120,128}... | collective-permute-start | bytes 98312 | tf_op jit(solution)/shard_map/ppermute | solution.py:562
  59.5 9.2 %collective-permute-start.2 = (f32[64,128]{1,0:T(8,128)S(1)}, f32[64,128]{1,0:T(8,128)S(1)}, u32[]{:S(2)}, u32[]{:S(2)}) collective-permute-start(f32[64,128]{1,0:T(8,128)S(1)} %get-tuple-element.43.own), channel_id=1, source_target_pairs={{8,16},{24,32},{40,48},{56,64},{72,80},{88,96},{104,112},{120,128}... | collective-permute-start | bytes 98312 | tf_op jit(solution)/shard_map/ppermute | solution.py:562

commit v8 on v7

--- a/solution.py
+++ b/solution.py
@@ -185,7 +185,14 @@
     )
 
 
-def pack_kernel(velocity, packed):
+def pack_kernel(velocity, packed_far, packed, left):
+    half = QUADS // 2
+    copies = [
+        pltpu.make_async_copy(
+            packed.at[pl.ds(half * i, half)], packed_far.at[pl.ds(half * i, half)], left.at[i]
+        )
+        for i in range(2)
+    ]
     for q in range(QUADS):
         for c in range(3):
             start, stop = QUAD_NODES * c, QUAD_NODES * (c + 1)
@@ -196,6 +203,10 @@
                     c, :, node + low : node + high
                 ]
         packed[q, 1, :, 3 * QUAD_NODES - LANES :] = jnp.zeros((ROWS, PACK - 3 * QUAD_NODES), f32)
+        if q % half == half - 1:
+            copies[q // half].start()
+    for copy in copies:
+        copy.wait()
 
 
 def matches(column, row):
@@ -529,7 +540,7 @@
 ANY = pl.BlockSpec(memory_space=pl.ANY)
 
 
-def call(kernel, ins, outs, scratch=(), flops=0, name=None, aliases={}):
+def call(kernel, ins, outs, scratch=(), flops=0, name=None, aliases={}, far_outs=()):
     specs = [SMEM if a.dtype == jnp.int32 and a.shape == (1,) else VMEM for a in ins]
     specs = [ANY if i in aliases else spec for i, spec in enumerate(specs)]
     shapes = [jax.ShapeDtypeStruct(s, d) for s, d in outs]
@@ -537,7 +548,7 @@
     return pl.pallas_call(
         kernel,
         in_specs=specs,
-        out_specs=[ANY if i in aliases.values() else VMEM for i in range(len(shapes))],
+        out_specs=[ANY if i in aliases.values() or i in far_outs else VMEM for i in range(len(shapes))],
         out_shape=shapes,
         scratch_shapes=list(scratch),
         input_output_aliases=aliases,
@@ -566,7 +577,8 @@
     block = (QUADS, 2, ROWS, LANES)
     (packed,) = call(
         pack_kernel, [velocity], [(block, f32)],
-        name="pack",
+        scratch=[pltpu.VMEM(block, f32), pltpu.SemaphoreType.DMA((2,))],
+        name="pack", far_outs=(0,),
     )
     nodal = jnp.concatenate([metric, mass[None]], axis=0)
     tables = [fourier, derive]

time: 94 us -> 93.9 us (level)
  no operation moved by 1% of the time
where the time goes in v8:
time: 93.9 us; the launch traced here: 93.5 us
  blocking collectives  49.9 us (53%)
  starting transfers between devices  23.7 us (25%)
  Pallas kernels  9.48 us (10%)
  waiting for transfers between devices  5.57 us (6%)
  local copies, waits for them, and re-layouts  3.97 us (4%)
    all_to_all x1, blocking collectives, on_device(): gathered = lax.all_to_all(spread, 'elem', 0, 0)  22.6 us
    ppermute x3, starting transfers between devices, swap(): lax.ppermute(first, 'elem', across)  19.2 us
    all_gather x3, blocking collectives, swap(): lax.all_gather(second, 'elem', axis_index_groups=beside)  14.5 us
    all_to_all x1, blocking collectives, on_device(): returned = lax.all_to_all(spectral, 'mode', 0, 0)  12.8 us
    pallas_call x8, Pallas kernels, call(): pl.pallas_call(kernel, in_specs=specs, out_specs=[ANY if i in aliases.val...  9.48 us
    all_to_all x1, waiting for transfers between devices, on_device(): arrived = lax.all_to_all(packed, 'mode', 0, 0)  5.56 us
    all_to_all x1, starting transfers between devices, on_device(): arrived = lax.all_to_all(packed, 'mode', 0, 0)  4.44 us
    unnamed x25, local copies, waits for them, and re-layouts  3.97 us
  transfers between devices with their start and end apart: 4, of which 1 were waited for; matrix products, arithmetic and copies ran while one was open for 0% of the time, Pallas kernels for 2%

profile of v8, /device:TPU:8, one launch (start us, length us, event | category | flops | bytes accessed | tf_op | source)
XLA Modules:
  0.0 93.5 jit_solution(5768579117298301374)
XLA Ops:
  0.6 0.0 copy-start
  0.6 1.1 %copy-done = f32[3,64,648]{2,1,0:T(8,128)S(1)} copy-done((f32[3,64,648]{2,1,0:T(8,128)S(1)}, f32[3,64,648]{2,1,0:T(8,128)}, u32[]{:S(2)}) %copy-start) | copy-done | bytes 497688
  1.7 1.1 %pack.1 = f32[8,2,64,128]{3,2,1,0:T(8,128)} custom-call(f32[3,64,648]{2,1,0:T(8,128)S(1)} %copy-done), custom_call_target="tpu_custom_call" | custom-call | bytes 1021952 | tf_op jit(solution)/shard_map/pack/pallas_call | solution.py:548
  2.8 0.0 copy-start.7
  2.9 0.0 copy-start.6
  2.9 4.4 %all-to-all-start = ((f32[8,2,64,128]{3,2,1,0:T(8,128)}), f32[8,2,64,128]{3,2,1,0:T(8,128)S(1)}, u32[]{:S(2)}, u32[]{:S(2)}) async-start(f32[8,2,64,128]{3,2,1,0:T(8,128)} %pack.1), calls=%async_computation | async-start | bytes 1048576 | tf_op jit(solution)/shard_map/all_to_all | solution.py:600
  7.3 0.0 copy-start.9
  7.3 0.0 copy-start.10
  7.3 0.7 copy-done.9
  8.0 0.0 copy-done.10
  8.0 0.0 copy-done.7
  8.0 0.0 copy-done.6
  8.1 0.0 copy-start.8
  8.1 0.0 copy-start.1
  8.1 0.6 copy-done.8
  8.8 0.0 copy-start.4
  8.8 0.3 copy-done.1
  9.1 0.4 copy-done.4
  9.5 1.8 %prepare.1 = (f32[192,1024]{1,0:T(8,128)S(1)}, f32[8,1024]{1,0:T(8,128)S(1)}, f32[8,128]{1,0:T(8,128)S(1)}, bf16[256,1024]{1,0:T(8,128)(2,1)S(1)}, bf16[1024,256...) custom-call(s32[1]{0:T(128)} %bitcast.mode, ...), custom_call_target="tpu_custom_call", output_to_operand_aliasing={{5}: (6, {}), {6}: (7, {})} | custom-call | flops 16777216 | bytes 3827408 | tf_op jit(solution)/shard_map/prepare/pallas_call | solution.py:548
  11.3 0.0 copy-start.2
  11.3 0.8 copy-done.2
  12.1 5.6 %all-to-all-done.packed = f32[8,2,64,128]{3,2,1,0:T(8,128)S(1)} async-done(((f32[8,2,64,128]{3,2,1,0:T(8,128)}), f32[8,2,64,128]{3,2,1,0:T(8,128)S(1)}, u32[]{:S(2)}, u32[]{:S(2)}) %all-to-all-start) | async-done | bytes 524320 | tf_op jit(solution)/shard_map/all_to_all | solution.py:600
  17.7 1.8 %convect.1 = f32[8,2,64,128]{3,2,1,0:T(8,128)S(1)} custom-call(f32[8,2,64,128]{3,2,1,0:T(8,128)S(1)} %all-to-all-done.packed, f32[8,128]{1,0:T(8,128)S(1)} %get-tuple-element.28.own_metric, bf16[2,256,512]{2,1,0:T(8,128)(2,1)S(1)} %get-tuple-element.29.fourier, bf16[384,256]{1,0:T(8,128)(2,1)S(1)} %get-tuple-element.30.derive), custom_call_target="tpu_custom_call" | custom-call | flops 1073741824 | bytes 1773568 | tf_op jit(solution)/shard_map/convect/pallas_call | solution.py:548
  19.4 12.8 %all_to_all.15.spectral = f32[8,2,64,128]{3,2,1,0:T(8,128)S(1)} all-to-all(f32[8,2,64,128]{3,2,1,0:T(8,128)S(1)} %convect.1), channel_id=1, replica_groups=mesh['elem'=64,'mode'=8] {'mode'}, dimensions={0} | all-to-all | bytes 1048576 | tf_op jit(solution)/shard_map/all_to_all | solution.py:609
  32.2 0.0 copy-start.3
  32.2 0.4 weigh.1
  32.7 11.3 %collective-permute-start = (f32[200,128]{1,0:T(8,128)S(1)}, f32[200,128]{1,0:T(8,128)S(1)}, u32[]{:S(2)}, u32[]{:S(2)}) collective-permute-start(f32[200,128]{1,0:T(8,128)S(1)} %get-tuple-element.34.own), channel_id=1, source_target_pairs={{8,16},{24,32},{40,48},{56,64},{72,80},{88,96},{104,112},{120,128}... | collective-permute-start | bytes 307208 | tf_op jit(solution)/shard_map/ppermute | solution.py:573
  44.0 5.3 %all-gather = f32[400,128]{1,0:T(8,128)S(1)} all-gather(f32[200,128]{1,0:T(8,128)S(1)} %get-tuple-element.35), channel_id=2, replica_groups={{0,8},{16,24},{32,40},{48,56},{64,72},{80,88},{96,104},{112,120},{128,1..., dimensions={0}, use_global_device_ids=true | all-gather | bytes 307200 | tf_op jit(solution)/shard_map/all_gather | solution.py:574
  49.3 0.0 collective-permute-done.first_in
  49.3 0.0 copy-done.3
  49.3 0.0 copy-start.5
  49.3 1.1 %star.1 = (f32[192,1024]{1,0:T(8,128)S(1)}, f32[1,1024]{1,0:T(1,128)S(1)}, f32[64,1024]{1,0:T(8,128)S(1)}, f32[64,128]{1,0:T(8,128)S(1)}, f32[64,128]{1,0:T(8,128)S(1)}) custom-call(s32[1]{0:T(128)} %bitcast.mode, s32[1]{0:T(128)} %bitcast.1.parity, f32[200,1024]{1,0:T(8,128)S(1)} %get-tuple-element.33.share, f32[200,128]{1,0:T(8,128)S(1)} %get-tuple-element.34.own, ...), custom_call_target="tpu_custom_call" | custom-call | flops 536870912 | bytes 4411400 | tf_op jit(solution)/shard_map/star/pallas_call | solution.py:548
  50.5 3.3 %collective-permute-start.1 = (f32[64,128]{1,0:T(8,128)S(1)}, f32[64,128]{1,0:T(8,128)S(1)}, u32[]{:S(2)}, u32[]{:S(2)}) collective-permute-start(f32[64,128]{1,0:T(8,128)S(1)} %get-tuple-element.39.own), channel_id=1, source_target_pairs={{8,16},{24,32},{40,48},{56,64},{72,80},{88,96},{104,112},{120,128}... | collective-permute-start | bytes 98312 | tf_op jit(solution)/shard_map/ppermute | solution.py:573
  53.8 4.6 %all-gather.1 = f32[128,128]{1,0:T(8,128)S(1)} all-gather(f32[64,128]{1,0:T(8,128)S(1)} %get-tuple-element.40), channel_id=3, replica_groups={{0,8},{16,24},{32,40},{48,56},{64,72},{80,88},{96,104},{112,120},{128,1..., dimensions={0}, use_global_device_ids=true | all-gather | bytes 98304 | tf_op jit(solution)/shard_map/all_gather | solution.py:574
  58.4 0.0 collective-permute-done.1.first_in
  58.4 0.0 copy-done.5
  58.4 1.1 %helmholtz.1 = (f32[64,1024]{1,0:T(8,128)S(1)}, f32[64,1024]{1,0:T(8,128)S(1)}, f32[64,1024]{1,0:T(8,128)S(1)}, f32[64,1024]{1,0:T(8,128)S(1)}, f32[64,128]{1,0:...) custom-call(s32[1]{0:T(128)} %bitcast.mode, s32[1]{0:T(128)} %bitcast.1.parity, ...), custom_call_target="tpu_custom_call" | custom-call | flops 536870912 | bytes 3018760 | tf_op jit(solution)/shard_map/helmholtz/pallas_call | solution.py:548
  59.4 4.6 %collective-permute-start.2 = (f32[64,128]{1,0:T(8,128)S(1)}, f32[64,128]{1,0:T(8,128)S(1)}, u32[]{:S(2)}, u32[]{:S(2)}) collective-permute-start(f32[64,128]{1,0:T(8,128)S(1)} %get-tuple-element.43.own), channel_id=1, source_target_pairs={{8,16},{24,32},{40,48},{56,64},{72,80},{88,96},{104,112},{120,128}... | collective-permute-start | bytes 98312 | tf_op jit(solution)/shard_map/ppermute | solution.py:573
  64.1 4.6 %all-gather.2 = f32[128,128]{1,0:T(8,128)S(1)} all-gather(f32[64,128]{1,0:T(8,128)S(1)} %get-tuple-element.44), channel_id=4, replica_groups={{0,8},{16,24},{32,40},{48,56},{64,72},{80,88},{96,104},{112,120},{128,1..., dimensions={0}, use_global_device_ids=true | all-gather | bytes 98304 | tf_op jit(solution)/shard_map/all_gather | solution.py:574
  68.7 0.0 collective-permute-done.2.first_in
  68.7 0.7 image.1
  69.4 22.6 %all_to_all.16 = f32[64,1,256]{2,1,0:T(1,128)S(1)} all-to-all(f32[64,1,256]{2,1,0:T(1,128)S(1)} %get-tuple-element.46), channel_id=1, replica_groups=mesh['elem'=64,'mode'=8] {'elem'}, dimensions={0} | all-to-all | bytes 131072 | tf_op jit(solution)/shard_map/all_to_all | solution.py:638
  92.0 1.5 %finish.1 = (f32[3,64,648]{2,1,0:T(8,128)}, f32[64,648]{1,0:T(8,128)}) custom-call(s32[1]{0:T(128)} %bitcast.mode, f32[64,256]{1,0:T(8,128)S(1)} %bitcast.10, f32[192,1024]{1,0:T(8,128)S(1)} %get-tuple-element.47.star, f32[64,1024]{1,0:T(8,128)S(1)} %get-tuple-element.48.right, f32[64,1024]{1,0:T(8,128)S(1)} %get-tuple-element.49.right_x, ...), custom_call_target="tpu_custom_call" | custom-call | bytes 3088388 | tf_op jit(solution)/shard_map/finish/pallas_call | solution.py:548
  (6 shorter events, 0.1 us)
Async XLA Ops:
  0.6 1.1 %copy-start = (f32[3,64,648]{2,1,0:T(8,128)S(1)}, f32[3,64,648]{2,1,0:T(8,128)}, u32[]{:S(2)}) copy-start(f32[3,64,648]{2,1,0:T(8,128)} %velocity.3) | copy-start | bytes 1492996
  2.8 5.2 %copy-start.7 = (bf16[384,256]{1,0:T(8,128)(2,1)S(1)}, bf16[384,256]{1,0:T(8,128)(2,1)}, u32[]{:S(2)}) copy-start(bf16[384,256]{1,0:T(8,128)(2,1)} %constant.28.clone) | copy-start | bytes 589828
  2.9 5.2 %copy-start.6 = (bf16[2,256,512]{2,1,0:T(8,128)(2,1)S(1)}, bf16[2,256,512]{2,1,0:T(8,128)(2,1)}, u32[]{:S(2)}) copy-start(bf16[2,256,512]{2,1,0:T(8,128)(2,1)} %constant.30.clone) | copy-start | bytes 1572868
  2.9 14.8 %all-to-all-start = ((f32[8,2,64,128]{3,2,1,0:T(8,128)}), f32[8,2,64,128]{3,2,1,0:T(8,128)S(1)}, u32[]{:S(2)}, u32[]{:S(2)}) async-start(f32[8,2,64,128]{3,2,1,0:T(8,128)} %pack.1), calls=%async_computation | async-start | bytes 1048576 | tf_op jit(solution)/shard_map/all_to_all | solution.py:600
  7.3 0.7 copy-start.9
  7.3 0.7 copy-start.10
  8.1 0.7 copy-start.8
  8.1 1.1 %copy-start.1 = (f32[3,64,648]{2,1,0:T(8,128)S(1)}, f32[3,64,648]{2,1,0:T(8,128)}, u32[]{:S(2)}) copy-start(f32[3,64,648]{2,1,0:T(8,128)} %velocity.3) | copy-start | bytes 1492996
  8.8 0.7 copy-start.4
  11.3 0.8 copy-start.2
  32.2 17.1 %copy-start.3 = (bf16[256,1024]{1,0:T(8,128)(2,1)S(1)}, bf16[256,1024]{1,0:T(8,128)(2,1)}, u32[]{:S(2)}) copy-start(bf16[256,1024]{1,0:T(8,128)(2,1)} %copy-done.2) | copy-start | bytes 1572868
  32.7 16.6 %collective-permute-start = (f32[200,128]{1,0:T(8,128)S(1)}, f32[200,128]{1,0:T(8,128)S(1)}, u32[]{:S(2)}, u32[]{:S(2)}) collective-permute-start(f32[200,128]{1,0:T(8,128)S(1)} %get-tuple-element.34.own), channel_id=1, source_target_pairs={{8,16},{24,32},{40,48},{56,64},{72,80},{88,96},{104,112},{120,128}... | collective-permute-start | bytes 307208 | tf_op jit(solution)/shard_map/ppermute | solution.py:573
  49.3 9.1 %copy-start.5 = (bf16[768,128]{1,0:T(8,128)(2,1)S(1)}, bf16[768,128]{1,0:T(8,128)(2,1)}, u32[]{:S(2)}) copy-start(bf16[768,128]{1,0:T(8,128)(2,1)} %constant.29.clone.derive_back) | copy-start | bytes 589828
  50.5 7.9 %collective-permute-start.1 = (f32[64,128]{1,0:T(8,128)S(1)}, f32[64,128]{1,0:T(8,128)S(1)}, u32[]{:S(2)}, u32[]{:S(2)}) collective-permute-start(f32[64,128]{1,0:T(8,128)S(1)} %get-tuple-element.39.own), channel_id=1, source_target_pairs={{8,16},{24,32},{40,48},{56,64},{72,80},{88,96},{104,112},{120,128}... | collective-permute-start | bytes 98312 | tf_op jit(solution)/shard_map/ppermute | solution.py:573
  59.4 9.2 %collective-permute-start.2 = (f32[64,128]{1,0:T(8,128)S(1)}, f32[64,128]{1,0:T(8,128)S(1)}, u32[]{:S(2)}, u32[]{:S(2)}) collective-permute-start(f32[64,128]{1,0:T(8,128)S(1)} %get-tuple-element.43.own), channel_id=1, source_target_pairs={{8,16},{24,32},{40,48},{56,64},{72,80},{88,96},{104,112},{120,128}... | collective-permute-start | bytes 98312 | tf_op jit(solution)/shard_map/ppermute | solution.py:573
